TPU v7x, 512 devices: a whole 4x4x16 slice. The times are simulated.
512 devices in a mesh: lat: 8 (over x_lo, y), lon: 64 (over x_hi, z, core).
Axes of the slice: x: 4 (x_hi: 2, x_lo: 2; x = x_hi * 2 + x_lo), y: 4, z: 16, core: 2. Of those that a mesh axis runs over, the one named last changes fastest.
Arguments:
- input_field: float32 [96, 128, 8192], P(None, 'lat', 'lon'), may hold values from -6 to 6
- conv_weight: float32 [96, 864], replicated, may hold values from -0.21875 to 0.21875
- conv_bias: float32 [96], replicated, may hold values from -0.5 to 0.5
- cotangent: float32 [96, 128, 8192], P(None, 'lat', 'lon'), may hold values from -6 to 6
Outputs:
- output_field: float32 [96, 128, 8192], P(None, 'lat', 'lon')
- field_grad: float32 [96, 128, 8192], P(None, 'lat', 'lon')
- weight_grad: float32 [96, 864], replicated
- bias_grad: float32 [96], replicated
All inputs are finite; a program needn't handle non-finite values.
Results may differ from a plain program's by a relative error of at most 0.00012.
Values sent between devices are 32-bit elements; how exact they have to be, the bound alone decides.
No kernel may reach another device: no remote copies, remote signals or barrier semaphores. Data moves between devices by JAX's collectives and lax.ppermute only.
A program may use at most 64 MiB of HBM per device.

v0:
```python
import math

import jax
import jax.numpy as jnp
from jax import lax
from jax.sharding import PartitionSpec as P

HIGHEST = lax.Precision.HIGHEST


def with_halo(shard, sides, width, wrap):
    for axis, dim in sides:
        count, length = (lax.axis_size(axis), shard.shape[dim])
        up = [(i, (i + 1) % count) for i in range(count if wrap else count - 1)]
        down = [(j, i) for i, j in up]
        last = lax.slice_in_dim(shard, length - width, length, axis=dim)
        leading = lax.slice_in_dim(shard, 0, width, axis=dim)
        before = lax.ppermute(last, axis, up)
        after = lax.ppermute(leading, axis, down)
        shard = jnp.concatenate([before, shard, after], axis=dim)
    return shard


def shifted(shard, axis, by):
    count = lax.axis_size(axis)
    return lax.ppermute(shard, axis, [(i, (i + by) % count) for i in range(count)])


def shifted_2(value, axis, steps):
    count = lax.axis_size(axis)
    leading, last = (max(0, -steps), min(count, count - steps))
    return lax.ppermute(value, axis, [(source, source + steps) for source in range(leading, last)])


def tap_windows(padded, row_count, col_count):
    return jnp.concatenate(
        [padded[:, a : a + row_count, b : b + col_count] for a in range(3) for b in range(3)],
        axis=0,
    )


def place_polar(padded, top_row, bottom_row, at_top, at_bottom):
    padded = padded.at[:, 0, :].set(jnp.where(at_top, top_row, padded[:, 0, :]))
    return padded.at[:, -1, :].set(jnp.where(at_bottom, bottom_row, padded[:, -1, :]))


def shards(input_field, conv_weight, conv_bias, cotangent):
    channels, row_count, col_count = input_field.shape
    lat_count = lax.axis_size("lat")
    lon_count = lax.axis_size("lon")
    lat_place = lax.axis_index("lat")
    at_top = lat_place == 0
    at_bottom = lat_place == lat_count - 1
    half_turn = lon_count // 2
    kernel = conv_weight.reshape(channels, 9, channels)
    with_columns = with_halo(input_field, (("lon", 2),), 1, True)
    with_rows = with_halo(with_columns, (("lat", 1),), 1, False)
    polar_rows = shifted(
        jnp.stack([with_columns[:, 0, :], with_columns[:, -1, :]]), "lon", half_turn
    )
    padded_field = place_polar(with_rows, polar_rows[0], polar_rows[1], at_top, at_bottom)
    windows = tap_windows(padded_field, row_count, col_count)
    output_field = (
        jnp.einsum("ok,krc->orc", conv_weight, windows, precision=HIGHEST)
        + conv_bias[:, None, None]
    )
    local_weight = jnp.einsum("orc,krc->ok", cotangent, windows, precision=HIGHEST)
    local_bias = jnp.sum(cotangent, axis=(1, 2))
    pieces = jnp.einsum("otc,orl->tcrl", kernel, cotangent, precision=HIGHEST)
    spread = jnp.zeros((channels, row_count + 2, col_count + 2), jnp.float32)
    for a in range(3):
        for b in range(3):
            spread = spread.at[:, a : a + row_count, b : b + col_count].add(pieces[3 * a + b])
    upper_strip = spread[:, 0, :]
    lower_strip = spread[:, -1, :]
    from_above = shifted_2(lower_strip, "lat", 1)
    from_below = shifted_2(upper_strip, "lat", -1)
    opposite = shifted(jnp.stack([upper_strip, lower_strip]), "lon", half_turn)
    inner_rows = spread[:, 1 : row_count + 1, :]
    inner_rows = inner_rows.at[:, 0, :].add(from_above + jnp.where(at_top, opposite[0], 0.0))
    inner_rows = inner_rows.at[:, -1, :].add(from_below + jnp.where(at_bottom, opposite[1], 0.0))
    from_east = shifted(inner_rows[:, :, 0], "lon", -1)
    from_west = shifted(inner_rows[:, :, -1], "lon", 1)
    field_grad = inner_rows[:, :, 1 : col_count + 1]
    field_grad = field_grad.at[:, :, 0].add(from_west)
    field_grad = field_grad.at[:, :, -1].add(from_east)
    summed_weight, summed_bias = lax.psum((local_weight, local_bias), ("lat", "lon"))
    factor = 1.0 / math.sqrt(row_count * lat_count * col_count * lon_count)
    return (output_field, field_grad, summed_weight * factor, summed_bias * factor)


def solution(mesh):
    in_specs = (P(None, "lat", "lon"), P(), P(), P(None, "lat", "lon"))
    out_specs = (P(None, "lat", "lon"), P(None, "lat", "lon"), P(), P())
    return jax.shard_map(shards, mesh=mesh, in_specs=in_specs, out_specs=out_specs, check_vma=False)
```

profile of v0, /device:TPU:1, one launch (start us, length us, event | category | flops | bytes accessed | tf_op | source)
XLA Modules:
  0.0 772.5 jit_solution(9365704045245786128)
XLA Ops:
  7.2 1.2 copy.53
  8.4 7.0 fusion.10
  16.2 1.0 fusion.29
  17.4 1.7 fusion.9
  19.8 16.7 %scatter-add.45 = f32[96,18,130]{2,0,1:T(8,128)S(1)} dynamic-update-slice(f32[96,18,130]{2,0,1:T(8,128)S(1)} %scatter-add.44, f32[96,16,128]{2,0,1:T(8,128)S(1)} %fusion.9, s32[]{:T(128)} %constant.427.clone.1, s32[]{:T(128)} %bitcast.11, s32[]{:T(128)} %bitcast.12) | dynamic-update-slice | bytes 1572868 | tf_op jit(solution)/shard_map/scatter-add | solution.py:73
  36.5 3.3 add_select_fusion
  39.9 16.6 %scatter-add.46 = f32[96,18,130]{2,0,1:T(8,128)S(1)} dynamic-update-slice(f32[96,18,130]{2,0,1:T(8,128)S(1)} %scatter-add.45, f32[96,16,128]{2,0,1:T(8,128)S(1)} %add_select_fusion, s32[]{:T(128)} %constant.427.clone.1, s32[]{:T(128)} %bitcast.14, s32[]{:T(128)} %bitcast.15) | dynamic-update-slice | bytes 1572868 | tf_op jit(solution)/shard_map/scatter-add | solution.py:73
  56.4 1.3 fusion.8
  57.8 1.4 fusion.6
  59.2 14.8 %scatter-add.50 = f32[96,18,130]{2,0,1:T(8,128)S(1)} dynamic-update-slice(f32[96,18,130]{2,0,1:T(8,128)S(1)} %fusion.8, f32[96,16,128]{2,0,1:T(8,128)S(1)} %fusion.6, s32[]{:T(128)} %constant.427.clone.1, s32[]{:T(128)} %constant.435.clone.1, s32[]{:T(128)} %constant.435.clone.1) | dynamic-update-slice | bytes 1572868 | tf_op jit(solution)/shard_map/scatter-add | solution.py:73
  74.0 1.4 fusion.5
  75.4 14.8 %scatter-add.51 = f32[96,18,130]{2,0,1:T(8,128)S(1)} dynamic-update-slice(f32[96,18,130]{2,0,1:T(8,128)S(1)} %scatter-add.50, f32[96,16,128]{2,0,1:T(8,128)S(1)} %fusion.5, s32[]{:T(128)} %constant.427.clone.1, s32[]{:T(128)} %constant.435.clone.1, s32[]{:T(128)} %constant.432.clone.1) | dynamic-update-slice | bytes 1572868 | tf_op jit(solution)/shard_map/scatter-add | solution.py:73
  90.2 1.3 fusion.4
  91.5 1.4 fusion.2
  92.9 14.3 %scatter-add.55 = f32[96,18,130]{2,0,1:T(8,128)S(1)} dynamic-update-slice(f32[96,18,130]{2,0,1:T(8,128)S(1)} %fusion.4, f32[96,16,128]{2,0,1:T(8,128)S(1)} %fusion.2, s32[]{:T(128)} %constant.427.clone.1, s32[]{:T(128)} %constant.432.clone.1, s32[]{:T(128)} %constant.435.clone.1) | dynamic-update-slice | bytes 1572868 | tf_op jit(solution)/shard_map/scatter-add | solution.py:73
  107.2 1.4 fusion.1
  108.7 14.3 %scatter-add.56 = f32[96,18,130]{2,0,1:T(8,128)S(1)} dynamic-update-slice(f32[96,18,130]{2,0,1:T(8,128)S(1)} %scatter-add.55, f32[96,16,128]{2,0,1:T(8,128)S(1)} %fusion.1, s32[]{:T(128)} %constant.427.clone.1, s32[]{:T(128)} %constant.432.clone.1, s32[]{:T(128)} %constant.432.clone.1) | dynamic-update-slice | bytes 1572868 | tf_op jit(solution)/shard_map/scatter-add | solution.py:73
  123.7 5.5 collective-permute-start.6
  129.2 3.8 collective-permute-start.5
  133.0 1.4 collective-permute-start.7
  134.5 1.4 fusion.28
  135.8 1.5 copy.61
  137.3 4.7 collective-permute-start
  142.0 2.1 copy.62
  144.0 1.9 collective-permute-start.1
  146.7 108.9 %psum.15 = f32[96]{0:T(128)S(1)} all-reduce(f32[96]{0:T(128)S(1)} %reduce_sum.9), channel_id=1, replica_groups=mesh['lat'=8,'lon'=64] {'lat','lon'}, use_global_device_ids=true, to_apply=%region_3.4 | all-reduce | flops 96 | bytes 768 | tf_op jit(solution)/shard_map/psum | solution.py:87
  256.8 1.1 copy.51
  257.9 1.2 copy.50
  259.1 1.9 copy.52
  261.0 1.2 pad_maximum_fusion.5
  262.2 2.0 collective-permute-start.2
  264.2 1.3 collective-permute-start.3
  265.8 3.3 collective-permute-start.4
  271.2 2.8 collective-permute-done.4
  274.1 1.0 fusion.19
  276.2 4.9 collective-permute-start.8
  281.2 1.9 collective-permute-start.9
  285.0 2.9 copy-done
  287.9 7.6 convolution_bitcast_fusion
  295.4 6.8 fusion
  302.2 1.3 copy.58
  303.6 1.2 copy.55
  304.8 1.4 slice_add_fusion.1
  306.5 5.0 scatter-add.61
  311.8 6.4 scatter-add.64
  318.2 1.3 copy.59
  319.5 444.5 %all-reduce.3.cloned.1.call-done = f32[96,864]{1,0:T(8,128)} async-done(((f32[96,864]{1,0:T(8,128)}), f32[96,864]{1,0:T(8,128)}) %all-reduce.3.cloned.1.call-update) | async-done | bytes 331792 | tf_op jit(solution)/shard_map/psum | solution.py:87
  764.0 1.7 broadcast_multiply_fusion
  (60 shorter events, 10.3 us)
Async XLA Ops:
  7.2 756.8 %all-reduce.3.cloned.1.call-start = ((), (), s32[]{:S(2)}) async-start(), calls=%async_computation | async-start | bytes 688128 | tf_op jit(solution)/shard_map/psum | solution.py:87
  15.4 3.7 copy-start.1
  17.4 1.7 copy-start.10
  108.6 25.8 %copy-start.2 = (f32[96,16,128]{2,1,0:T(8,128)S(1)}, f32[96,16,128]{2,1,0:T(8,128)}, u32[]{:S(2)}) copy-start(f32[96,16,128]{2,1,0:T(8,128)} %param.34) | copy-start | bytes 2359300
  123.7 146.6 %collective-permute-start.6 = (f32[2,96,130]{2,1,0:T(8,128)S(1)}, f32[2,96,130]{2,1,0:T(8,128)}, u32[]{:S(2)}, u32[]{:S(2)}) collective-permute-start(f32[2,96,130]{2,1,0:T(8,128)S(1)} %pad_maximum_fusion.2), channel_id=1, source_target_pairs={{0,32},{1,33},{2,34},{3,35},{4,36},{5,37},{6,38},{7,39},{8,40},{9,... | collective-permute-start | bytes 299528 | tf_op jit(solution)/shard_map/ppermute | solution.py:26
  129.2 141.1 %collective-permute-start.5 = (f32[96,130]{1,0:T(8,128)}, f32[96,130]{1,0:T(8,128)}, u32[]{:S(2)}, u32[]{:S(2)}) collective-permute-start(f32[96,130]{1,0:T(8,128)} %get-tuple-element.211), channel_id=1, source_target_pairs={{0,64},{64,128},{128,192},{192,256},{256,320},{320,384},{384,448},... | collective-permute-start | bytes 149768 | tf_op jit(solution)/shard_map/ppermute | solution.py:32
  133.0 12.9 %copy-start.7 = (f32[96,16,128]{2,1,0:T(8,128)S(1)}, f32[96,16,128]{2,1,0:T(8,128)}, u32[]{:S(2)}) copy-start(f32[96,16,128]{2,1,0:T(8,128)} %param.37) | copy-start | bytes 2359300
  133.0 141.1 %collective-permute-start.7 = (f32[96,130]{1,0:T(8,128)}, f32[96,130]{1,0:T(8,128)}, u32[]{:S(2)}, u32[]{:S(2)}) collective-permute-start(f32[96,130]{1,0:T(8,128)} %get-tuple-element.208), channel_id=1, source_target_pairs={{64,0},{128,64},{192,128},{256,192},{320,256},{384,320},{448,384},... | collective-permute-start | bytes 149768 | tf_op jit(solution)/shard_map/ppermute | solution.py:32
  137.3 120.6 %collective-permute-start = (f32[96,16,1]{0,1,2:T(8,128)S(1)}, f32[96,16,1]{0,1,2:T(8,128)S(1)}, u32[]{:S(2)}, u32[]{:S(2)}) collective-permute-start(f32[96,16,1]{0,1,2:T(8,128)S(1)} %copy.61), channel_id=1, source_target_pairs={{0,1},{1,2},{2,3},{3,4},{4,5},{5,6},{6,7},{7,8},{8,9},{9,10},{10,1... | collective-permute-start | bytes 18440 | tf_op jit(solution)/shard_map/ppermute | solution.py:18
  144.0 115.1 %collective-permute-start.1 = (f32[96,16,1]{0,1,2:T(8,128)}, f32[96,16,1]{0,1,2:T(8,128)}, u32[]{:S(2)}, u32[]{:S(2)}) collective-permute-start(f32[96,16,1]{0,1,2:T(8,128)} %copy.62), channel_id=1, source_target_pairs={{1,0},{2,1},{3,2},{4,3},{5,4},{6,5},{7,6},{8,7},{9,8},{10,9},{11,1... | collective-permute-start | bytes 18440 | tf_op jit(solution)/shard_map/ppermute | solution.py:19
  255.6 1.1 copy-start.3
  261.0 8.6 %copy-start.4 = (f32[96,16,128]{2,0,1:T(8,128)S(1)}, f32[96,16,128]{2,0,1:T(8,128)}, u32[]{:S(2)}) copy-start(f32[96,16,128]{2,0,1:T(8,128)} %copy.51) | copy-start | bytes 2359300
  261.0 8.6 %copy-start.5 = (f32[96,16,1]{2,0,1:T(8,128)S(1)}, f32[96,16,1]{2,0,1:T(8,128)}, u32[]{:S(2)}) copy-start(f32[96,16,1]{2,0,1:T(8,128)} %copy.50) | copy-start | bytes 18436
  261.0 8.6 %copy-start.6 = (f32[96,16,1]{2,0,1:T(8,128)S(1)}, f32[96,16,1]{2,0,1:T(8,128)}, u32[]{:S(2)}) copy-start(f32[96,16,1]{2,0,1:T(8,128)} %copy.52) | copy-start | bytes 18436
  262.2 3.6 collective-permute-start.2
  264.2 5.4 collective-permute-start.3
  265.8 8.3 %collective-permute-start.4 = (f32[2,96,130]{2,1,0:T(8,128)S(1)}, f32[2,96,130]{2,1,0:T(8,128)S(1)}, u32[]{:S(2)}, u32[]{:S(2)}) collective-permute-start(f32[2,96,130]{2,1,0:T(8,128)S(1)} %pad_maximum_fusion.1), channel_id=1, source_target_pairs={{0,32},{1,33},{2,34},{3,35},{4,36},{5,37},{6,38},{7,39},{8,40},{9,... | collective-permute-start | bytes 299528 | tf_op jit(solution)/shard_map/ppermute | solution.py:26
  276.2 27.4 %collective-permute-start.8 = (f32[96,16]{0,1:T(8,128)S(1)}, f32[96,16]{0,1:T(8,128)S(1)}, u32[]{:S(2)}, u32[]{:S(2)}) collective-permute-start(f32[96,16]{0,1:T(8,128)S(1)} %get-tuple-element.205), channel_id=1, source_target_pairs={{0,1},{1,2},{2,3},{3,4},{4,5},{5,6},{6,7},{7,8},{8,9},{9,10},{10,1... | collective-permute-start | bytes 18440 | tf_op jit(solution)/shard_map/ppermute | solution.py:26
  281.2 25.0 %collective-permute-start.9 = (f32[96,16]{0,1:T(8,128)S(1)}, f32[96,16]{0,1:T(8,128)S(1)}, u32[]{:S(2)}, u32[]{:S(2)}) collective-permute-start(f32[96,16]{0,1:T(8,128)S(1)} %get-tuple-element.204), channel_id=1, source_target_pairs={{0,63},{1,0},{2,1},{3,2},{4,3},{5,4},{6,5},{7,6},{8,7},{9,8},{10,9... | collective-permute-start | bytes 18440 | tf_op jit(solution)/shard_map/ppermute | solution.py:26
  284.4 3.5 copy-start.8
  284.9 2.9 copy-start
  287.9 7.6 copy-start.9
Sparse Core Ops, SparseCore 0:
  303.7 460.2 all-reduce.2
where the time goes:
time: 774 us; the launch traced here: 773 us
  waiting for transfers between devices  448 us (58%)
  local copies, waits for them, and re-layouts  126 us (16%)
  blocking collectives  109 us (14%)
  starting transfers between devices  30.8 us (4%)
  other arithmetic  22.6 us (3%)
  matrix products  21.3 us (3%)
  between operations  14.5 us (2%)
    psum x1, waiting for transfers between devices, shards(): lax.psum((local_weight, local_bias), ('lat', 'lon'))  444 us
    psum x1, blocking collectives, shards(): lax.psum((local_weight, local_bias), ('lat', 'lon'))  109 us
    scatter-add x7, local copies, waits for them, and re-layouts, shards(): spread.at[:, a:a + row_count, b:b + col_count].add(pieces[3 * a + b])  91.7 us
    ppermute x4, starting transfers between devices, shifted(): lax.ppermute(shard, axis, [(i, (i + by) % count) for i in range(count)])  15.7 us
  transfers between devices with their start and end apart: 11, of which 4 were waited for; matrix products, arithmetic and copies ran while one was open for 6% of the time, Pallas kernels for 0%

commit v1 on v0

v1 whole, which is shorter than its diff:
```python
import functools
import math

import jax
import jax.numpy as jnp
from jax import lax
from jax.experimental import pallas as pl
from jax.experimental.pallas import tpu as pltpu
from jax.sharding import Mesh
from jax.sharding import PartitionSpec as P

F32 = jnp.float32
BF16 = jnp.bfloat16
C = 96
R = 16
L = 128
NT = (((1,), (1,)), ((), ()))

AXES = ("lat", "xh", "zr", "zd", "c")
LON = ("xh", "zr", "zd", "c")
NEAR = ("lat", "xh", "zd", "c")
FAR = ("zr",)

VMEM = pl.BlockSpec(memory_space=pltpu.VMEM)
SMEM = pl.BlockSpec(memory_space=pltpu.SMEM)


def call(kernel, outs, args, scratch=(), flops=0, moved=0):
    return pl.pallas_call(
        kernel,
        out_shape=outs,
        in_specs=[SMEM] + [VMEM] * (len(args) - 1),
        out_specs=[VMEM] * len(outs),
        scratch_shapes=list(scratch),
        compiler_params=pltpu.CompilerParams(vmem_limit_bytes=40 * 1024 * 1024),
        cost_estimate=pl.CostEstimate(flops=flops, bytes_accessed=moved, transcendentals=0),
    )(*args)


def out(*shape):
    return jax.ShapeDtypeStruct(shape, F32)


def roll(value, by):
    by = by % L
    return value if by == 0 else pltpu.roll(value, by, 1)


def lanes():
    return lax.broadcasted_iota(jnp.int32, (C, L), 1)


def row(ref, r):
    return ref[pl.ds(r, C, stride=R), :]


def pick(flag, when_set, otherwise):
    return jnp.where(flag == 1, when_set, otherwise)


def split(value):
    high = value.astype(BF16)
    return high, (value - high.astype(F32)).astype(BF16)


def edges_kernel(flags, x, g, near_col, far_col, row_1, row_2):
    lane = lanes()
    east = jnp.zeros((C, L), F32)
    west = jnp.zeros((C, L), F32)
    for r in range(R):
        for ref, base in ((x, 0), (g, R)):
            here = row(ref, r)
            east = jnp.where(lane == base + r, roll(here, base + r + 1), east)
            west = jnp.where(lane == base + r, roll(here, base + r), west)
    near_col[...] = pick(flags[0], west, east)
    far_col[...] = pick(flags[0], east, west)
    top = row(g, 0)
    bottom = row(g, R - 1)
    row_1[...] = pick(flags[1], top, bottom)
    row_2[...] = pick(flags[1], bottom, top)


def corners_kernel(flags, x, near_col, far_col, msg_1, msg_2):
    lane = lanes()
    west = pick(flags[0], near_col[...], far_col[...])
    east = pick(flags[0], far_col[...], near_col[...])

    def corner(r):
        parts = ((west, r), (east, r), (west, R + r), (east, R + r))
        total = jnp.zeros((C, L), F32)
        for k, (source, at) in enumerate(parts):
            total = jnp.where(lane == k, roll(source, k - at), total)
        return total

    for part, (top, bottom) in enumerate(
        ((row(x, 0), row(x, R - 1)), (corner(0), corner(R - 1)))
    ):
        msg_1[part] = pick(flags[1], top, bottom)
        msg_2[part] = pick(flags[1], bottom, top)


def taps(value, west, west_lane, east, east_lane):
    lane = lanes()
    before = jnp.where(lane == 0, roll(west, -west_lane), roll(value, 1))
    after = jnp.where(lane == L - 1, roll(east, L - 1 - east_lane), roll(value, -1))
    return before, value, after


def weight_kernel(
    chunk, flags, x, g, near_col, far_col, row_1, row_2, packed, s_hi, s_lo, c_hi, c_lo
):
    west = pick(flags[0], near_col[...], far_col[...])
    east = pick(flags[0], far_col[...], near_col[...])
    north = pick(flags[1], row_1[...], row_2[...])
    south = pick(flags[1], row_2[...], row_1[...])
    at_top = flags[2].astype(F32)
    at_bottom = flags[3].astype(F32)
    total = jnp.zeros((C, L), F32)
    for r in range(R):
        at = pl.ds(r * L, L)
        for b, value in enumerate(taps(row(x, r), west, r, east, r)):
            s_hi[pl.ds(b * C, C), at], s_lo[pl.ds(b * C, C), at] = split(value)
        here = row(g, r)
        total = total + here
        below = row(g, r + 1) if r + 1 < R else south * (1.0 - at_bottom)
        above = row(g, r - 1) if r > 0 else north * (1.0 - at_top)
        if r == 0:
            below = below + north * at_top
        if r == R - 1:
            above = above + south * at_bottom
        for a, value in enumerate((below, here, above)):
            c_hi[pl.ds(a * C, C), at], c_lo[pl.ds(a * C, C), at] = split(value)

    def product(left, right):
        return lax.dot_general(left[...], right[...], NT, preferred_element_type=F32)

    grad = product(c_hi, s_hi) + product(c_hi, s_lo) + product(c_lo, s_hi)
    wide = jnp.concatenate(
        [grad[a * C : (a + 1) * C] for a in range(3)] + [jnp.zeros((C, 32), F32)], axis=1
    )
    bias = lax.dot_general(
        jnp.ones((8, L), F32), total, NT, preferred_element_type=F32, precision=lax.Precision.HIGHEST
    )
    bias = jnp.concatenate([bias, jnp.zeros((8, L - C), F32)], axis=1)

    def put(q, value):
        packed[q // chunk, :, pl.ds((q % chunk) * L, L)] = value

    q = 0
    for i in range(C // 8):
        for j in range(7):
            tile = wide[8 * i : 8 * i + 8, L * j : L * j + L]
            for s in range(8):
                put(q, tile[s : s + 1])
                q += 1
    put(q, bias[0:1])
    for rest in range(q + 1, packed.shape[0] * chunk):
        put(rest, jnp.zeros((1, L), F32))


def unpack_kernel(chunk, factor, flags, gathered, weight_grad, bias_grad):
    def get(q):
        return gathered[q // chunk, :, pl.ds((q % chunk) * L, L)] * factor

    q = 0
    for i in range(C // 8):
        for j in range(7):
            tile = jnp.concatenate([get(q + s) for s in range(8)], axis=0)
            width = min(L, 9 * C - L * j)
            weight_grad[pl.ds(8 * i, 8), pl.ds(L * j, width)] = tile[:, :width]
            q += 8
    bias_grad[...] = get(q)[:, :C]


def conv_kernel(
    is_grad, flags, field, near_col, far_col, row_1, row_2, msg_1, msg_2, weight, bias, result, hi, lo
):
    west = pick(flags[0], near_col[...], far_col[...])
    east = pick(flags[0], far_col[...], near_col[...])
    if is_grad:
        north = pick(flags[1], row_1[...], row_2[...])
        south = pick(flags[1], row_2[...], row_1[...])
    else:
        north = pick(flags[1], msg_1[0], msg_2[0])
        south = pick(flags[1], msg_2[0], msg_1[0])
    north_ends = pick(flags[1], msg_1[1], msg_2[1])
    south_ends = pick(flags[1], msg_2[1], msg_1[1])
    base = R if is_grad else 0
    end = 2 if is_grad else 0

    def shifts(r):
        if r < 0:
            return taps(north, north_ends, end, north_ends, end + 1)
        if r >= R:
            return taps(south, south_ends, end, south_ends, end + 1)
        return taps(row(field, r), west, base + r, east, base + r)

    def put(block, half, values):
        for b, value in enumerate(values):
            at = (pl.ds((3 * block + b) * C, C), pl.ds(half * L, L))
            hi[at], lo[at] = split(value)

    half = R // 2
    if is_grad:
        at_top = flags[2].astype(F32)
        at_bottom = flags[3].astype(F32)
        outer_top = shifts(-1)
        outer_bottom = shifts(R)
        put(0, 0, [v * (1.0 - at_top) for v in outer_top])
        put(0, 1, shifts(half - 1))
        put(1, 0, shifts(0))
        put(1, 1, shifts(half))
        put(2, 0, [v + o * at_top for v, o in zip(shifts(1), outer_top)])
        put(2, 1, shifts(half + 1))
        for r in range(half):
            put(3 + r, 0, shifts(r))
            put(3 + r, 1, shifts(r + half))
        k = 3 + half
        put(k, 0, shifts(half - 2))
        put(k, 1, [v + o * at_bottom for v, o in zip(shifts(R - 2), outer_bottom)])
        put(k + 1, 0, shifts(half - 1))
        put(k + 1, 1, shifts(R - 1))
        put(k + 2, 0, shifts(half))
        put(k + 2, 1, [v * (1.0 - at_bottom) for v in outer_bottom])
        starts = [0] + [2 + r for r in range(1, half - 1)] + [k]
    else:
        for j in range(half + 2):
            put(j, 0, shifts(j - 1))
            put(j, 1, shifts(j - 1 + half))
        starts = list(range(half))
    w_hi, w_lo = split(weight[...])
    both = jnp.concatenate([w_hi, w_lo], axis=0)
    for r, start in enumerate(starts):
        at = pl.ds(start * 3 * C, 9 * C)
        first = jnp.dot(both, hi[at, :], preferred_element_type=F32)
        second = jnp.dot(w_hi, lo[at, :], preferred_element_type=F32)
        value = first[:C] + first[C:] + second
        if not is_grad:
            value = value + bias[...]
        result[pl.ds(r, C, stride=R), :] = value[:, :L]
        result[pl.ds(r + half, C, stride=R), :] = value[:, L:]


def conv(is_grad, *args):
    blocks = 3 + R // 2 + 3 if is_grad else R // 2 + 2
    scratch = pltpu.VMEM((blocks * 3 * C, 2 * L), BF16)
    return call(
        functools.partial(conv_kernel, is_grad),
        [out(C * R, L)],
        args,
        [scratch, scratch],
        flops=6 * 9 * C * C * R * L,
        moved=3 * 4 * C * R * L,
    )[0]


def shards(nlat, nlon, factor, x, weight, bias, g):
    lat = lax.axis_index("lat")
    lon = lax.axis_index(LON)
    flags = jnp.stack([lon % 2, lat % 2, lat == 0, lat == nlat - 1]).astype(jnp.int32)
    x = x.reshape(C * R, L)
    g = g.reshape(C * R, L)

    def pairs_of(partner):
        pairs = []
        for i in range(nlat):
            for j in range(nlon):
                to_lat, to_lon = partner(i, j)
                pairs.append((i * nlon + j, to_lat * nlon + to_lon))
        return pairs

    def across_2(i, j):
        to = i + 1 if i % 2 else i - 1
        return (to, j) if 0 <= to < nlat else (i, (j + nlon // 2) % nlon)

    near = pairs_of(lambda i, j: (i, j ^ 1))
    far = pairs_of(lambda i, j: (i, (j + (1 if j % 2 else -1)) % nlon))
    first = pairs_of(lambda i, j: (i ^ 1, j))
    second = pairs_of(across_2)

    def send(value, pairs):
        return lax.ppermute(value, AXES, pairs)

    block = 4 * C * R * L
    near_col, far_col, row_1, row_2 = call(
        edges_kernel, [out(C, L)] * 4, (flags, x, g), flops=block, moved=2 * block
    )
    far_col = send(far_col, far)
    row_2 = send(row_2, second)
    row_1 = send(row_1, first)
    near_col = send(near_col, near)

    n_near = nlat * nlon // lax.axis_size(FAR)
    chunk = -(-(7 * C + 1) // n_near)
    packed = call(
        functools.partial(weight_kernel, chunk),
        [out(n_near, 1, chunk * L)],
        (flags, x, g, near_col, far_col, row_1, row_2),
        [pltpu.VMEM((3 * C, R * L), BF16)] * 4,
        flops=6 * 9 * C * C * R * L,
        moved=2 * block,
    )[0]

    near_col, far_col, packed, weight, bias = lax.optimization_barrier(
        (near_col, far_col, packed, weight, bias)
    )
    parts = lax.all_to_all(packed, NEAR, 0, 0)
    mine = jnp.sum(parts, axis=0, keepdims=True)
    n_far = lax.axis_size(FAR)
    mine = lax.all_to_all(jnp.broadcast_to(mine, (n_far, 1, chunk * L)), FAR, 0, 0)
    mine = jnp.sum(mine, axis=0, keepdims=True)
    gathered = lax.all_to_all(jnp.broadcast_to(mine, (n_near, 1, chunk * L)), NEAR, 0, 0)
    weight_grad, bias_grad = call(
        functools.partial(unpack_kernel, chunk, factor),
        [out(C, 9 * C), out(1, C)],
        (flags, gathered),
    )

    msg_1, msg_2 = call(
        corners_kernel, [out(2, C, L)] * 2, (flags, x, near_col, far_col), moved=block
    )
    msg_2 = send(msg_2, second)
    msg_1 = send(msg_1, first)
    flipped = weight.reshape(C, 3, 3, C)[:, ::-1, ::-1].transpose(3, 1, 2, 0).reshape(C, 9 * C)
    halo = (near_col, far_col, row_1, row_2, msg_1, msg_2)
    column = bias.reshape(C, 1)
    output = conv(False, flags, x, *halo, weight, column)
    grad = conv(True, flags, g, *halo, flipped, column)
    return (
        output.reshape(C, R, L),
        grad.reshape(C, R, L),
        weight_grad,
        bias_grad.reshape(C),
    )


def solution(mesh):
    nlat, nlon = mesh.shape["lat"], mesh.shape["lon"]
    fine = Mesh(mesh.devices.reshape(nlat, 2, nlon // 8, 2, 2), AXES)
    factor = 1.0 / math.sqrt(nlat * R * nlon * L)
    field = P(None, "lat", LON)
    return jax.shard_map(
        functools.partial(shards, nlat, nlon, factor),
        mesh=fine,
        in_specs=(field, P(), P(), field),
        out_specs=(field, field, P(), P()),
        check_vma=False,
    )
```

time: 774 us -> 99.7 us (0.13)
  waiting for transfers between devices: 448 us -> 5.83 us
  local copies, waits for them, and re-layouts: 126 us -> 4.58 us
  blocking collectives: 109 us -> 43.3 us
  other arithmetic: 22.6 us -> 0.35 us
  matrix products: 21.3 us -> 0 us
  Pallas kernels: 0 us -> 14.9 us
  between operations: 14.5 us -> 0.82 us
    psum x1 -> x0, waiting for transfers between devices: 444 us -> none  [shards(): lax.psum((local_weight, local_bias), ('lat', 'lon'))]
    psum x1 -> x0, blocking collectives: 109 us -> none  [shards(): lax.psum((local_weight, local_bias), ('lat', 'lon'))]
    scatter-add x9 -> x0, local copies, waits for them, and re-layouts: 103 us -> none  [the longest x7 91.7 us: shards(): spread.at[:, a:a + row_count, b:b + col_count].add(pieces[3 * a + b])]
    all_to_all x0 -> x2, blocking collectives: none -> 43.3 us  [the longest x1 24.6 us: shards(): parts = lax.all_to_all(packed, NEAR, 0, 0)]
    dot_general x3 -> x0, matrix products: 21.3 us -> none  [the longest x1 7.56 us: shards(): jnp.einsum('orc,krc->ok', cotangent, windows, precision=HIGHEST)]
    pallas_call x0 -> x6, Pallas kernels: none -> 14.9 us  [call(): pl.pallas_call(kernel, out_shape=outs, in_specs=[SMEM] + [VMEM] * (len(ar...]
    unnamed x36 -> x12, local copies, waits for them, and re-layouts: 13.4 us -> 2.93 us
    add x7 -> x0, other arithmetic: 8.94 us -> none  [the longest x5 7.27 us: shards(): spread.at[:, a:a + row_count, b:b + col_count].add(pieces[3 * a + b])]
  transfers between devices with their start and end apart: 11 -> 7, of which waited for: 4 -> 3; matrix products, arithmetic and copies ran while one was open for 6% -> 1% of each run, Pallas kernels for 0% -> 8%
where the time goes in v1:
time: 99.7 us; the launch traced here: 98.2 us
  blocking collectives  43.3 us (43%)
  starting transfers between devices  28.3 us (28%)
  Pallas kernels  14.9 us (15%)
  waiting for transfers between devices  5.83 us (6%)
  local copies, waits for them, and re-layouts  4.58 us (5%)
    all_to_all x1, blocking collectives, shards(): parts = lax.all_to_all(packed, NEAR, 0, 0)  24.6 us
    ppermute x6, starting transfers between devices, send(): return lax.ppermute(value, AXES, pairs)  22.7 us
    all_to_all x1, blocking collectives, shards(): lax.all_to_all(jnp.broadcast_to(mine, (n_far, 1, chunk * L)), FAR, 0, 0)  18.8 us
    pallas_call x6, Pallas kernels, call(): pl.pallas_call(kernel, out_shape=outs, in_specs=[SMEM] + [VMEM] * (len(ar...  14.9 us
    ppermute x6, waiting for transfers between devices, send(): return lax.ppermute(value, AXES, pairs)  5.83 us
    all_to_all x1, starting transfers between devices, shards(): lax.all_to_all(jnp.broadcast_to(mine, (n_near, 1, chunk * L)), NEAR, 0, 0)  5.6 us
    unnamed x12, local copies, waits for them, and re-layouts  2.93 us
  transfers between devices with their start and end apart: 7, of which 3 were waited for; matrix products, arithmetic and copies ran while one was open for 1% of the time, Pallas kernels for 8%

profile of v1, /device:TPU:1, one launch (start us, length us, event | category | flops | bytes accessed | tf_op | source)
XLA Modules:
  0.0 98.2 jit_solution(17333158717981486207)
XLA Ops:
  0.7 0.1 pad_add_fusion.flags
  0.7 0.0 copy-start
  0.7 1.1 %copy-done = f32[96,16,128]{2,1,0:T(8,128)S(1)} copy-done((f32[96,16,128]{2,1,0:T(8,128)S(1)}, f32[96,16,128]{2,1,0:T(8,128)}, u32[]{:S(2)}) %copy-start) | copy-done | bytes 786456
  1.9 0.0 copy-start.2
  1.9 1.1 %copy-done.2 = f32[96,16,128]{2,1,0:T(8,128)S(1)} copy-done((f32[96,16,128]{2,1,0:T(8,128)S(1)}, f32[96,16,128]{2,1,0:T(8,128)}, u32[]{:S(2)}) %copy-start.2) | copy-done | bytes 786456
  3.0 1.6 %shard_map.75 = (f32[96,128]{1,0:T(8,128)S(1)}, f32[96,128]{1,0:T(8,128)S(1)}, f32[96,128]{1,0:T(8,128)S(1)}, f32[96,128]{1,0:T(8,128)S(1)}) custom-call(s32[4]{0:T(128)S(1)} %pad_add_fusion.flags, f32[1536,128]{1,0:T(8,128)S(1)} %bitcast.14, f32[1536,128]{1,0:T(8,128)S(1)} %bitcast.18), custom_call_target="tpu_custom_call" | custom-call | flops 786432 | bytes 1572864 | tf_op jit(solution)/shard_map/pallas_call | solution.py:29
  4.6 8.8 %collective-permute-start = (f32[96,128]{1,0:T(8,128)S(1)}, f32[96,128]{1,0:T(8,128)S(1)}, u32[]{:S(2)}, u32[]{:S(2)}) collective-permute-start(f32[96,128]{1,0:T(8,128)S(1)} %get-tuple-element.17), channel_id=1, source_target_pairs={{0,1},{1,0},{2,3},{3,2},{4,5},{5,4},{6,7},{7,6},{8,9},{9,8},{10,11... | collective-permute-start | bytes 147464 | tf_op jit(solution)/shard_map/ppermute | solution.py:282
  13.4 1.9 %collective-permute-start.1 = (f32[96,128]{1,0:T(8,128)S(1)}, f32[96,128]{1,0:T(8,128)S(1)}, u32[]{:S(2)}, u32[]{:S(2)}) collective-permute-start(f32[96,128]{1,0:T(8,128)S(1)} %get-tuple-element.18), channel_id=1, source_target_pairs={{0,63},{1,2},{2,1},{3,4},{4,3},{5,6},{6,5},{7,8},{8,7},{9,10},{10,... | collective-permute-start | bytes 147464 | tf_op jit(solution)/shard_map/ppermute | solution.py:282
  15.3 1.9 %collective-permute-start.2 = (f32[96,128]{1,0:T(8,128)S(1)}, f32[96,128]{1,0:T(8,128)S(1)}, u32[]{:S(2)}, u32[]{:S(2)}) collective-permute-start(f32[96,128]{1,0:T(8,128)S(1)} %get-tuple-element.19), channel_id=1, source_target_pairs={{0,64},{1,65},{2,66},{3,67},{4,68},{5,69},{6,70},{7,71},{8,72},{9,... | collective-permute-start | bytes 147464 | tf_op jit(solution)/shard_map/ppermute | solution.py:282
  17.3 2.1 %collective-permute-start.3 = (f32[96,128]{1,0:T(8,128)S(1)}, f32[96,128]{1,0:T(8,128)S(1)}, u32[]{:S(2)}, u32[]{:S(2)}) collective-permute-start(f32[96,128]{1,0:T(8,128)S(1)} %get-tuple-element.20), channel_id=1, source_target_pairs={{0,32},{1,33},{2,34},{3,35},{4,36},{5,37},{6,38},{7,39},{8,40},{9,... | collective-permute-start | bytes 147464 | tf_op jit(solution)/shard_map/ppermute | solution.py:282
  19.3 0.0 collective-permute-done.near_col
  19.4 0.0 collective-permute-done.1.far_col
  19.4 0.8 collective-permute-done.2.row_1
  20.2 3.4 %collective-permute-done.3.row_2 = f32[96,128]{1,0:T(8,128)S(1)} collective-permute-done((f32[96,128]{1,0:T(8,128)S(1)}, f32[96,128]{1,0:T(8,128)S(1)}, u32[]{:S(2)}, u32[]{:S(2)}) %collective-permute-start.3) | collective-permute-done | bytes 49184 | tf_op jit(solution)/shard_map/ppermute | solution.py:282
  23.6 3.7 %shard_map.76 = f32[64,1,1408]{2,1,0:T(1,128)S(1)} custom-call(s32[4]{0:T(128)S(1)} %pad_add_fusion.flags, f32[1536,128]{1,0:T(8,128)S(1)} %bitcast.15, f32[1536,128]{1,0:T(8,128)S(1)} %bitcast.19, f32[96,128]{1,0:T(8,128)S(1)} %collective-permute-done.near_col, f32[96,128]{1,0:T(8,128)S(1)} %collective-permute-done.1.far_col, ...), custom_call_target="tpu_custom_call" | custom-call | flops 1019215872 | bytes 1572864 | tf_op jit(solution)/shard_map/pallas_call | solution.py:29
  27.3 24.6 %all_to_all.15 = f32[64,1,1408]{2,1,0:T(1,128)S(1)} all-to-all(f32[64,1,1408]{2,1,0:T(1,128)S(1)} %shard_map.76), channel_id=1, replica_groups=mesh['lat'=8,'xh'=2,'zr'=8,'zd'=2,'c'=2] {'lat','xh','zd','c'}, dimensions={0} | all-to-all | bytes 720896 | tf_op jit(solution)/shard_map/all_to_all | solution.py:307
  51.9 0.0 copy-start.1
  51.9 0.2 reduce_sum.18
  52.2 18.8 %all_to_all.16 = f32[8,1,1408]{2,1,0:T(1,128)S(1)} all-to-all(f32[8,1,1408]{2,1,0:T(1,128)S(1)} %broadcast_in_dim.4), channel_id=1, replica_groups=mesh['lat'=8,'xh'=2,'zr'=8,'zd'=2,'c'=2] {'zr'}, dimensions={0} | all-to-all | bytes 90112 | tf_op jit(solution)/shard_map/all_to_all | solution.py:310
  71.0 0.9 broadcast_in_dim.5
  71.9 5.6 %all-to-all-start.2 = ((f32[64,1,1408]{2,1,0:T(1,128)}), f32[64,1,1408]{2,1,0:T(1,128)S(1)}, u32[]{:S(2)}, u32[]{:S(2)}) async-start(f32[64,1,1408]{2,1,0:T(1,128)} %broadcast_in_dim.5), calls=%async_computation.2 | async-start | bytes 720896 | tf_op jit(solution)/shard_map/all_to_all | solution.py:312
  77.5 0.0 copy-start.5
  77.5 0.6 copy-done.5
  78.2 0.1 copy.21.bias
  78.3 0.0 copy-done.1
  78.3 0.0 copy-start.4
  78.3 0.7 shard_map.77
  79.0 3.3 %collective-permute-start.4 = (f32[2,96,128]{2,1,0:T(8,128)S(1)}, f32[2,96,128]{2,1,0:T(8,128)S(1)}, u32[]{:S(2)}, u32[]{:S(2)}) collective-permute-start(f32[2,96,128]{2,1,0:T(8,128)S(1)} %get-tuple-element.23), channel_id=1, source_target_pairs={{0,64},{1,65},{2,66},{3,67},{4,68},{5,69},{6,70},{7,71},{8,72},{9,... | collective-permute-start | bytes 294920 | tf_op jit(solution)/shard_map/ppermute | solution.py:282
  82.4 4.6 %collective-permute-start.5 = (f32[2,96,128]{2,1,0:T(8,128)S(1)}, f32[2,96,128]{2,1,0:T(8,128)S(1)}, u32[]{:S(2)}, u32[]{:S(2)}) collective-permute-start(f32[2,96,128]{2,1,0:T(8,128)S(1)} %get-tuple-element.24), channel_id=1, source_target_pairs={{0,32},{1,33},{2,34},{3,35},{4,36},{5,37},{6,38},{7,39},{8,40},{9,... | collective-permute-start | bytes 294920 | tf_op jit(solution)/shard_map/ppermute | solution.py:282
  87.0 0.0 copy-done.4
  87.0 0.2 copy.22
  87.2 0.2 copy.23
  87.4 0.2 copy.24.weight
  87.6 0.0 copy-start.3
  87.6 0.0 collective-permute-done.4.msg_1
  87.6 1.6 %collective-permute-done.5.msg_2 = f32[2,96,128]{2,1,0:T(8,128)S(1)} collective-permute-done((f32[2,96,128]{2,1,0:T(8,128)S(1)}, f32[2,96,128]{2,1,0:T(8,128)S(1)}, u32[]{:S(2)}, u32[]{:S(2)}) %collective-permute-start.5) | collective-permute-done | bytes 98336 | tf_op jit(solution)/shard_map/ppermute | solution.py:282
  89.2 3.5 %shard_map.78 = f32[1536,128]{1,0:T(8,128)} custom-call(s32[4]{0:T(128)S(1)} %pad_add_fusion.flags, f32[1536,128]{1,0:T(8,128)S(1)} %bitcast.17, f32[96,128]{1,0:T(8,128)S(1)} %collective-permute-done.near_col, f32[96,128]{1,0:T(8,128)S(1)} %collective-permute-done.1.far_col, f32[96,128]{1,0:T(8,128)S(1)} %collective-permute-done.2.row_1, ...), custom_call_target="tpu_custom_call" | custom-call | flops 1019215872 | bytes 2359296 | tf_op jit(solution)/shard_map/pallas_call | solution.py:29
  92.7 0.0 copy-done.3
  92.7 3.8 %shard_map.79 = f32[1536,128]{1,0:T(8,128)} custom-call(s32[4]{0:T(128)S(1)} %pad_add_fusion.flags, f32[1536,128]{1,0:T(8,128)S(1)} %bitcast.20, f32[96,128]{1,0:T(8,128)S(1)} %collective-permute-done.near_col, f32[96,128]{1,0:T(8,128)S(1)} %collective-permute-done.1.far_col, f32[96,128]{1,0:T(8,128)S(1)} %collective-permute-done.2.row_1, ...), custom_call_target="tpu_custom_call" | custom-call | flops 1019215872 | bytes 2359296 | tf_op jit(solution)/shard_map/pallas_call | solution.py:29
  96.6 0.0 all-to-all-done.2.gathered
  96.6 1.6 %shard_map.80 = (f32[96,864]{1,0:T(8,128)}, f32[1,96]{1,0:T(1,128)}) custom-call(s32[4]{0:T(128)S(1)} %pad_add_fusion.flags, f32[64,1,1408]{2,1,0:T(1,128)S(1)} %all-to-all-done.2.gathered), custom_call_target="tpu_custom_call" | custom-call | tf_op jit(solution)/shard_map/pallas_call | solution.py:29
  (3 shorter events, 0.1 us)
Async XLA Ops:
  0.7 1.1 %copy-start = (f32[96,16,128]{2,1,0:T(8,128)S(1)}, f32[96,16,128]{2,1,0:T(8,128)}, u32[]{:S(2)}) copy-start(f32[96,16,128]{2,1,0:T(8,128)} %param.4) | copy-start | bytes 2359300
  1.9 1.1 %copy-start.2 = (f32[96,16,128]{2,1,0:T(8,128)S(1)}, f32[96,16,128]{2,1,0:T(8,128)}, u32[]{:S(2)}) copy-start(f32[96,16,128]{2,1,0:T(8,128)} %param.7) | copy-start | bytes 2359300
  4.6 14.7 %collective-permute-start = (f32[96,128]{1,0:T(8,128)S(1)}, f32[96,128]{1,0:T(8,128)S(1)}, u32[]{:S(2)}, u32[]{:S(2)}) collective-permute-start(f32[96,128]{1,0:T(8,128)S(1)} %get-tuple-element.17), channel_id=1, source_target_pairs={{0,1},{1,0},{2,3},{3,2},{4,5},{5,4},{6,7},{7,6},{8,9},{9,8},{10,11... | collective-permute-start | bytes 147464 | tf_op jit(solution)/shard_map/ppermute | solution.py:282
  13.4 6.0 %collective-permute-start.1 = (f32[96,128]{1,0:T(8,128)S(1)}, f32[96,128]{1,0:T(8,128)S(1)}, u32[]{:S(2)}, u32[]{:S(2)}) collective-permute-start(f32[96,128]{1,0:T(8,128)S(1)} %get-tuple-element.18), channel_id=1, source_target_pairs={{0,63},{1,2},{2,1},{3,4},{4,3},{5,6},{6,5},{7,8},{8,7},{9,10},{10,... | collective-permute-start | bytes 147464 | tf_op jit(solution)/shard_map/ppermute | solution.py:282
  15.3 4.8 %collective-permute-start.2 = (f32[96,128]{1,0:T(8,128)S(1)}, f32[96,128]{1,0:T(8,128)S(1)}, u32[]{:S(2)}, u32[]{:S(2)}) collective-permute-start(f32[96,128]{1,0:T(8,128)S(1)} %get-tuple-element.19), channel_id=1, source_target_pairs={{0,64},{1,65},{2,66},{3,67},{4,68},{5,69},{6,70},{7,71},{8,72},{9,... | collective-permute-start | bytes 147464 | tf_op jit(solution)/shard_map/ppermute | solution.py:282
  17.3 6.4 %collective-permute-start.3 = (f32[96,128]{1,0:T(8,128)S(1)}, f32[96,128]{1,0:T(8,128)S(1)}, u32[]{:S(2)}, u32[]{:S(2)}) collective-permute-start(f32[96,128]{1,0:T(8,128)S(1)} %get-tuple-element.20), channel_id=1, source_target_pairs={{0,32},{1,33},{2,34},{3,35},{4,36},{5,37},{6,38},{7,39},{8,40},{9,... | collective-permute-start | bytes 147464 | tf_op jit(solution)/shard_map/ppermute | solution.py:282
  51.9 26.4 %copy-start.1 = (f32[96,16,128]{2,1,0:T(8,128)S(1)}, f32[96,16,128]{2,1,0:T(8,128)}, u32[]{:S(2)}) copy-start(f32[96,16,128]{2,1,0:T(8,128)} %param.4) | copy-start | bytes 2359300
  71.9 24.7 %all-to-all-start.2 = ((f32[64,1,1408]{2,1,0:T(1,128)}), f32[64,1,1408]{2,1,0:T(1,128)S(1)}, u32[]{:S(2)}, u32[]{:S(2)}) async-start(f32[64,1,1408]{2,1,0:T(1,128)} %broadcast_in_dim.5), calls=%async_computation.2 | async-start | bytes 720896 | tf_op jit(solution)/shard_map/all_to_all | solution.py:312
  77.5 0.7 copy-start.5
  78.3 8.7 %copy-start.4 = (f32[96,864]{1,0:T(8,128)S(1)}, f32[96,864]{1,0:T(8,128)}, u32[]{:S(2)}) copy-start(f32[96,864]{1,0:T(8,128)} %weight) | copy-start | bytes 995332
  79.0 8.6 %collective-permute-start.4 = (f32[2,96,128]{2,1,0:T(8,128)S(1)}, f32[2,96,128]{2,1,0:T(8,128)S(1)}, u32[]{:S(2)}, u32[]{:S(2)}) collective-permute-start(f32[2,96,128]{2,1,0:T(8,128)S(1)} %get-tuple-element.23), channel_id=1, source_target_pairs={{0,64},{1,65},{2,66},{3,67},{4,68},{5,69},{6,70},{7,71},{8,72},{9,... | collective-permute-start | bytes 294920 | tf_op jit(solution)/shard_map/ppermute | solution.py:282
  82.4 6.9 %collective-permute-start.5 = (f32[2,96,128]{2,1,0:T(8,128)S(1)}, f32[2,96,128]{2,1,0:T(8,128)S(1)}, u32[]{:S(2)}, u32[]{:S(2)}) collective-permute-start(f32[2,96,128]{2,1,0:T(8,128)S(1)} %get-tuple-element.24), channel_id=1, source_target_pairs={{0,32},{1,33},{2,34},{3,35},{4,36},{5,37},{6,38},{7,39},{8,40},{9,... | collective-permute-start | bytes 294920 | tf_op jit(solution)/shard_map/ppermute | solution.py:282
  87.6 5.1 %copy-start.3 = (f32[96,16,128]{2,1,0:T(8,128)S(1)}, f32[96,16,128]{2,1,0:T(8,128)}, u32[]{:S(2)}) copy-start(f32[96,16,128]{2,1,0:T(8,128)} %param.7) | copy-start | bytes 2359300

commit v2 on v1

v2 whole, which is shorter than its diff:
```python
import functools
import math

import jax
import jax.numpy as jnp
from jax import lax
from jax.experimental import pallas as pl
from jax.experimental.pallas import tpu as pltpu
from jax.sharding import Mesh
from jax.sharding import PartitionSpec as P

F32 = jnp.float32
BF16 = jnp.bfloat16
C = 96
R = 16
L = 128
HALF = L // 2
NT = (((1,), (1,)), ((), ()))

AXES = ("lat", "xh", "zr", "zd", "c")
LON = ("xh", "zr", "zd", "c")
NEAR = ("lat", "xh", "zd", "c")
FAR = ("zr",)

VMEM = pl.BlockSpec(memory_space=pltpu.VMEM)
ANY = pl.BlockSpec(memory_space=pl.ANY)


GRANT = (64 << 20) - 600 * 1024


def call(kernel, outs, args, scratch=(), after=(), specs=None, grant=40 << 20, flops=0, moved=0):
    def body(*refs):
        kernel(*refs[: len(args)], *refs[len(args) + len(after) :])

    return pl.pallas_call(
        body,
        out_shape=outs,
        in_specs=(specs or [VMEM] * len(args)) + [ANY] * len(after),
        out_specs=[VMEM] * len(outs),
        scratch_shapes=list(scratch),
        compiler_params=pltpu.CompilerParams(vmem_limit_bytes=grant),
        cost_estimate=pl.CostEstimate(flops=flops, bytes_accessed=moved, transcendentals=0),
    )(*args, *after)


def out(*shape):
    return jax.ShapeDtypeStruct(shape, F32)


def roll(value, by):
    by = by % L
    return value if by == 0 else pltpu.roll(value, by, 1)


def lanes():
    return lax.broadcasted_iota(jnp.int32, (C, L), 1)


def row(ref, r):
    return ref[pl.ds(r, C, stride=R), :]


def pick(flag, when_set, otherwise):
    return jnp.where(flag == 1, when_set, otherwise)


def split(value):
    high = value.astype(BF16)
    return high, (value - high.astype(F32)).astype(BF16)


def odd_lat():
    return lax.axis_index("lat") % 2


def at_end(place):
    return jnp.where(lax.axis_index("lat") == place, 1.0, 0.0)


def place_of(to):
    nlat = lax.axis_size("lat")
    half = lax.axis_index("xh")
    outside = jnp.logical_or(to < 0, to >= nlat)
    lat = jnp.clip(to, 0, nlat - 1)
    half = jnp.where(outside, 1 - half, half)
    return ((lat * 2 + half) * 2 + lax.axis_index("zd")) * 2 + lax.axis_index("c")


def lat_neighbours():
    lat = lax.axis_index("lat")
    return place_of(lat - 1), place_of(lat + 1)


class Chunks:
    CORNERS = 2

    def __init__(self, n):
        self.n = n
        self.tiles = 7 * C // 8
        self.rows = 4 * -(-(8 * self.tiles + 1) // (4 * n))

    def pieces(self, first, count):
        end = first + count
        while first < end:
            now = min(self.rows - first % self.rows, end - first)
            yield first // self.rows, first % self.rows, now
            first += now


PIECES = 4


def front_kernel(x, g, own_1, own_2, west, east, x_here, g_here, sems):
    step = C // PIECES
    copies = {}
    for k in range(PIECES):
        at = pl.ds(k * step * R, step * R)
        for part, (source, here) in enumerate(((x, x_here), (g, g_here))):
            copies[k, part] = pltpu.make_async_copy(source.at[at, :], here.at[at, :], sems.at[k, part])
            copies[k, part].start()
    odd = odd_lat()
    lane = lax.broadcasted_iota(jnp.int32, (step, L), 1)
    for k in range(PIECES):
        to = pl.ds(k * step, step)
        first = jnp.zeros((step, L), F32)
        last = jnp.zeros((step, L), F32)
        for part, here in enumerate((x_here, g_here)):
            copies[k, part].wait()
            base = HALF * part
            for r in range(R):
                value = here[pl.ds(k * step * R + r, step, stride=R), :]
                if r == 0:
                    top = value
                moved = roll(value, base + r + 1)
                last = jnp.where(lane == base + r, moved, last)
                first = jnp.where(lane == base + r + 1, moved, first)
            own_1[part, to, :] = pick(odd, top, value)
            own_2[part, to, :] = pick(odd, value, top)
        west[to, :] = roll(first, -1)
        east[to, :] = roll(last, 1)


def whole_column(east, row_1, row_2):
    lane = lanes()
    column = east[...]
    odd = odd_lat()
    for part in range(2):
        north = pick(odd, row_1[part], row_2[part])
        south = pick(odd, row_2[part], row_1[part])
        column = jnp.where(lane == HALF * part, roll(north, 1 + HALF * part), column)
        column = jnp.where(lane == HALF * part + R + 1, roll(south, HALF * part + R + 2), column)
    return column


def column_kernel(east, row_1, row_2, column):
    column[...] = whole_column(east, row_1, row_2)


def taps(value, west, west_lane, east, east_lane):
    lane = lanes()
    before = jnp.where(lane == 0, roll(west, -west_lane), roll(value, 1))
    after = jnp.where(lane == L - 1, roll(east, L - 1 - east_lane), roll(value, -1))
    return before, value, after


def nt(left, right):
    return lax.dot_general(left[...], right[...], NT, preferred_element_type=F32)


def three_products(c_hi, c_lo, s_hi, s_lo):
    grad = nt(c_hi, s_hi) + nt(c_hi, s_lo) + nt(c_lo, s_hi)
    return jnp.concatenate(
        [grad[a * C : (a + 1) * C] for a in range(3)] + [jnp.zeros((C, 7 * L - 9 * C), F32)], axis=1
    )


def inner_taps(value):
    lane = lanes()
    before = jnp.where(lane == 0, 0.0, roll(value, 1))
    after = jnp.where(lane == L - 1, 0.0, roll(value, -1))
    return before, value, after


def inner_weight_kernel(x, g, inner, bias, s_hi, s_lo, c_hi, c_lo):
    zero = jnp.zeros((C, L), F32)
    total = zero
    for r in range(R):
        at = pl.ds(r * L, L)
        for b, value in enumerate(inner_taps(row(x, r))):
            s_hi[pl.ds(b * C, C), at], s_lo[pl.ds(b * C, C), at] = split(value)
        here_hi, here_lo = split(row(g, r))
        total = total + row(g, r)
        for a in range(3):
            to = r + a - 1
            if 0 <= to < R:
                c_hi[pl.ds(a * C, C), pl.ds(to * L, L)] = here_hi
                c_lo[pl.ds(a * C, C), pl.ds(to * L, L)] = here_lo
    for a, to in ((0, R - 1), (2, 0)):
        c_hi[pl.ds(a * C, C), pl.ds(to * L, L)] = zero.astype(BF16)
        c_lo[pl.ds(a * C, C), pl.ds(to * L, L)] = zero.astype(BF16)
    inner[...] = three_products(c_hi, c_lo, s_hi, s_lo)
    bias[...] = jnp.zeros((8, L), F32)
    bias[:, pl.ds(0, C)] = lax.dot_general(
        jnp.ones((8, L), F32), total, NT, preferred_element_type=F32, precision=lax.Precision.HIGHEST
    )


def outer_weight_kernel(
    chunks, inner, bias, own_east, own_1, own_2, east, row_1, row_2, packed, s_hi, s_lo, c_hi, c_lo
):
    lane = lanes()
    zero = jnp.zeros((C, L), F32)
    odd = odd_lat()
    north = pick(odd, row_1[1], row_2[1])
    south = pick(odd, row_2[1], row_1[1])
    x_top = pick(odd, own_1[0], own_2[0])
    x_bottom = pick(odd, own_2[0], own_1[0])
    column = whole_column(own_east, row_1, row_2)
    beyond = east[...]
    at_top = at_end(0)
    at_bottom = at_end(lax.axis_size("lat") - 1)

    def put(k, left, right):
        at = pl.ds(k * L, L)
        for part, value in enumerate(left):
            c_hi[pl.ds(part * C, C), at], c_lo[pl.ds(part * C, C), at] = split(value)
        for part, value in enumerate(right):
            s_hi[pl.ds(part * C, C), at], s_lo[pl.ds(part * C, C), at] = split(value)

    put(0, (north * at_top, zero, north * (1.0 - at_top)), inner_taps(x_top))
    put(1, (south * (1.0 - at_bottom), zero, south * at_bottom), inner_taps(x_bottom))
    g_column = roll(column, -HALF)
    below = roll(g_column, -2)
    above = g_column
    south_end = jnp.where(lane == R - 1, below * at_bottom, 0.0)
    north_end = jnp.where(lane == 0, above * at_top, 0.0)
    put(
        2,
        (below - south_end + north_end, roll(g_column, -1), above - north_end + south_end),
        (zero, zero, jnp.where(lane < R, beyond, 0.0)),
    )
    g_beyond = jnp.where(lane < R, roll(beyond, -HALF), 0.0)
    put(
        3,
        (g_beyond, roll(g_beyond, 1), roll(g_beyond, 2)),
        (jnp.where(lane < R + 2, column, 0.0), zero, zero),
    )
    wide = inner[...] + three_products(c_hi, c_lo, s_hi, s_lo)
    height = chunks.rows + chunks.CORNERS
    for tile in range(chunks.tiles):
        i, j = divmod(tile, 7)
        at = 8 * i
        for chunk, place, count in chunks.pieces(8 * tile, 8):
            packed[pl.ds(chunk * height + place, count), :] = wide[at : at + count, L * j : L * j + L]
            at += count
    at = 0
    for chunk, place, count in chunks.pieces(8 * chunks.tiles, 8):
        packed[pl.ds(chunk * height + place, count), :] = bias[pl.ds(at, count), :]
        at += count
    for chunk, place, count in chunks.pieces(
        8 * chunks.tiles + 8, chunks.n * chunks.rows - 8 * chunks.tiles - 8
    ):
        packed[pl.ds(chunk * height + place, count), :] = jnp.zeros((count, L), F32)

    cells = zero
    for k, at in enumerate((0, HALF, R - 1, HALF + R - 1)):
        cells = jnp.where(lane == k, roll(beyond, k - at), cells)
    cells = jnp.concatenate([cells, jnp.zeros((L - C, L), F32)], axis=0).T
    to_north, to_south = lat_neighbours()
    for chunk in range(chunks.n):
        value = jnp.where(to_north == chunk, cells[0:2], 0.0)
        value = jnp.where(to_south == chunk, cells[2:4], value)
        packed[pl.ds(chunk * height + chunks.rows, chunks.CORNERS), :] = value


def unpack_kernel(tiles, factor, gathered, weight_grad, bias_grad):
    for tile in range(tiles):
        i, j = divmod(tile, 7)
        width = min(L, 9 * C - L * j)
        value = gathered[pl.ds(8 * tile, 8), :] * factor
        weight_grad[pl.ds(8 * i, 8), pl.ds(L * j, width)] = value[:, :width]
    bias_grad[...] = gathered[pl.ds(8 * tiles, 1), :][:, :C] * factor


def conv_kernel(
    is_grad, field, west, east, row_1, row_2, weight, bias, parts, result, token, hi, lo, ends, sems
):
    part = 1 if is_grad else 0
    copies = [
        pltpu.make_async_copy(
            parts.at[at, :, pl.ds(parts.shape[2] - 2 * L, 2 * L)], ends.at[k], sems.at[k]
        )
        for k, at in enumerate(lat_neighbours())
    ]
    for copy in copies:
        copy.start()
    odd = odd_lat()
    north = pick(odd, row_1[part], row_2[part])
    south = pick(odd, row_2[part], row_1[part])
    for copy in copies:
        copy.wait()
    corners = [ends[k][:, at : at + L] for k in range(2) for at in (0, L)]
    corners = jnp.concatenate(corners + [jnp.zeros((L - 4, L), F32)], axis=0).T[:C]
    first = HALF * part

    def shifts(r):
        if r < 0:
            return taps(north, west[...], first + r + 1, corners, part)
        if r >= R:
            return taps(south, west[...], first + r + 1, corners, 2 + part)
        return taps(row(field, r), west[...], first + r + 1, east[...], first + r)

    def put(block, half, values):
        for b, value in enumerate(values):
            at = (pl.ds((3 * block + b) * C, C), pl.ds(half * L, L))
            hi[at], lo[at] = split(value)

    half = R // 2
    if is_grad:
        at_top = at_end(0)
        at_bottom = at_end(lax.axis_size("lat") - 1)
        outer_top = shifts(-1)
        outer_bottom = shifts(R)
        put(0, 0, [v * (1.0 - at_top) for v in outer_top])
        put(0, 1, shifts(half - 1))
        put(1, 0, shifts(0))
        put(1, 1, shifts(half))
        put(2, 0, [v + o * at_top for v, o in zip(shifts(1), outer_top)])
        put(2, 1, shifts(half + 1))
        for r in range(half):
            put(3 + r, 0, shifts(r))
            put(3 + r, 1, shifts(r + half))
        k = 3 + half
        put(k, 0, shifts(half - 2))
        put(k, 1, [v + o * at_bottom for v, o in zip(shifts(R - 2), outer_bottom)])
        put(k + 1, 0, shifts(half - 1))
        put(k + 1, 1, shifts(R - 1))
        put(k + 2, 0, shifts(half))
        put(k + 2, 1, [v * (1.0 - at_bottom) for v in outer_bottom])
        starts = [0] + [2 + r for r in range(1, half - 1)] + [k]
    else:
        for j in range(half + 2):
            put(j, 0, shifts(j - 1))
            put(j, 1, shifts(j - 1 + half))
        starts = list(range(half))
    w_hi, w_lo = split(weight[...])
    both = jnp.concatenate([w_hi, w_lo], axis=0)
    for r, start in enumerate(starts):
        at = pl.ds(start * 3 * C, 9 * C)
        first = jnp.dot(both, hi[at, :], preferred_element_type=F32)
        second = jnp.dot(w_hi, lo[at, :], preferred_element_type=F32)
        value = first[:C] + first[C:] + second
        if not is_grad:
            value = value + bias[...]
        result[pl.ds(r, C, stride=R), :] = value[:, :L]
        result[pl.ds(r + half, C, stride=R), :] = value[:, L:]
    token[...] = jnp.zeros((8, L), F32)


def conv(is_grad, *args, after=()):
    blocks = 3 + R // 2 + 3 if is_grad else R // 2 + 2
    scratch = pltpu.VMEM((blocks * 3 * C, 2 * L), BF16)
    return call(
        functools.partial(conv_kernel, is_grad),
        [out(C * R, L), out(8, L)],
        args,
        [scratch, scratch, pltpu.VMEM((2, 1, 2 * L), F32), pltpu.SemaphoreType.DMA((2,))],
        after,
        specs=[VMEM] * (len(args) - 1) + [ANY],
        flops=6 * 9 * C * C * R * L,
        moved=3 * 4 * C * R * L,
    )


def shards(nlat, nlon, factor, x, weight, bias, g):
    x = x.reshape(C * R, L)
    g = g.reshape(C * R, L)

    def pairs_of(partner):
        pairs = []
        for i in range(nlat):
            for j in range(nlon):
                to_lat, to_lon = partner(i, j)
                pairs.append((i * nlon + j, to_lat * nlon + to_lon))
        return pairs

    def across_2(i, j):
        to = i + 1 if i % 2 else i - 1
        return (to, j) if 0 <= to < nlat else (i, (j + nlon // 2) % nlon)

    to_west = pairs_of(lambda i, j: (i, (j - 1) % nlon))
    to_east = pairs_of(lambda i, j: (i, (j + 1) % nlon))
    first = pairs_of(lambda i, j: (i ^ 1, j))
    second = pairs_of(across_2)

    def send(value, pairs):
        return lax.ppermute(value, AXES, pairs)

    block = 4 * C * R * L
    product = 6 * 9 * C * C * R * L
    own_1, own_2, own_west, own_east = call(
        front_kernel,
        [out(2, C, L)] * 2 + [out(C, L)] * 2,
        (x, g),
        [pltpu.VMEM((C * R, L), F32)] * 2 + [pltpu.SemaphoreType.DMA((PIECES, 2))],
        specs=[ANY] * 2,
        grant=GRANT,
        flops=block,
        moved=2 * block,
    )
    row_2 = send(own_2, second)
    row_1 = send(own_1, first)
    east = send(own_west, to_west)
    inner_sum, bias_sum = call(
        inner_weight_kernel,
        [out(C, 7 * L), out(8, L)],
        (x, g),
        [pltpu.VMEM((3 * C, R * L), BF16)] * 4,
        after=(own_west,),
        flops=product,
        moved=2 * block,
    )

    n_far = lax.axis_size(FAR)
    n_near = nlat * nlon // n_far
    chunks = Chunks(n_near)
    height = chunks.rows + chunks.CORNERS
    packed = call(
        functools.partial(outer_weight_kernel, chunks),
        [out(n_near * height, L)],
        (inner_sum, bias_sum, own_east, own_1, own_2, east, row_1, row_2),
        [pltpu.VMEM((3 * C, 4 * L), BF16)] * 4,
        flops=product // 4,
        moved=block,
    )[0]
    parts = lax.all_to_all(packed.reshape(n_near, 1, height * L), NEAR, 0, 0)
    column = call(column_kernel, [out(C, L)], (own_east, row_1, row_2), after=(packed,))[0]
    west = send(column, to_east)
    parts, west = lax.optimization_barrier((parts, west))
    mine = jnp.sum(parts[:, :, : chunks.rows * L], axis=0, keepdims=True)
    others = lax.all_to_all(jnp.broadcast_to(mine, (n_far, 1, chunks.rows * L)), FAR, 0, 0)
    flipped = weight.reshape(C, 3, 3, C)[:, ::-1, ::-1].transpose(3, 1, 2, 0).reshape(C, 9 * C)
    halo = (west, east, row_1, row_2)
    bias = bias.reshape(C, 1)
    output, token = conv(False, x, *halo, weight, bias, parts)
    others, token = lax.optimization_barrier((others, token))
    mine = jnp.sum(others, axis=0, keepdims=True)
    mine = jnp.broadcast_to(mine, (n_near, 1, chunks.rows * L))
    gathered = lax.all_to_all(mine, NEAR, 0, 0)
    grad, _ = conv(True, g, *halo, flipped, bias, parts, after=(mine,))
    weight_grad, bias_grad = call(
        functools.partial(unpack_kernel, chunks.tiles, factor),
        [out(C, 9 * C), out(1, C)],
        (gathered.reshape(n_near * chunks.rows, L),),
        moved=block,
    )
    return (
        output.reshape(C, R, L),
        grad.reshape(C, R, L),
        weight_grad,
        bias_grad.reshape(C),
    )


def solution(mesh):
    nlat, nlon = mesh.shape["lat"], mesh.shape["lon"]
    fine = Mesh(mesh.devices.reshape(nlat, 2, nlon // 8, 2, 2), AXES)
    factor = 1.0 / math.sqrt(nlat * R * nlon * L)
    field = P(None, "lat", LON)
    return jax.shard_map(
        functools.partial(shards, nlat, nlon, factor),
        mesh=fine,
        in_specs=(field, P(), P(), field),
        out_specs=(field, field, P(), P()),
        check_vma=False,
    )
```

time: 99.7 us -> 87 us (0.87)
  blocking collectives: 43.3 us -> 17.5 us
  starting transfers between devices: 28.3 us -> 36.3 us
  waiting for transfers between devices: 5.83 us -> 10.8 us
  local copies, waits for them, and re-layouts: 4.58 us -> 6.17 us
    all_to_all x2 -> x1, blocking collectives: 43.3 us -> 17.5 us  [shards(): lax.all_to_all(jnp.broadcast_to(mine, (n_far, 1, chunks.rows * L)), FAR,...]
    all_to_all x1 -> x2, starting transfers between devices: 5.6 us -> 20.1 us  [the longest x1 13.7 us: shards(): parts = lax.all_to_all(packed.reshape(n_near, 1, height * L), NEAR, 0, 0)]
    all_to_all x1 -> x2, waiting for transfers between devices: 0.01 us -> 8.55 us  [the longest x1 6 us: shards(): parts = lax.all_to_all(packed.reshape(n_near, 1, height * L), NEAR, 0, 0)]
    ppermute x6 -> x4, starting transfers between devices: 22.7 us -> 16.2 us  [send(): return lax.ppermute(value, AXES, pairs)]
    ppermute x6 -> x4, waiting for transfers between devices: 5.83 us -> 2.21 us  [send(): return lax.ppermute(value, AXES, pairs)]
    unnamed x12 -> x21, local copies, waits for them, and re-layouts: 2.93 us -> 4.67 us
    pallas_call x6 -> x7, Pallas kernels: 14.9 us -> 14.6 us  [call(): pl.pallas_call(body, out_shape=outs, in_specs=(specs or [VMEM] * len(args...]
  transfers between devices with their start and end apart: 7 -> 6, of which waited for: 3 -> 3; matrix products, arithmetic and copies ran while one was open for 1% -> 1% of each run, Pallas kernels for 8% -> 11%
where the time goes in v2:
time: 87 us; the launch traced here: 86.3 us
  starting transfers between devices  36.3 us (42%)
  blocking collectives  17.5 us (20%)
  Pallas kernels  14.6 us (17%)
  waiting for transfers between devices  10.8 us (12%)
  local copies, waits for them, and re-layouts  6.17 us (7%)
    all_to_all x1, blocking collectives, shards(): lax.all_to_all(jnp.broadcast_to(mine, (n_far, 1, chunks.rows * L)), FAR,...  17.5 us
    ppermute x4, starting transfers between devices, send(): return lax.ppermute(value, AXES, pairs)  16.2 us
    pallas_call x7, Pallas kernels, call(): pl.pallas_call(body, out_shape=outs, in_specs=(specs or [VMEM] * len(args...  14.6 us
    all_to_all x1, starting transfers between devices, shards(): parts = lax.all_to_all(packed.reshape(n_near, 1, height * L), NEAR, 0, 0)  13.7 us
    all_to_all x1, starting transfers between devices, shards(): gathered = lax.all_to_all(mine, NEAR, 0, 0)  6.39 us
    all_to_all x1, waiting for transfers between devices, shards(): parts = lax.all_to_all(packed.reshape(n_near, 1, height * L), NEAR, 0, 0)  6 us
    unnamed x21, local copies, waits for them, and re-layouts  4.67 us
    all_to_all x1, waiting for transfers between devices, shards(): gathered = lax.all_to_all(mine, NEAR, 0, 0)  2.55 us
  transfers between devices with their start and end apart: 6, of which 3 were waited for; matrix products, arithmetic and copies ran while one was open for 1% of the time, Pallas kernels for 11%

profile of v2, /device:TPU:1, one launch (start us, length us, event | category | flops | bytes accessed | tf_op | source)
XLA Modules:
  0.0 86.3 jit_solution(10971327103558576055)
XLA Ops:
  0.6 2.9 %shard_map.75 = (f32[2,96,128]{2,1,0:T(8,128)}, f32[2,96,128]{2,1,0:T(8,128)}, f32[96,128]{1,0:T(8,128)}, f32[96,128]{1,0:T(8,128)}) custom-call(f32[1536,128]{1,0:T(8,128)} %bitcast.13, f32[1536,128]{1,0:T(8,128)} %bitcast.16), custom_call_target="tpu_custom_call" | custom-call | flops 786432 | bytes 1572864 | tf_op jit(solution)/shard_map/pallas_call | solution.py:36
  3.6 4.0 %collective-permute-start.1 = (f32[2,96,128]{2,1,0:T(8,128)}, f32[2,96,128]{2,1,0:T(8,128)S(1)}, u32[]{:S(2)}, u32[]{:S(2)}) collective-permute-start(f32[2,96,128]{2,1,0:T(8,128)} %get-tuple-element.20.refs_3_), channel_id=1, source_target_pairs={{0,64},{1,65},{2,66},{3,67},{4,68},{5,69},{6,70},{7,71},{8,72},{9,... | collective-permute-start | bytes 294920 | tf_op jit(solution)/shard_map/ppermute | solution.py:398
  7.6 4.7 %collective-permute-start.2 = (f32[2,96,128]{2,1,0:T(8,128)}, f32[2,96,128]{2,1,0:T(8,128)S(1)}, u32[]{:S(2)}, u32[]{:S(2)}) collective-permute-start(f32[2,96,128]{2,1,0:T(8,128)} %get-tuple-element.21.refs_4_), channel_id=1, source_target_pairs={{0,32},{1,33},{2,34},{3,35},{4,36},{5,37},{6,38},{7,39},{8,40},{9,... | collective-permute-start | bytes 294920 | tf_op jit(solution)/shard_map/ppermute | solution.py:398
  12.3 3.9 %collective-permute-start = (f32[96,128]{1,0:T(8,128)}, f32[96,128]{1,0:T(8,128)S(1)}, u32[]{:S(2)}, u32[]{:S(2)}) collective-permute-start(f32[96,128]{1,0:T(8,128)} %get-tuple-element.16.refs_2_), channel_id=1, source_target_pairs={{0,63},{1,0},{2,1},{3,2},{4,3},{5,4},{6,5},{7,6},{8,7},{9,8},{10,9... | collective-permute-start | bytes 147464 | tf_op jit(solution)/shard_map/ppermute | solution.py:398
  16.2 0.0 copy-start
  16.2 1.1 %copy-done = f32[96,16,128]{2,1,0:T(8,128)S(1)} copy-done((f32[96,16,128]{2,1,0:T(8,128)S(1)}, f32[96,16,128]{2,1,0:T(8,128)}, u32[]{:S(2)}) %copy-start) | copy-done | bytes 786456
  17.3 0.0 copy-start.2
  17.3 1.1 %copy-done.2 = f32[96,16,128]{2,1,0:T(8,128)S(1)} copy-done((f32[96,16,128]{2,1,0:T(8,128)S(1)}, f32[96,16,128]{2,1,0:T(8,128)}, u32[]{:S(2)}) %copy-start.2) | copy-done | bytes 786456
  18.5 0.0 copy-start.8
  18.5 0.8 copy-done.8
  19.3 0.0 copy-start.5
  19.3 0.0 copy-start.6
  19.3 0.0 copy-start.7
  19.3 2.7 %shard_map.76 = (f32[96,896]{1,0:T(8,128)S(1)}, f32[8,128]{1,0:T(8,128)S(1)}) custom-call(f32[1536,128]{1,0:T(8,128)S(1)} %bitcast.14, f32[1536,128]{1,0:T(8,128)S(1)} %bitcast.17, f32[96,128]{1,0:T(8,128)S(1)} %copy-done.8), custom_call_target="tpu_custom_call" | custom-call | flops 1019215872 | bytes 1572864 | tf_op jit(solution)/shard_map/pallas_call | solution.py:36
  21.9 0.0 collective-permute-done.refs_5_.refs_2_
  21.9 0.0 collective-permute-done.1.refs_6_.refs_1_.refs_3_
  22.0 0.0 collective-permute-done.2.refs_7_.refs_2_.refs_4_
  22.0 0.0 copy-done.5
  22.0 0.0 copy-done.6
  22.0 0.0 copy-done.7
  22.0 1.8 %shard_map.77.refs_3_ = f32[896,128]{1,0:T(8,128)} custom-call(f32[96,896]{1,0:T(8,128)S(1)} %get-tuple-element.17.refs_0_, f32[8,128]{1,0:T(8,128)S(1)} %get-tuple-element.18.refs_1_, f32[96,128]{1,0:T(8,128)S(1)} %copy-done.5, f32[2,96,128]{2,1,0:T(8,128)S(1)} %copy-done.6, f32[2,96,128]{2,1,0:T(8,128)S(1)} %copy-done.7, ...), custom_call_target="tpu_custom_call" | custom-call | flops 254803968 | bytes 786432 | tf_op jit(solution)/shard_map/pallas_call | solution.py:36
  23.8 13.7 %all-to-all-start = ((f32[64,1,1792]{2,1,0:T(1,128)}), f32[64,1,1792]{2,1,0:T(1,128)S(1)}, u32[]{:S(2)}, u32[]{:S(2)}) async-start(f32[64,1,1792]{2,1,0:T(1,128)} %bitcast.2), calls=%async_computation | async-start | bytes 917504 | tf_op jit(solution)/shard_map/all_to_all | solution.py:437
  37.6 0.1 shard_map.78
  37.7 3.5 %collective-permute-start.3 = (f32[96,128]{1,0:T(8,128)S(1)}, f32[96,128]{1,0:T(8,128)S(1)}, u32[]{:S(2)}, u32[]{:S(2)}) collective-permute-start(f32[96,128]{1,0:T(8,128)S(1)} %shard_map.78), channel_id=1, source_target_pairs={{0,1},{1,2},{2,3},{3,4},{4,5},{5,6},{6,7},{7,8},{8,9},{9,10},{10,1... | collective-permute-start | bytes 147464 | tf_op jit(solution)/shard_map/ppermute | solution.py:398
  41.3 2.2 %collective-permute-done.3.refs_1_ = f32[96,128]{1,0:T(8,128)S(1)} collective-permute-done((f32[96,128]{1,0:T(8,128)S(1)}, f32[96,128]{1,0:T(8,128)S(1)}, u32[]{:S(2)}, u32[]{:S(2)}) %collective-permute-start.3) | collective-permute-done | bytes 49184 | tf_op jit(solution)/shard_map/ppermute | solution.py:398
  43.4 6.0 %all-to-all-done.refs_7_ = f32[64,1,1792]{2,1,0:T(1,128)S(1)} async-done(((f32[64,1,1792]{2,1,0:T(1,128)}), f32[64,1,1792]{2,1,0:T(1,128)S(1)}, u32[]{:S(2)}, u32[]{:S(2)}) %all-to-all-start) | async-done | bytes 458784 | tf_op jit(solution)/shard_map/all_to_all | solution.py:437
  49.4 0.2 slice_reduce_fusion
  49.7 17.5 %all_to_all.15 = f32[8,1,1536]{2,1,0:T(1,128)S(1)} all-to-all(f32[8,1,1536]{2,1,0:T(1,128)S(1)} %broadcast_in_dim.4), channel_id=1, replica_groups=mesh['lat'=8,'xh'=2,'zr'=8,'zd'=2,'c'=2] {'zr'}, dimensions={0} | all-to-all | bytes 98304 | tf_op jit(solution)/shard_map/all_to_all | solution.py:442
  67.2 1.0 %broadcast_in_dim.5.refs_8_ = f32[64,1,1536]{2,1,0:T(1,128)} broadcast(f32[1536]{0:T(1024)S(1)} %reduce_sum.19), dimensions={2} | broadcast | bytes 399360 | tf_op jit(solution)/shard_map/broadcast_in_dim | solution.py:449
  68.1 0.0 copy-start.4
  68.1 6.4 %all-to-all-start.2 = ((f32[64,1,1536]{2,1,0:T(1,128)}), f32[64,1,1536]{2,1,0:T(1,128)S(1)}, u32[]{:S(2)}, u32[]{:S(2)}) async-start(f32[64,1,1536]{2,1,0:T(1,128)} %broadcast_in_dim.5.refs_8_), calls=%async_computation.2 | async-start | bytes 786432 | tf_op jit(solution)/shard_map/all_to_all | solution.py:450
  74.5 0.0 copy-start.9
  74.5 0.6 copy-done.9
  75.2 0.1 copy.11.refs_6_
  75.3 0.0 copy-done.4
  75.3 0.2 copy.12
  75.5 0.0 copy-start.1
  75.5 0.2 copy.13
  75.7 0.2 copy.14.refs_5_
  75.9 0.7 copy-done.1
  76.7 0.0 copy-start.3
  76.7 3.0 %shard_map.79 = (f32[1536,128]{1,0:T(8,128)}, f32[8,128]{1,0:T(8,128)}) custom-call(f32[1536,128]{1,0:T(8,128)S(1)} %bitcast.15, f32[96,128]{1,0:T(8,128)S(1)} %collective-permute-done.3.refs_1_, f32[96,128]{1,0:T(8,128)S(1)} %collective-permute-done.refs_5_.refs_2_, f32[2,96,128]{2,1,0:T(8,128)S(1)} %collective-permute-done.1.refs_6_.refs_1_.refs_3_, ...), custom_call_target="tpu_custom_call" | custom-call | flops 1019215872 | bytes 2359296 | tf_op jit(solution)/shard_map/pallas_call | solution.py:36
  79.6 0.0 copy-done.3
  79.7 3.4 %shard_map.80 = (f32[1536,128]{1,0:T(8,128)}, f32[8,128]{1,0:T(8,128)}) custom-call(f32[1536,128]{1,0:T(8,128)S(1)} %bitcast.18, f32[96,128]{1,0:T(8,128)S(1)} %collective-permute-done.3.refs_1_, f32[96,128]{1,0:T(8,128)S(1)} %collective-permute-done.refs_5_.refs_2_, f32[2,96,128]{2,1,0:T(8,128)S(1)} %collective-permute-done.1.refs_6_.refs_1_.refs_3_, ...), custom_call_target="tpu_custom_call" | custom-call | flops 1019215872 | bytes 2359296 | tf_op jit(solution)/shard_map/pallas_call | solution.py:36
  83.0 2.6 %all-to-all-done.2 = f32[64,1,1536]{2,1,0:T(1,128)S(1)} async-done(((f32[64,1,1536]{2,1,0:T(1,128)}), f32[64,1,1536]{2,1,0:T(1,128)S(1)}, u32[]{:S(2)}, u32[]{:S(2)}) %all-to-all-start.2) | async-done | bytes 393248 | tf_op jit(solution)/shard_map/all_to_all | solution.py:450
  85.6 0.8 shard_map.81
  (3 shorter events, 0.1 us)
Async XLA Ops:
  3.6 18.4 %collective-permute-start.1 = (f32[2,96,128]{2,1,0:T(8,128)}, f32[2,96,128]{2,1,0:T(8,128)S(1)}, u32[]{:S(2)}, u32[]{:S(2)}) collective-permute-start(f32[2,96,128]{2,1,0:T(8,128)} %get-tuple-element.20.refs_3_), channel_id=1, source_target_pairs={{0,64},{1,65},{2,66},{3,67},{4,68},{5,69},{6,70},{7,71},{8,72},{9,... | collective-permute-start | bytes 294920 | tf_op jit(solution)/shard_map/ppermute | solution.py:398
  7.6 14.4 %collective-permute-start.2 = (f32[2,96,128]{2,1,0:T(8,128)}, f32[2,96,128]{2,1,0:T(8,128)S(1)}, u32[]{:S(2)}, u32[]{:S(2)}) collective-permute-start(f32[2,96,128]{2,1,0:T(8,128)} %get-tuple-element.21.refs_4_), channel_id=1, source_target_pairs={{0,32},{1,33},{2,34},{3,35},{4,36},{5,37},{6,38},{7,39},{8,40},{9,... | collective-permute-start | bytes 294920 | tf_op jit(solution)/shard_map/ppermute | solution.py:398
  12.3 9.7 %collective-permute-start = (f32[96,128]{1,0:T(8,128)}, f32[96,128]{1,0:T(8,128)S(1)}, u32[]{:S(2)}, u32[]{:S(2)}) collective-permute-start(f32[96,128]{1,0:T(8,128)} %get-tuple-element.16.refs_2_), channel_id=1, source_target_pairs={{0,63},{1,0},{2,1},{3,2},{4,3},{5,4},{6,5},{7,6},{8,7},{9,8},{10,9... | collective-permute-start | bytes 147464 | tf_op jit(solution)/shard_map/ppermute | solution.py:398
  16.2 1.1 %copy-start = (f32[96,16,128]{2,1,0:T(8,128)S(1)}, f32[96,16,128]{2,1,0:T(8,128)}, u32[]{:S(2)}) copy-start(f32[96,16,128]{2,1,0:T(8,128)} %param.4) | copy-start | bytes 2359300
  17.3 1.1 %copy-start.2 = (f32[96,16,128]{2,1,0:T(8,128)S(1)}, f32[96,16,128]{2,1,0:T(8,128)}, u32[]{:S(2)}) copy-start(f32[96,16,128]{2,1,0:T(8,128)} %param.7) | copy-start | bytes 2359300
  18.5 0.8 copy-start.8
  19.3 2.7 %copy-start.5 = (f32[96,128]{1,0:T(8,128)S(1)}, f32[96,128]{1,0:T(8,128)}, u32[]{:S(2)}) copy-start(f32[96,128]{1,0:T(8,128)} %get-tuple-element.19.refs_2_.refs_0_) | copy-start | bytes 147460
  19.3 2.7 %copy-start.6 = (f32[2,96,128]{2,1,0:T(8,128)S(1)}, f32[2,96,128]{2,1,0:T(8,128)}, u32[]{:S(2)}) copy-start(f32[2,96,128]{2,1,0:T(8,128)} %get-tuple-element.20.refs_3_) | copy-start | bytes 294916
  19.3 2.7 %copy-start.7 = (f32[2,96,128]{2,1,0:T(8,128)S(1)}, f32[2,96,128]{2,1,0:T(8,128)}, u32[]{:S(2)}) copy-start(f32[2,96,128]{2,1,0:T(8,128)} %get-tuple-element.21.refs_4_) | copy-start | bytes 294916
  23.8 25.6 %all-to-all-start = ((f32[64,1,1792]{2,1,0:T(1,128)}), f32[64,1,1792]{2,1,0:T(1,128)S(1)}, u32[]{:S(2)}, u32[]{:S(2)}) async-start(f32[64,1,1792]{2,1,0:T(1,128)} %bitcast.2), calls=%async_computation | async-start | bytes 917504 | tf_op jit(solution)/shard_map/all_to_all | solution.py:437
  37.7 5.7 %collective-permute-start.3 = (f32[96,128]{1,0:T(8,128)S(1)}, f32[96,128]{1,0:T(8,128)S(1)}, u32[]{:S(2)}, u32[]{:S(2)}) collective-permute-start(f32[96,128]{1,0:T(8,128)S(1)} %shard_map.78), channel_id=1, source_target_pairs={{0,1},{1,2},{2,3},{3,4},{4,5},{5,6},{6,7},{7,8},{8,9},{9,10},{10,1... | collective-permute-start | bytes 147464 | tf_op jit(solution)/shard_map/ppermute | solution.py:398
  68.1 7.2 %copy-start.4 = (f32[96,864]{1,0:T(8,128)S(1)}, f32[96,864]{1,0:T(8,128)}, u32[]{:S(2)}) copy-start(f32[96,864]{1,0:T(8,128)} %refs_5_.1) | copy-start | bytes 995332
  68.1 17.5 %all-to-all-start.2 = ((f32[64,1,1536]{2,1,0:T(1,128)}), f32[64,1,1536]{2,1,0:T(1,128)S(1)}, u32[]{:S(2)}, u32[]{:S(2)}) async-start(f32[64,1,1536]{2,1,0:T(1,128)} %broadcast_in_dim.5.refs_8_), calls=%async_computation.2 | async-start | bytes 786432 | tf_op jit(solution)/shard_map/all_to_all | solution.py:450
  74.5 0.7 copy-start.9
  75.5 1.1 %copy-start.1 = (f32[96,16,128]{2,1,0:T(8,128)S(1)}, f32[96,16,128]{2,1,0:T(8,128)}, u32[]{:S(2)}) copy-start(f32[96,16,128]{2,1,0:T(8,128)} %param.4) | copy-start | bytes 2359300
  76.7 3.0 %copy-start.3 = (f32[96,16,128]{2,1,0:T(8,128)S(1)}, f32[96,16,128]{2,1,0:T(8,128)}, u32[]{:S(2)}) copy-start(f32[96,16,128]{2,1,0:T(8,128)} %param.7) | copy-start | bytes 2359300

commit v3 on v2

--- a/solution.py
+++ b/solution.py
@@ -24,9 +24,6 @@
 
 VMEM = pl.BlockSpec(memory_space=pltpu.VMEM)
 ANY = pl.BlockSpec(memory_space=pl.ANY)
-
-
-GRANT = (64 << 20) - 600 * 1024
 
 
 def call(kernel, outs, args, scratch=(), after=(), specs=None, grant=40 << 20, flops=0, moved=0):
@@ -48,6 +45,14 @@
     return jax.ShapeDtypeStruct(shape, F32)
 
 
+def kept(*shape):
+    return pltpu.VMEM(shape, F32)
+
+
+def in_hbm(value):
+    return pltpu.with_memory_space_constraint(value, pltpu.HBM)
+
+
 def roll(value, by):
     by = by % L
     return value if by == 0 else pltpu.roll(value, by, 1)
@@ -78,47 +83,30 @@
     return jnp.where(lax.axis_index("lat") == place, 1.0, 0.0)
 
 
-def place_of(to):
-    nlat = lax.axis_size("lat")
-    half = lax.axis_index("xh")
-    outside = jnp.logical_or(to < 0, to >= nlat)
-    lat = jnp.clip(to, 0, nlat - 1)
-    half = jnp.where(outside, 1 - half, half)
-    return ((lat * 2 + half) * 2 + lax.axis_index("zd")) * 2 + lax.axis_index("c")
-
-
-def lat_neighbours():
-    lat = lax.axis_index("lat")
-    return place_of(lat - 1), place_of(lat + 1)
-
-
 class Chunks:
-    CORNERS = 2
-
     def __init__(self, n):
         self.n = n
         self.tiles = 7 * C // 8
-        self.rows = 4 * -(-(8 * self.tiles + 1) // (4 * n))
-
-    def pieces(self, first, count):
-        end = first + count
-        while first < end:
-            now = min(self.rows - first % self.rows, end - first)
-            yield first // self.rows, first % self.rows, now
-            first += now
-
-
-PIECES = 4
-
-
-def front_kernel(x, g, own_1, own_2, west, east, x_here, g_here, sems):
-    step = C // PIECES
+        self.rows = -(-(8 * self.tiles + 1) // n)
+
+
+PIECES = 3
+
+
+def stream(x, g, x_here, g_here, sems):
+    size = C * R // PIECES
     copies = {}
     for k in range(PIECES):
-        at = pl.ds(k * step * R, step * R)
+        at = pl.ds(k * size, size)
         for part, (source, here) in enumerate(((x, x_here), (g, g_here))):
             copies[k, part] = pltpu.make_async_copy(source.at[at, :], here.at[at, :], sems.at[k, part])
             copies[k, part].start()
+    return copies
+
+
+def front_kernel(x, g, own_1, own_2, west, east, done, x_here, g_here, sems):
+    step = C // PIECES
+    copies = stream(x, g, x_here, g_here, sems)
     odd = odd_lat()
     lane = lax.broadcasted_iota(jnp.int32, (step, L), 1)
     for k in range(PIECES):
@@ -139,6 +127,7 @@
             own_2[part, to, :] = pick(odd, value, top)
         west[to, :] = roll(first, -1)
         east[to, :] = roll(last, 1)
+    done[...] = jnp.zeros((8, L), F32)
 
 
 def whole_column(east, row_1, row_2):
@@ -153,8 +142,17 @@
     return column
 
 
-def column_kernel(east, row_1, row_2, column):
-    column[...] = whole_column(east, row_1, row_2)
+def columns_kernel(own_east, row_1, row_2, column, corners):
+    column[...] = whole_column(own_east, row_1, row_2)
+    lane = lanes()
+    odd = odd_lat()
+    value = jnp.zeros((C, L), F32)
+    for part in range(2):
+        north = pick(odd, row_1[part], row_2[part])
+        south = pick(odd, row_2[part], row_1[part])
+        value = jnp.where(lane == HALF * part, roll(north, HALF * part), value)
+        value = jnp.where(lane == HALF * part + 1, roll(south, HALF * part + 1), value)
+    corners[...] = value
 
 
 def taps(value, west, west_lane, east, east_lane):
@@ -168,8 +166,7 @@
     return lax.dot_general(left[...], right[...], NT, preferred_element_type=F32)
 
 
-def three_products(c_hi, c_lo, s_hi, s_lo):
-    grad = nt(c_hi, s_hi) + nt(c_hi, s_lo) + nt(c_lo, s_hi)
+def wide_form(grad):
     return jnp.concatenate(
         [grad[a * C : (a + 1) * C] for a in range(3)] + [jnp.zeros((C, 7 * L - 9 * C), F32)], axis=1
     )
@@ -182,27 +179,47 @@
     return before, value, after
 
 
-def inner_weight_kernel(x, g, inner, bias, s_hi, s_lo, c_hi, c_lo):
-    zero = jnp.zeros((C, L), F32)
-    total = zero
-    for r in range(R):
-        at = pl.ds(r * L, L)
-        for b, value in enumerate(inner_taps(row(x, r))):
-            s_hi[pl.ds(b * C, C), at], s_lo[pl.ds(b * C, C), at] = split(value)
-        here_hi, here_lo = split(row(g, r))
-        total = total + row(g, r)
-        for a in range(3):
-            to = r + a - 1
-            if 0 <= to < R:
-                c_hi[pl.ds(a * C, C), pl.ds(to * L, L)] = here_hi
-                c_lo[pl.ds(a * C, C), pl.ds(to * L, L)] = here_lo
+def inner_weight_kernel(x, g, inner, bias, x_here, g_here, sems, s_both, c_hi, c_lo):
+    step = C // PIECES
+    copies = stream(x, g, x_here, g_here, sems)
+    lane = lax.broadcasted_iota(jnp.int32, (step, L), 1)
+    zero = jnp.zeros((C, L), BF16)
     for a, to in ((0, R - 1), (2, 0)):
-        c_hi[pl.ds(a * C, C), pl.ds(to * L, L)] = zero.astype(BF16)
-        c_lo[pl.ds(a * C, C), pl.ds(to * L, L)] = zero.astype(BF16)
-    inner[...] = three_products(c_hi, c_lo, s_hi, s_lo)
+        c_hi[pl.ds(a * C, C), pl.ds(to * L, L)] = zero
+        c_lo[pl.ds(a * C, C), pl.ds(to * L, L)] = zero
+    totals = []
+    for k in range(PIECES):
+        copies[k, 0].wait()
+        for r in range(R):
+            at = pl.ds(r * L, L)
+            value = x_here[pl.ds(k * step * R + r, step, stride=R), :]
+            before = jnp.where(lane == 0, 0.0, roll(value, 1))
+            after = jnp.where(lane == L - 1, 0.0, roll(value, -1))
+            for b, shifted in enumerate((before, value, after)):
+                high, low = split(shifted)
+                s_both[pl.ds(b * C + k * step, step), at] = high
+                s_both[pl.ds((3 + b) * C + k * step, step), at] = low
+        copies[k, 1].wait()
+        total = jnp.zeros((step, L), F32)
+        for r in range(R):
+            value = g_here[pl.ds(k * step * R + r, step, stride=R), :]
+            total = total + value
+            high, low = split(value)
+            for a in range(3):
+                to = r + a - 1
+                if 0 <= to < R:
+                    c_hi[pl.ds(a * C + k * step, step), pl.ds(to * L, L)] = high
+                    c_lo[pl.ds(a * C + k * step, step), pl.ds(to * L, L)] = low
+        totals.append(total)
+    both = nt(c_hi, s_both)
+    inner[...] = wide_form(both[:, : 3 * C] + both[:, 3 * C :] + nt(c_lo, s_both.at[pl.ds(0, 3 * C), :]))
     bias[...] = jnp.zeros((8, L), F32)
     bias[:, pl.ds(0, C)] = lax.dot_general(
-        jnp.ones((8, L), F32), total, NT, preferred_element_type=F32, precision=lax.Precision.HIGHEST
+        jnp.ones((8, L), F32),
+        jnp.concatenate(totals, axis=0),
+        NT,
+        preferred_element_type=F32,
+        precision=lax.Precision.HIGHEST,
     )
 
 
@@ -246,32 +263,22 @@
         (g_beyond, roll(g_beyond, 1), roll(g_beyond, 2)),
         (jnp.where(lane < R + 2, column, 0.0), zero, zero),
     )
-    wide = inner[...] + three_products(c_hi, c_lo, s_hi, s_lo)
-    height = chunks.rows + chunks.CORNERS
+    wide = inner[...] + wide_form(nt(c_hi, s_hi) + nt(c_hi, s_lo) + nt(c_lo, s_hi))
     for tile in range(chunks.tiles):
         i, j = divmod(tile, 7)
-        at = 8 * i
-        for chunk, place, count in chunks.pieces(8 * tile, 8):
-            packed[pl.ds(chunk * height + place, count), :] = wide[at : at + count, L * j : L * j + L]
-            at += count
-    at = 0
-    for chunk, place, count in chunks.pieces(8 * chunks.tiles, 8):
-        packed[pl.ds(chunk * height + place, count), :] = bias[pl.ds(at, count), :]
-        at += count
-    for chunk, place, count in chunks.pieces(
-        8 * chunks.tiles + 8, chunks.n * chunks.rows - 8 * chunks.tiles - 8
-    ):
-        packed[pl.ds(chunk * height + place, count), :] = jnp.zeros((count, L), F32)
-
-    cells = zero
-    for k, at in enumerate((0, HALF, R - 1, HALF + R - 1)):
-        cells = jnp.where(lane == k, roll(beyond, k - at), cells)
-    cells = jnp.concatenate([cells, jnp.zeros((L - C, L), F32)], axis=0).T
-    to_north, to_south = lat_neighbours()
-    for chunk in range(chunks.n):
-        value = jnp.where(to_north == chunk, cells[0:2], 0.0)
-        value = jnp.where(to_south == chunk, cells[2:4], value)
-        packed[pl.ds(chunk * height + chunks.rows, chunks.CORNERS), :] = value
+        packed[pl.ds(8 * tile, 8), :] = wide[8 * i : 8 * i + 8, L * j : L * j + L]
+    at = 8 * chunks.tiles
+    packed[pl.ds(at, 8), :] = bias[...]
+    rest = packed.shape[0] - at - 8
+    packed[pl.ds(at + 8, rest), :] = jnp.zeros((rest, L), F32)
+
+
+def sum_kernel(parts, result):
+    total = parts[0]
+    for k in range(1, parts.shape[0]):
+        total = total + parts[k]
+    for k in range(result.shape[0]):
+        result[k] = total
 
 
 def unpack_kernel(tiles, factor, gathered, weight_grad, bias_grad):
@@ -284,31 +291,19 @@
 
 
 def conv_kernel(
-    is_grad, field, west, east, row_1, row_2, weight, bias, parts, result, token, hi, lo, ends, sems
+    is_grad, field, west, east, corners, row_1, row_2, weight, bias, result, token, hi, lo
 ):
     part = 1 if is_grad else 0
-    copies = [
-        pltpu.make_async_copy(
-            parts.at[at, :, pl.ds(parts.shape[2] - 2 * L, 2 * L)], ends.at[k], sems.at[k]
-        )
-        for k, at in enumerate(lat_neighbours())
-    ]
-    for copy in copies:
-        copy.start()
     odd = odd_lat()
     north = pick(odd, row_1[part], row_2[part])
     south = pick(odd, row_2[part], row_1[part])
-    for copy in copies:
-        copy.wait()
-    corners = [ends[k][:, at : at + L] for k in range(2) for at in (0, L)]
-    corners = jnp.concatenate(corners + [jnp.zeros((L - 4, L), F32)], axis=0).T[:C]
     first = HALF * part
 
     def shifts(r):
         if r < 0:
-            return taps(north, west[...], first + r + 1, corners, part)
+            return taps(north, west[...], first + r + 1, corners[...], first)
         if r >= R:
-            return taps(south, west[...], first + r + 1, corners, 2 + part)
+            return taps(south, west[...], first + r + 1, corners[...], first + 1)
         return taps(row(field, r), west[...], first + r + 1, east[...], first + r)
 
     def put(block, half, values):
@@ -365,10 +360,9 @@
         functools.partial(conv_kernel, is_grad),
         [out(C * R, L), out(8, L)],
         args,
-        [scratch, scratch, pltpu.VMEM((2, 1, 2 * L), F32), pltpu.SemaphoreType.DMA((2,))],
+        [scratch, scratch],
         after,
-        specs=[VMEM] * (len(args) - 1) + [ANY],
-        flops=6 * 9 * C * C * R * L,
+        flops=4 * 6 * 9 * C * C * R * L,
         moved=3 * 4 * C * R * L,
     )
 
@@ -399,13 +393,12 @@
 
     block = 4 * C * R * L
     product = 6 * 9 * C * C * R * L
-    own_1, own_2, own_west, own_east = call(
+    own_1, own_2, own_west, own_east, done = call(
         front_kernel,
-        [out(2, C, L)] * 2 + [out(C, L)] * 2,
-        (x, g),
+        [kept(2, C, L)] * 2 + [kept(C, L)] * 2 + [kept(8, L)],
+        (in_hbm(x), in_hbm(g)),
         [pltpu.VMEM((C * R, L), F32)] * 2 + [pltpu.SemaphoreType.DMA((PIECES, 2))],
         specs=[ANY] * 2,
-        grant=GRANT,
         flops=block,
         moved=2 * block,
     )
@@ -415,9 +408,12 @@
     inner_sum, bias_sum = call(
         inner_weight_kernel,
         [out(C, 7 * L), out(8, L)],
-        (x, g),
-        [pltpu.VMEM((3 * C, R * L), BF16)] * 4,
-        after=(own_west,),
+        (in_hbm(x), in_hbm(g)),
+        [pltpu.VMEM((C * R, L), F32)] * 2
+        + [pltpu.SemaphoreType.DMA((PIECES, 2)), pltpu.VMEM((6 * C, R * L), BF16)]
+        + [pltpu.VMEM((3 * C, R * L), BF16)] * 2,
+        after=(done,),
+        specs=[ANY] * 2,
         flops=product,
         moved=2 * block,
     )
@@ -425,30 +421,37 @@
     n_far = lax.axis_size(FAR)
     n_near = nlat * nlon // n_far
     chunks = Chunks(n_near)
-    height = chunks.rows + chunks.CORNERS
     packed = call(
         functools.partial(outer_weight_kernel, chunks),
-        [out(n_near * height, L)],
+        [kept(n_near * chunks.rows, L)],
         (inner_sum, bias_sum, own_east, own_1, own_2, east, row_1, row_2),
         [pltpu.VMEM((3 * C, 4 * L), BF16)] * 4,
         flops=product // 4,
         moved=block,
     )[0]
-    parts = lax.all_to_all(packed.reshape(n_near, 1, height * L), NEAR, 0, 0)
-    column = call(column_kernel, [out(C, L)], (own_east, row_1, row_2), after=(packed,))[0]
+    parts = lax.all_to_all(packed.reshape(n_near, 1, chunks.rows * L), NEAR, 0, 0)
+    column, ends = call(
+        columns_kernel, [kept(C, L)] * 2, (own_east, row_1, row_2), after=(packed,)
+    )
     west = send(column, to_east)
-    parts, west = lax.optimization_barrier((parts, west))
-    mine = jnp.sum(parts[:, :, : chunks.rows * L], axis=0, keepdims=True)
-    others = lax.all_to_all(jnp.broadcast_to(mine, (n_far, 1, chunks.rows * L)), FAR, 0, 0)
+    corners = send(ends, to_west)
+    mine = call(
+        sum_kernel,
+        [kept(n_far, 1, chunks.rows * L)],
+        (parts,),
+        after=(column, ends),
+        moved=block // 2,
+    )[0]
+    others = lax.all_to_all(mine, FAR, 0, 0)
     flipped = weight.reshape(C, 3, 3, C)[:, ::-1, ::-1].transpose(3, 1, 2, 0).reshape(C, 9 * C)
-    halo = (west, east, row_1, row_2)
+    halo = (west, east, corners, row_1, row_2)
     bias = bias.reshape(C, 1)
-    output, token = conv(False, x, *halo, weight, bias, parts)
-    others, token = lax.optimization_barrier((others, token))
-    mine = jnp.sum(others, axis=0, keepdims=True)
-    mine = jnp.broadcast_to(mine, (n_near, 1, chunks.rows * L))
+    output, token = conv(False, x, *halo, weight, bias)
+    mine = call(
+        sum_kernel, [kept(n_near, 1, chunks.rows * L)], (others,), after=(token,), moved=block // 2
+    )[0]
     gathered = lax.all_to_all(mine, NEAR, 0, 0)
-    grad, _ = conv(True, g, *halo, flipped, bias, parts, after=(mine,))
+    grad, _ = conv(True, g, *halo, flipped, bias, after=(mine,))
     weight_grad, bias_grad = call(
         functools.partial(unpack_kernel, chunks.tiles, factor),
         [out(C, 9 * C), out(1, C)],

time: 87 us -> 83.2 us (0.956)
  blocking collectives: 17.5 us -> 0 us
  waiting for transfers between devices: 10.8 us -> 20.3 us
  starting transfers between devices: 36.3 us -> 43.7 us
  local copies, waits for them, and re-layouts: 6.17 us -> 1.47 us
  Pallas kernels: 14.6 us -> 16.4 us
    all_to_all x1 -> x0, blocking collectives: 17.5 us -> none  [shards(): lax.all_to_all(jnp.broadcast_to(mine, (n_far, 1, chunks.rows * L)), FAR,...]
    all_to_all x1 -> x2, waiting for transfers between devices: 6 us -> 14 us  [the longest x1 9.21 us: shards(): others = lax.all_to_all(mine, FAR, 0, 0)]
    all_to_all x1 -> x2, starting transfers between devices: 13.7 us -> 19.9 us  [the longest x1 13.9 us: shards(): lax.all_to_all(packed.reshape(n_near, 1, chunks.rows * L), NEAR, 0, 0)]
    unnamed x21 -> x9, local copies, waits for them, and re-layouts: 4.67 us -> 0.95 us
    all_to_all x1, waiting for transfers between devices: 2.55 us -> 6.2 us  [shards(): gathered = lax.all_to_all(mine, NEAR, 0, 0)]
    ppermute x4 -> x5, waiting for transfers between devices: 2.21 us -> 0.01 us  [send(): return lax.ppermute(value, AXES, pairs)]
    ppermute x4 -> x5, starting transfers between devices: 16.2 us -> 18.2 us  [send(): return lax.ppermute(value, AXES, pairs)]
    pallas_call x7 -> x9, Pallas kernels: 14.6 us -> 16.4 us  [call(): pl.pallas_call(body, out_shape=outs, in_specs=(specs or [VMEM] * len(args...]
  transfers between devices with their start and end apart: 6 -> 8, of which waited for: 3 -> 3; matrix products, arithmetic and copies ran while one was open for 1% -> 1% of each run, Pallas kernels for 11% -> 13%
where the time goes in v3:
time: 83.2 us; the launch traced here: 82.6 us
  starting transfers between devices  43.7 us (53%)
  waiting for transfers between devices  20.3 us (24%)
  Pallas kernels  16.4 us (20%)
  local copies, waits for them, and re-layouts  1.47 us (2%)
    ppermute x5, starting transfers between devices, send(): return lax.ppermute(value, AXES, pairs)  18.2 us
    pallas_call x9, Pallas kernels, call(): pl.pallas_call(body, out_shape=outs, in_specs=(specs or [VMEM] * len(args...  16.4 us
    all_to_all x1, starting transfers between devices, shards(): lax.all_to_all(packed.reshape(n_near, 1, chunks.rows * L), NEAR, 0, 0)  13.9 us
    all_to_all x1, waiting for transfers between devices, shards(): others = lax.all_to_all(mine, FAR, 0, 0)  9.21 us
    all_to_all x1, waiting for transfers between devices, shards(): gathered = lax.all_to_all(mine, NEAR, 0, 0)  6.2 us
    all_to_all x1, starting transfers between devices, shards(): others = lax.all_to_all(mine, FAR, 0, 0)  5.99 us
    all_to_all x1, starting transfers between devices, shards(): gathered = lax.all_to_all(mine, NEAR, 0, 0)  5.6 us
    all_to_all x1, waiting for transfers between devices, shards(): lax.all_to_all(packed.reshape(n_near, 1, chunks.rows * L), NEAR, 0, 0)  4.83 us
  transfers between devices with their start and end apart: 8, of which 3 were waited for; matrix products, arithmetic and copies ran while one was open for 1% of the time, Pallas kernels for 13%

profile of v3, /device:TPU:1, one launch (start us, length us, event | category | flops | bytes accessed | tf_op | source)
XLA Modules:
  0.0 82.6 jit_solution(1125732239557975142)
XLA Ops:
  0.6 2.1 %shard_map.75 = (f32[2,96,128]{2,1,0:T(8,128)S(1)}, f32[2,96,128]{2,1,0:T(8,128)S(1)}, f32[96,128]{1,0:T(8,128)S(1)}, f32[96,128]{1,0:T(8,128)S(1)}, f32[8,128]{1,0:T(8,128)S(1)}) custom-call(f32[1536,128]{1,0:T(8,128)} %bitcast.13, f32[1536,128]{1,0:T(8,128)} %bitcast.16), custom_call_target="tpu_custom_call" | custom-call | flops 786432 | bytes 1572864 | tf_op jit(solution)/shard_map/pallas_call | solution.py:33
  2.7 4.0 %collective-permute-start = (f32[2,96,128]{2,1,0:T(8,128)S(1)}, f32[2,96,128]{2,1,0:T(8,128)S(1)}, u32[]{:S(2)}, u32[]{:S(2)}) collective-permute-start(f32[2,96,128]{2,1,0:T(8,128)S(1)} %get-tuple-element.19.refs_3_), channel_id=1, source_target_pairs={{0,64},{1,65},{2,66},{3,67},{4,68},{5,69},{6,70},{7,71},{8,72},{9,... | collective-permute-start | bytes 294920 | tf_op jit(solution)/shard_map/ppermute | solution.py:392
  6.8 4.7 %collective-permute-start.1 = (f32[2,96,128]{2,1,0:T(8,128)S(1)}, f32[2,96,128]{2,1,0:T(8,128)S(1)}, u32[]{:S(2)}, u32[]{:S(2)}) collective-permute-start(f32[2,96,128]{2,1,0:T(8,128)S(1)} %get-tuple-element.20.refs_4_), channel_id=1, source_target_pairs={{0,32},{1,33},{2,34},{3,35},{4,36},{5,37},{6,38},{7,39},{8,40},{9,... | collective-permute-start | bytes 294920 | tf_op jit(solution)/shard_map/ppermute | solution.py:392
  11.4 3.9 %collective-permute-start.2 = (f32[96,128]{1,0:T(8,128)S(1)}, f32[96,128]{1,0:T(8,128)S(1)}, u32[]{:S(2)}, u32[]{:S(2)}) collective-permute-start(f32[96,128]{1,0:T(8,128)S(1)} %get-tuple-element.24), channel_id=1, source_target_pairs={{0,63},{1,0},{2,1},{3,2},{4,3},{5,4},{6,5},{7,6},{8,7},{9,8},{10,9... | collective-permute-start | bytes 147464 | tf_op jit(solution)/shard_map/ppermute | solution.py:392
  15.4 4.0 %shard_map.76 = (f32[96,896]{1,0:T(8,128)S(1)}, f32[8,128]{1,0:T(8,128)S(1)}) custom-call(f32[1536,128]{1,0:T(8,128)} %bitcast.14, f32[1536,128]{1,0:T(8,128)} %bitcast.17, f32[8,128]{1,0:T(8,128)S(1)} %get-tuple-element.21.refs_2_), custom_call_target="tpu_custom_call" | custom-call | flops 1019215872 | bytes 1572864 | tf_op jit(solution)/shard_map/pallas_call | solution.py:33
  19.4 0.0 collective-permute-done.2.refs_5_.refs_2_
  19.4 0.0 collective-permute-done.refs_6_.refs_1_.refs_4_
  19.4 0.0 collective-permute-done.1.refs_7_.refs_2_.refs_5_
  19.4 1.7 %shard_map.77.refs_3_ = f32[704,128]{1,0:T(8,128)} custom-call(f32[96,896]{1,0:T(8,128)S(1)} %get-tuple-element.22.refs_0_, f32[8,128]{1,0:T(8,128)S(1)} %get-tuple-element.23.refs_1_, f32[96,128]{1,0:T(8,128)S(1)} %get-tuple-element.18.refs_2_.refs_0_, f32[2,96,128]{2,1,0:T(8,128)S(1)} %get-tuple-element.19.refs_3_, ...), custom_call_target="tpu_custom_call" | custom-call | flops 254803968 | bytes 786432 | tf_op jit(solution)/shard_map/pallas_call | solution.py:33
  21.1 0.0 copy-start.3
  21.1 13.9 %all-to-all-start = ((f32[64,1,1408]{2,1,0:T(1,128)}), f32[64,1,1408]{2,1,0:T(1,128)S(1)}, u32[]{:S(2)}, u32[]{:S(2)}) async-start(f32[64,1,1408]{2,1,0:T(1,128)} %bitcast.7), calls=%async_computation | async-start | bytes 720896 | tf_op jit(solution)/shard_map/all_to_all | solution.py:432
  35.0 0.0 copy-start
  35.0 0.2 shard_map.78
  35.2 0.0 copy-start.2
  35.2 3.7 %collective-permute-start.3 = (f32[96,128]{1,0:T(8,128)S(1)}, f32[96,128]{1,0:T(8,128)S(1)}, u32[]{:S(2)}, u32[]{:S(2)}) collective-permute-start(f32[96,128]{1,0:T(8,128)S(1)} %get-tuple-element.25.refs_1_), channel_id=1, source_target_pairs={{0,1},{1,2},{2,3},{3,4},{4,5},{5,6},{6,7},{7,8},{8,9},{9,10},{10,1... | collective-permute-start | bytes 147464 | tf_op jit(solution)/shard_map/ppermute | solution.py:392
  38.9 1.9 %collective-permute-start.4 = (f32[96,128]{1,0:T(8,128)S(1)}, f32[96,128]{1,0:T(8,128)S(1)}, u32[]{:S(2)}, u32[]{:S(2)}) collective-permute-start(f32[96,128]{1,0:T(8,128)S(1)} %get-tuple-element.26.refs_2_), channel_id=1, source_target_pairs={{0,63},{1,0},{2,1},{3,2},{4,3},{5,4},{6,5},{7,6},{8,7},{9,8},{10,9... | collective-permute-start | bytes 147464 | tf_op jit(solution)/shard_map/ppermute | solution.py:392
  40.8 0.0 copy-done.3
  40.8 0.1 copy.11.refs_7_
  40.9 4.8 %all-to-all-done.refs_0_ = f32[64,1,1408]{2,1,0:T(1,128)S(1)} async-done(((f32[64,1,1408]{2,1,0:T(1,128)}), f32[64,1,1408]{2,1,0:T(1,128)S(1)}, u32[]{:S(2)}, u32[]{:S(2)}) %all-to-all-start) | async-done | bytes 360480 | tf_op jit(solution)/shard_map/all_to_all | solution.py:432
  45.7 0.7 shard_map.80
  46.4 6.0 %all-to-all-start.1 = ((f32[8,1,1408]{2,1,0:T(1,128)}), f32[8,1,1408]{2,1,0:T(1,128)S(1)}, u32[]{:S(2)}, u32[]{:S(2)}) async-start(f32[8,1,1408]{2,1,0:T(1,128)} %shard_map.80), calls=%async_computation.1 | async-start | bytes 90112 | tf_op jit(solution)/shard_map/all_to_all | solution.py:445
  52.4 0.0 collective-permute-done.3.refs_1_
  52.4 0.0 collective-permute-done.4.refs_3_
  52.4 0.0 copy-done
  52.4 0.0 copy-done.2
  52.5 3.0 %shard_map.79 = (f32[1536,128]{1,0:T(8,128)}, f32[8,128]{1,0:T(8,128)S(1)}) custom-call(f32[1536,128]{1,0:T(8,128)S(1)} %bitcast.15, f32[96,128]{1,0:T(8,128)S(1)} %collective-permute-done.3.refs_1_, f32[96,128]{1,0:T(8,128)S(1)} %collective-permute-done.2.refs_5_.refs_2_, f32[96,128]{1,0:T(8,128)S(1)} %collective-permute-done.4.refs_3_, ...), custom_call_target="tpu_custom_call" | custom-call | flops 4076863488 | bytes 2359296 | tf_op jit(solution)/shard_map/pallas_call | solution.py:33
  55.4 9.2 %all-to-all-done.1.refs_0_ = f32[8,1,1408]{2,1,0:T(1,128)S(1)} async-done(((f32[8,1,1408]{2,1,0:T(1,128)}), f32[8,1,1408]{2,1,0:T(1,128)S(1)}, u32[]{:S(2)}, u32[]{:S(2)}) %all-to-all-start.1) | async-done | bytes 45088 | tf_op jit(solution)/shard_map/all_to_all | solution.py:445
  64.6 0.8 shard_map.81.refs_8_
  65.4 5.6 %all-to-all-start.2 = ((f32[64,1,1408]{2,1,0:T(1,128)}), f32[64,1,1408]{2,1,0:T(1,128)S(1)}, u32[]{:S(2)}, u32[]{:S(2)}) async-start(f32[64,1,1408]{2,1,0:T(1,128)} %shard_map.81.refs_8_), calls=%async_computation.2 | async-start | bytes 720896 | tf_op jit(solution)/shard_map/all_to_all | solution.py:453
  71.0 0.2 copy.12
  71.3 0.0 copy-start.1
  71.3 0.2 copy.13
  71.5 0.2 copy.14.refs_6_
  71.7 0.7 copy-done.1
  72.4 3.3 %shard_map.82 = (f32[1536,128]{1,0:T(8,128)}, f32[8,128]{1,0:T(8,128)}) custom-call(f32[1536,128]{1,0:T(8,128)S(1)} %bitcast.18, f32[96,128]{1,0:T(8,128)S(1)} %collective-permute-done.3.refs_1_, f32[96,128]{1,0:T(8,128)S(1)} %collective-permute-done.2.refs_5_.refs_2_, f32[96,128]{1,0:T(8,128)S(1)} %collective-permute-done.4.refs_3_, ...), custom_call_target="tpu_custom_call" | custom-call | flops 4076863488 | bytes 2359296 | tf_op jit(solution)/shard_map/pallas_call | solution.py:33
  75.7 6.2 %all-to-all-done.2 = f32[64,1,1408]{2,1,0:T(1,128)S(1)} async-done(((f32[64,1,1408]{2,1,0:T(1,128)}), f32[64,1,1408]{2,1,0:T(1,128)S(1)}, u32[]{:S(2)}, u32[]{:S(2)}) %all-to-all-start.2) | async-done | bytes 360480 | tf_op jit(solution)/shard_map/all_to_all | solution.py:453
  81.9 0.8 shard_map.83
  (1 shorter events, 0.0 us)
Async XLA Ops:
  2.7 16.6 %collective-permute-start = (f32[2,96,128]{2,1,0:T(8,128)S(1)}, f32[2,96,128]{2,1,0:T(8,128)S(1)}, u32[]{:S(2)}, u32[]{:S(2)}) collective-permute-start(f32[2,96,128]{2,1,0:T(8,128)S(1)} %get-tuple-element.19.refs_3_), channel_id=1, source_target_pairs={{0,64},{1,65},{2,66},{3,67},{4,68},{5,69},{6,70},{7,71},{8,72},{9,... | collective-permute-start | bytes 294920 | tf_op jit(solution)/shard_map/ppermute | solution.py:392
  6.8 12.6 %collective-permute-start.1 = (f32[2,96,128]{2,1,0:T(8,128)S(1)}, f32[2,96,128]{2,1,0:T(8,128)S(1)}, u32[]{:S(2)}, u32[]{:S(2)}) collective-permute-start(f32[2,96,128]{2,1,0:T(8,128)S(1)} %get-tuple-element.20.refs_4_), channel_id=1, source_target_pairs={{0,32},{1,33},{2,34},{3,35},{4,36},{5,37},{6,38},{7,39},{8,40},{9,... | collective-permute-start | bytes 294920 | tf_op jit(solution)/shard_map/ppermute | solution.py:392
  11.4 7.9 %collective-permute-start.2 = (f32[96,128]{1,0:T(8,128)S(1)}, f32[96,128]{1,0:T(8,128)S(1)}, u32[]{:S(2)}, u32[]{:S(2)}) collective-permute-start(f32[96,128]{1,0:T(8,128)S(1)} %get-tuple-element.24), channel_id=1, source_target_pairs={{0,63},{1,0},{2,1},{3,2},{4,3},{5,4},{6,5},{7,6},{8,7},{9,8},{10,9... | collective-permute-start | bytes 147464 | tf_op jit(solution)/shard_map/ppermute | solution.py:392
  21.1 19.7 %copy-start.3 = (f32[96]{0:T(128)S(1)}, f32[96]{0:T(128)}, u32[]{:S(2)}) copy-start(f32[96]{0:T(128)} %param.6) | copy-start | bytes 1156
  21.1 24.6 %all-to-all-start = ((f32[64,1,1408]{2,1,0:T(1,128)}), f32[64,1,1408]{2,1,0:T(1,128)S(1)}, u32[]{:S(2)}, u32[]{:S(2)}) async-start(f32[64,1,1408]{2,1,0:T(1,128)} %bitcast.7), calls=%async_computation | async-start | bytes 720896 | tf_op jit(solution)/shard_map/all_to_all | solution.py:432
  35.0 17.5 %copy-start = (f32[96,16,128]{2,1,0:T(8,128)S(1)}, f32[96,16,128]{2,1,0:T(8,128)}, u32[]{:S(2)}) copy-start(f32[96,16,128]{2,1,0:T(8,128)} %param.4) | copy-start | bytes 2359300
  35.2 17.3 %copy-start.2 = (f32[96,864]{1,0:T(8,128)S(1)}, f32[96,864]{1,0:T(8,128)}, u32[]{:S(2)}) copy-start(f32[96,864]{1,0:T(8,128)} %refs_6_.1) | copy-start | bytes 995332
  35.2 17.2 %collective-permute-start.3 = (f32[96,128]{1,0:T(8,128)S(1)}, f32[96,128]{1,0:T(8,128)S(1)}, u32[]{:S(2)}, u32[]{:S(2)}) collective-permute-start(f32[96,128]{1,0:T(8,128)S(1)} %get-tuple-element.25.refs_1_), channel_id=1, source_target_pairs={{0,1},{1,2},{2,3},{3,4},{4,5},{5,6},{6,7},{7,8},{8,9},{9,10},{10,1... | collective-permute-start | bytes 147464 | tf_op jit(solution)/shard_map/ppermute | solution.py:392
  38.9 13.6 %collective-permute-start.4 = (f32[96,128]{1,0:T(8,128)S(1)}, f32[96,128]{1,0:T(8,128)S(1)}, u32[]{:S(2)}, u32[]{:S(2)}) collective-permute-start(f32[96,128]{1,0:T(8,128)S(1)} %get-tuple-element.26.refs_2_), channel_id=1, source_target_pairs={{0,63},{1,0},{2,1},{3,2},{4,3},{5,4},{6,5},{7,6},{8,7},{9,8},{10,9... | collective-permute-start | bytes 147464 | tf_op jit(solution)/shard_map/ppermute | solution.py:392
  46.4 18.2 %all-to-all-start.1 = ((f32[8,1,1408]{2,1,0:T(1,128)}), f32[8,1,1408]{2,1,0:T(1,128)S(1)}, u32[]{:S(2)}, u32[]{:S(2)}) async-start(f32[8,1,1408]{2,1,0:T(1,128)} %shard_map.80), calls=%async_computation.1 | async-start | bytes 90112 | tf_op jit(solution)/shard_map/all_to_all | solution.py:445
  65.4 16.5 %all-to-all-start.2 = ((f32[64,1,1408]{2,1,0:T(1,128)}), f32[64,1,1408]{2,1,0:T(1,128)S(1)}, u32[]{:S(2)}, u32[]{:S(2)}) async-start(f32[64,1,1408]{2,1,0:T(1,128)} %shard_map.81.refs_8_), calls=%async_computation.2 | async-start | bytes 720896 | tf_op jit(solution)/shard_map/all_to_all | solution.py:453
  71.3 1.1 %copy-start.1 = (f32[96,16,128]{2,1,0:T(8,128)S(1)}, f32[96,16,128]{2,1,0:T(8,128)}, u32[]{:S(2)}) copy-start(f32[96,16,128]{2,1,0:T(8,128)} %param.7) | copy-start | bytes 2359300

commit v4 on v2

--- a/solution.py
+++ b/solution.py
@@ -24,9 +24,6 @@
 
 VMEM = pl.BlockSpec(memory_space=pltpu.VMEM)
 ANY = pl.BlockSpec(memory_space=pl.ANY)
-
-
-GRANT = (64 << 20) - 600 * 1024
 
 
 def call(kernel, outs, args, scratch=(), after=(), specs=None, grant=40 << 20, flops=0, moved=0):
@@ -48,6 +45,14 @@
     return jax.ShapeDtypeStruct(shape, F32)
 
 
+def kept(*shape):
+    return pltpu.VMEM(shape, F32)
+
+
+def in_hbm(value):
+    return pltpu.with_memory_space_constraint(value, pltpu.HBM)
+
+
 def roll(value, by):
     by = by % L
     return value if by == 0 else pltpu.roll(value, by, 1)
@@ -92,23 +97,27 @@
     return place_of(lat - 1), place_of(lat + 1)
 
 
+TILES = 7 * C // 8
+
+
 class Chunks:
-    CORNERS = 2
-
     def __init__(self, n):
         self.n = n
-        self.tiles = 7 * C // 8
-        self.rows = 4 * -(-(8 * self.tiles + 1) // (4 * n))
-
-    def pieces(self, first, count):
-        end = first + count
-        while first < end:
-            now = min(self.rows - first % self.rows, end - first)
-            yield first // self.rows, first % self.rows, now
-            first += now
-
-
-PIECES = 4
+        self.full = 8 * TILES // n
+        self.rows = self.full + 1
+        self.sent = self.full + 2
+        self.halves = 8 * TILES - self.full * n
+        assert self.halves in (0, n // 2) and self.full * n % 8 == 0
+
+    def pieces(self, tile):
+        at, end = 8 * tile, 8 * tile + 8
+        while at < end:
+            now = min(self.full - at % self.full, end - at)
+            yield at // self.full, at % self.full, now
+            at += now
+
+
+PIECES = 3
 
 
 def front_kernel(x, g, own_1, own_2, west, east, x_here, g_here, sems):
@@ -168,10 +177,11 @@
     return lax.dot_general(left[...], right[...], NT, preferred_element_type=F32)
 
 
-def three_products(c_hi, c_lo, s_hi, s_lo):
-    grad = nt(c_hi, s_hi) + nt(c_hi, s_lo) + nt(c_lo, s_hi)
+def wide_form(grad, bias):
     return jnp.concatenate(
-        [grad[a * C : (a + 1) * C] for a in range(3)] + [jnp.zeros((C, 7 * L - 9 * C), F32)], axis=1
+        [grad[a * C : (a + 1) * C] for a in range(3)]
+        + [bias, jnp.zeros((C, 7 * L - 9 * C - bias.shape[1]), F32)],
+        axis=1,
     )
 
 
@@ -182,32 +192,31 @@
     return before, value, after
 
 
-def inner_weight_kernel(x, g, inner, bias, s_hi, s_lo, c_hi, c_lo):
+def inner_weight_kernel(x, g, inner, s_both, c_hi, c_lo):
     zero = jnp.zeros((C, L), F32)
     total = zero
+    for a, to in ((0, R - 1), (2, 0)):
+        c_hi[pl.ds(a * C, C), pl.ds(to * L, L)] = zero.astype(BF16)
+        c_lo[pl.ds(a * C, C), pl.ds(to * L, L)] = zero.astype(BF16)
     for r in range(R):
         at = pl.ds(r * L, L)
-        for b, value in enumerate(inner_taps(row(x, r))):
-            s_hi[pl.ds(b * C, C), at], s_lo[pl.ds(b * C, C), at] = split(value)
-        here_hi, here_lo = split(row(g, r))
-        total = total + row(g, r)
+        for b, shifted in enumerate(inner_taps(row(x, r))):
+            s_both[pl.ds(b * C, C), at], s_both[pl.ds((3 + b) * C, C), at] = split(shifted)
+        value = row(g, r)
+        total = total + value
+        high, low = split(value)
         for a in range(3):
             to = r + a - 1
             if 0 <= to < R:
-                c_hi[pl.ds(a * C, C), pl.ds(to * L, L)] = here_hi
-                c_lo[pl.ds(a * C, C), pl.ds(to * L, L)] = here_lo
-    for a, to in ((0, R - 1), (2, 0)):
-        c_hi[pl.ds(a * C, C), pl.ds(to * L, L)] = zero.astype(BF16)
-        c_lo[pl.ds(a * C, C), pl.ds(to * L, L)] = zero.astype(BF16)
-    inner[...] = three_products(c_hi, c_lo, s_hi, s_lo)
-    bias[...] = jnp.zeros((8, L), F32)
-    bias[:, pl.ds(0, C)] = lax.dot_general(
-        jnp.ones((8, L), F32), total, NT, preferred_element_type=F32, precision=lax.Precision.HIGHEST
-    )
+                c_hi[pl.ds(a * C, C), pl.ds(to * L, L)] = high
+                c_lo[pl.ds(a * C, C), pl.ds(to * L, L)] = low
+    both = nt(c_hi, s_both)
+    grad = both[:, : 3 * C] + both[:, 3 * C :] + nt(c_lo, s_both.at[pl.ds(0, 3 * C), :])
+    inner[...] = wide_form(grad, jnp.sum(total, axis=1, keepdims=True))
 
 
 def outer_weight_kernel(
-    chunks, inner, bias, own_east, own_1, own_2, east, row_1, row_2, packed, s_hi, s_lo, c_hi, c_lo
+    chunks, inner, own_east, own_1, own_2, east, row_1, row_2, packed, s_hi, s_lo, c_hi, c_lo
 ):
     lane = lanes()
     zero = jnp.zeros((C, L), F32)
@@ -246,41 +255,80 @@
         (g_beyond, roll(g_beyond, 1), roll(g_beyond, 2)),
         (jnp.where(lane < R + 2, column, 0.0), zero, zero),
     )
-    wide = inner[...] + three_products(c_hi, c_lo, s_hi, s_lo)
-    height = chunks.rows + chunks.CORNERS
-    for tile in range(chunks.tiles):
-        i, j = divmod(tile, 7)
-        at = 8 * i
-        for chunk, place, count in chunks.pieces(8 * tile, 8):
-            packed[pl.ds(chunk * height + place, count), :] = wide[at : at + count, L * j : L * j + L]
-            at += count
-    at = 0
-    for chunk, place, count in chunks.pieces(8 * chunks.tiles, 8):
-        packed[pl.ds(chunk * height + place, count), :] = bias[pl.ds(at, count), :]
-        at += count
-    for chunk, place, count in chunks.pieces(
-        8 * chunks.tiles + 8, chunks.n * chunks.rows - 8 * chunks.tiles - 8
-    ):
-        packed[pl.ds(chunk * height + place, count), :] = jnp.zeros((count, L), F32)
-
+    grad = nt(c_hi, s_hi) + nt(c_hi, s_lo) + nt(c_lo, s_hi)
+    wide = inner[...] + wide_form(grad, jnp.zeros((C, 1), F32))
     cells = zero
     for k, at in enumerate((0, HALF, R - 1, HALF + R - 1)):
         cells = jnp.where(lane == k, roll(beyond, k - at), cells)
     cells = jnp.concatenate([cells, jnp.zeros((L - C, L), F32)], axis=0).T
+    x_cells = roll(cells[0:8], HALF)
+    g_cells = roll(cells[0:8], L // 4)
+    lane = lax.broadcasted_iota(jnp.int32, (1, L), 1)
+    corners = []
+    for k in (0, 2):
+        moved = x_cells[k : k + 1]
+        corners.append((moved, jnp.where(lane < L // 4, moved, g_cells[k + 1 : k + 2])))
     to_north, to_south = lat_neighbours()
+    left = chunks.full * chunks.n // 8
+    for tile in range(TILES):
+        i, j = divmod(tile, 7)
+        value = wide[8 * i : 8 * i + 8, L * j : L * j + L]
+        if tile < left:
+            at = 0
+            for chunk, place, count in chunks.pieces(tile):
+                packed[pl.ds(chunk * chunks.sent + place, count), :] = value[at : at + count]
+                at += count
+        else:
+            for k, half in enumerate((value, roll(value, HALF))):
+                for r in range(8):
+                    chunk = 2 * (8 * (tile - left) + r) + k
+                    packed[pl.ds(chunk * chunks.sent + chunks.full, 1), :] = half[r : r + 1]
     for chunk in range(chunks.n):
-        value = jnp.where(to_north == chunk, cells[0:2], 0.0)
-        value = jnp.where(to_south == chunk, cells[2:4], value)
-        packed[pl.ds(chunk * height + chunks.rows, chunks.CORNERS), :] = value
-
-
-def unpack_kernel(tiles, factor, gathered, weight_grad, bias_grad):
-    for tile in range(tiles):
+        at = chunk * chunks.sent + chunks.full
+        first = jnp.where(to_north == chunk, corners[0][0], jnp.where(to_south == chunk, corners[1][0], 0.0))
+        if chunks.halves:
+            first = jnp.where(lane < HALF, packed[pl.ds(at, 1), :], first)
+        packed[pl.ds(at, 1), :] = first
+        packed[pl.ds(at + 1, 1), :] = jnp.where(
+            to_north == chunk, corners[0][1], jnp.where(to_south == chunk, corners[1][1], 0.0)
+        )
+
+
+def sum_kernel(rows, height, parts, result):
+    total = parts[pl.ds(0, rows), :]
+    for k in range(1, parts.shape[0] // height):
+        total = total + parts[pl.ds(k * height, rows), :]
+    for k in range(result.shape[0] // rows):
+        result[pl.ds(k * rows, rows), :] = total
+
+
+def unpack_kernel(chunks, factor, gathered, weight_grad, bias_grad):
+    lane = lax.broadcasted_iota(jnp.int32, (8, L), 1)
+    left = chunks.full * chunks.n // 8
+    ends = []
+    for tile in range(TILES):
         i, j = divmod(tile, 7)
+        if tile < left:
+            value = jnp.concatenate(
+                [
+                    gathered[pl.ds(chunk * chunks.rows + place, count), :]
+                    for chunk, place, count in chunks.pieces(tile)
+                ],
+                axis=0,
+            )
+        else:
+            at = 16 * (tile - left) * chunks.rows + chunks.full
+            even, odd = (
+                gathered[pl.ds(at + k * chunks.rows, 8, stride=2 * chunks.rows), :] for k in range(2)
+            )
+            value = jnp.where(lane < HALF, even, roll(odd, HALF))
         width = min(L, 9 * C - L * j)
-        value = gathered[pl.ds(8 * tile, 8), :] * factor
-        weight_grad[pl.ds(8 * i, 8), pl.ds(L * j, width)] = value[:, :width]
-    bias_grad[...] = gathered[pl.ds(8 * tiles, 1), :][:, :C] * factor
+        weight_grad[pl.ds(8 * i, 8), pl.ds(L * j, width)] = value[:, :width] * factor
+        if width < L:
+            ends.append(value)
+    ends = jnp.concatenate(ends + [jnp.zeros((L - C, L), F32)], axis=0).T
+    at = 9 * C % L
+    bias_grad[...] = ends[at : at + 1, :C] * factor
 
 
 def conv_kernel(
@@ -300,15 +348,22 @@
     south = pick(odd, row_2[part], row_1[part])
     for copy in copies:
         copy.wait()
-    corners = [ends[k][:, at : at + L] for k in range(2) for at in (0, L)]
-    corners = jnp.concatenate(corners + [jnp.zeros((L - 4, L), F32)], axis=0).T[:C]
+    lane = lax.broadcasted_iota(jnp.int32, (1, L), 1)
+    corners = []
+    for k in range(2):
+        former, latter = ends[k][:, :L], ends[k][:, L:]
+        if is_grad:
+            corners.append(roll(latter, -(L // 4)))
+        else:
+            corners.append(jnp.where(lane < HALF, roll(former, HALF), roll(latter, HALF)))
+    corners = jnp.concatenate(corners + [jnp.zeros((L - 2, L), F32)], axis=0).T[:C]
     first = HALF * part
 
     def shifts(r):
         if r < 0:
-            return taps(north, west[...], first + r + 1, corners, part)
+            return taps(north, west[...], first + r + 1, corners, 0)
         if r >= R:
-            return taps(south, west[...], first + r + 1, corners, 2 + part)
+            return taps(south, west[...], first + r + 1, corners, 1)
         return taps(row(field, r), west[...], first + r + 1, east[...], first + r)
 
     def put(block, half, values):
@@ -368,7 +423,7 @@
         [scratch, scratch, pltpu.VMEM((2, 1, 2 * L), F32), pltpu.SemaphoreType.DMA((2,))],
         after,
         specs=[VMEM] * (len(args) - 1) + [ANY],
-        flops=6 * 9 * C * C * R * L,
+        flops=4 * 6 * 9 * C * C * R * L,
         moved=3 * 4 * C * R * L,
     )
 
@@ -399,58 +454,64 @@
 
     block = 4 * C * R * L
     product = 6 * 9 * C * C * R * L
-    own_1, own_2, own_west, own_east = call(
+    own_1, own_2, own_west, own_east, x, g = call(
         front_kernel,
-        [out(2, C, L)] * 2 + [out(C, L)] * 2,
-        (x, g),
-        [pltpu.VMEM((C * R, L), F32)] * 2 + [pltpu.SemaphoreType.DMA((PIECES, 2))],
+        [kept(2, C, L)] * 2 + [kept(C, L)] * 2 + [kept(C * R, L)] * 2,
+        (in_hbm(x), in_hbm(g)),
+        [pltpu.SemaphoreType.DMA((PIECES, 2))],
         specs=[ANY] * 2,
-        grant=GRANT,
         flops=block,
         moved=2 * block,
     )
     row_2 = send(own_2, second)
     row_1 = send(own_1, first)
     east = send(own_west, to_west)
-    inner_sum, bias_sum = call(
+    inner = call(
         inner_weight_kernel,
-        [out(C, 7 * L), out(8, L)],
+        [out(C, 7 * L)],
         (x, g),
-        [pltpu.VMEM((3 * C, R * L), BF16)] * 4,
-        after=(own_west,),
+        [pltpu.VMEM((6 * C, R * L), BF16)] + [pltpu.VMEM((3 * C, R * L), BF16)] * 2,
         flops=product,
         moved=2 * block,
-    )
+    )[0]
 
     n_far = lax.axis_size(FAR)
     n_near = nlat * nlon // n_far
     chunks = Chunks(n_near)
-    height = chunks.rows + chunks.CORNERS
     packed = call(
         functools.partial(outer_weight_kernel, chunks),
-        [out(n_near * height, L)],
-        (inner_sum, bias_sum, own_east, own_1, own_2, east, row_1, row_2),
+        [out(n_near * chunks.sent, L)],
+        (inner, own_east, own_1, own_2, east, row_1, row_2),
         [pltpu.VMEM((3 * C, 4 * L), BF16)] * 4,
         flops=product // 4,
         moved=block,
     )[0]
-    parts = lax.all_to_all(packed.reshape(n_near, 1, height * L), NEAR, 0, 0)
-    column = call(column_kernel, [out(C, L)], (own_east, row_1, row_2), after=(packed,))[0]
+    parts = lax.all_to_all(packed.reshape(n_near, 1, chunks.sent * L), NEAR, 0, 0)
+    column = call(column_kernel, [kept(C, L)], (own_east, row_1, row_2), after=(packed,))[0]
     west = send(column, to_east)
-    parts, west = lax.optimization_barrier((parts, west))
-    mine = jnp.sum(parts[:, :, : chunks.rows * L], axis=0, keepdims=True)
-    others = lax.all_to_all(jnp.broadcast_to(mine, (n_far, 1, chunks.rows * L)), FAR, 0, 0)
+    mine = call(
+        functools.partial(sum_kernel, chunks.rows, chunks.sent),
+        [out(n_far * chunks.rows, L)],
+        (parts.reshape(n_near * chunks.sent, L),),
+        after=(column,),
+        moved=block // 2,
+    )[0]
+    others = lax.all_to_all(mine.reshape(n_far, 1, chunks.rows * L), FAR, 0, 0)
     flipped = weight.reshape(C, 3, 3, C)[:, ::-1, ::-1].transpose(3, 1, 2, 0).reshape(C, 9 * C)
     halo = (west, east, row_1, row_2)
     bias = bias.reshape(C, 1)
     output, token = conv(False, x, *halo, weight, bias, parts)
-    others, token = lax.optimization_barrier((others, token))
-    mine = jnp.sum(others, axis=0, keepdims=True)
-    mine = jnp.broadcast_to(mine, (n_near, 1, chunks.rows * L))
-    gathered = lax.all_to_all(mine, NEAR, 0, 0)
+    mine = call(
+        functools.partial(sum_kernel, chunks.rows, chunks.rows),
+        [out(n_near * chunks.rows, L)],
+        (others.reshape(n_far * chunks.rows, L),),
+        after=(token,),
+        moved=block // 2,
+    )[0]
+    gathered = lax.all_to_all(mine.reshape(n_near, 1, chunks.rows * L), NEAR, 0, 0)
     grad, _ = conv(True, g, *halo, flipped, bias, parts, after=(mine,))
     weight_grad, bias_grad = call(
-        functools.partial(unpack_kernel, chunks.tiles, factor),
+        functools.partial(unpack_kernel, chunks, factor),
         [out(C, 9 * C), out(1, C)],
         (gathered.reshape(n_near * chunks.rows, L),),
         moved=block,

time: 87 us -> 82.5 us (0.948)
  blocking collectives: 17.5 us -> 0 us
  waiting for transfers between devices: 10.8 us -> 22.8 us
  starting transfers between devices: 36.3 us -> 42.4 us
  local copies, waits for them, and re-layouts: 6.17 us -> 0.72 us
    all_to_all x1 -> x0, blocking collectives: 17.5 us -> none  [shards(): lax.all_to_all(jnp.broadcast_to(mine, (n_far, 1, chunks.rows * L)), FAR,...]
    all_to_all x2 -> x3, waiting for transfers between devices: 8.55 us -> 22.5 us  [the longest x1 8.73 us: shards(): others = lax.all_to_all(mine.reshape(n_far, 1, chunks.rows * L), FAR, 0, 0)]
    all_to_all x2 -> x3, starting transfers between devices: 20.1 us -> 26.1 us  [the longest x1 13.5 us: shards(): lax.all_to_all(packed.reshape(n_near, 1, chunks.sent * L), NEAR, 0, 0)]
    unnamed x21 -> x5, local copies, waits for them, and re-layouts: 4.67 us -> 0.2 us
    ppermute x4, waiting for transfers between devices: 2.21 us -> 0.24 us  [send(): return lax.ppermute(value, AXES, pairs)]
    broadcast_in_dim x2 -> x0, local copies, waits for them, and re-layouts: 0.98 us -> none  [the longest x1 0.96 us: shards(): mine = jnp.broadcast_to(mine, (n_near, 1, chunks.rows * L))]
    pallas_call x7 -> x9, Pallas kernels: 14.6 us -> 15.4 us  [call(): pl.pallas_call(body, out_shape=outs, in_specs=(specs or [VMEM] * len(args...]
  transfers between devices with their start and end apart: 6 -> 7, of which waited for: 3 -> 4; matrix products, arithmetic and copies ran while one was open for 1% -> 1% of each run, Pallas kernels for 11% -> 12%
where the time goes in v4:
time: 82.5 us; the launch traced here: 82.1 us
  starting transfers between devices  42.4 us (51%)
  waiting for transfers between devices  22.8 us (28%)
  Pallas kernels  15.4 us (19%)
    ppermute x4, starting transfers between devices, send(): return lax.ppermute(value, AXES, pairs)  16.3 us
    pallas_call x9, Pallas kernels, call(): pl.pallas_call(body, out_shape=outs, in_specs=(specs or [VMEM] * len(args...  15.4 us
    all_to_all x1, starting transfers between devices, shards(): lax.all_to_all(packed.reshape(n_near, 1, chunks.sent * L), NEAR, 0, 0)  13.5 us
    all_to_all x1, waiting for transfers between devices, shards(): others = lax.all_to_all(mine.reshape(n_far, 1, chunks.rows * L), FAR, 0, 0)  8.73 us
    all_to_all x1, waiting for transfers between devices, shards(): lax.all_to_all(packed.reshape(n_near, 1, chunks.sent * L), NEAR, 0, 0)  7.11 us
    all_to_all x1, waiting for transfers between devices, shards(): lax.all_to_all(mine.reshape(n_near, 1, chunks.rows * L), NEAR, 0, 0)  6.71 us
    all_to_all x1, starting transfers between devices, shards(): others = lax.all_to_all(mine.reshape(n_far, 1, chunks.rows * L), FAR, 0, 0)  6.38 us
    all_to_all x1, starting transfers between devices, shards(): lax.all_to_all(mine.reshape(n_near, 1, chunks.rows * L), NEAR, 0, 0)  6.14 us
  transfers between devices with their start and end apart: 7, of which 4 were waited for; matrix products, arithmetic and copies ran while one was open for 1% of the time, Pallas kernels for 12%

profile of v4, /device:TPU:1, one launch (start us, length us, event | category | flops | bytes accessed | tf_op | source)
XLA Modules:
  0.0 82.1 jit_solution(12732214041134774766)
XLA Ops:
  0.6 2.1 %shard_map.75 = (f32[2,96,128]{2,1,0:T(8,128)S(1)}, f32[2,96,128]{2,1,0:T(8,128)S(1)}, f32[96,128]{1,0:T(8,128)S(1)}, f32[96,128]{1,0:T(8,128)S(1)}, f32[1536,128]{1,0:T(8,128)S(1)}, /*index=5*/f32[1536,128]{1,0:T(8,128)S(1)}) custom-call(f32[1536,128]{1,0:T(8,128)} %bitcast.21, f32[1536,128]{1,0:T(8,128)} %bitcast.22), custom_call_target="tpu_custom_call" | custom-call | flops 786432 | bytes 1572864 | tf_op jit(solution)/shard_map/pallas_call | solution.py:33
  2.7 4.0 %collective-permute-start = (f32[2,96,128]{2,1,0:T(8,128)S(1)}, f32[2,96,128]{2,1,0:T(8,128)S(1)}, u32[]{:S(2)}, u32[]{:S(2)}) collective-permute-start(f32[2,96,128]{2,1,0:T(8,128)S(1)} %get-tuple-element.17.refs_2_), channel_id=1, source_target_pairs={{0,64},{1,65},{2,66},{3,67},{4,68},{5,69},{6,70},{7,71},{8,72},{9,... | collective-permute-start | bytes 294920 | tf_op jit(solution)/shard_map/ppermute | solution.py:453
  6.8 4.7 %collective-permute-start.1 = (f32[2,96,128]{2,1,0:T(8,128)S(1)}, f32[2,96,128]{2,1,0:T(8,128)S(1)}, u32[]{:S(2)}, u32[]{:S(2)}) collective-permute-start(f32[2,96,128]{2,1,0:T(8,128)S(1)} %get-tuple-element.18.refs_3_), channel_id=1, source_target_pairs={{0,32},{1,33},{2,34},{3,35},{4,36},{5,37},{6,38},{7,39},{8,40},{9,... | collective-permute-start | bytes 294920 | tf_op jit(solution)/shard_map/ppermute | solution.py:453
  11.4 3.9 %collective-permute-start.2 = (f32[96,128]{1,0:T(8,128)S(1)}, f32[96,128]{1,0:T(8,128)S(1)}, u32[]{:S(2)}, u32[]{:S(2)}) collective-permute-start(f32[96,128]{1,0:T(8,128)S(1)} %get-tuple-element.20), channel_id=1, source_target_pairs={{0,63},{1,0},{2,1},{3,2},{4,3},{5,4},{6,5},{7,6},{8,7},{9,8},{10,9... | collective-permute-start | bytes 147464 | tf_op jit(solution)/shard_map/ppermute | solution.py:453
  15.4 2.5 %shard_map.76.refs_0_ = f32[96,896]{1,0:T(8,128)S(1)} custom-call(f32[1536,128]{1,0:T(8,128)S(1)} %get-tuple-element.15.refs_0_, f32[1536,128]{1,0:T(8,128)S(1)} %get-tuple-element.19.refs_1_.refs_0_), custom_call_target="tpu_custom_call" | custom-call | flops 1019215872 | bytes 1572864 | tf_op jit(solution)/shard_map/pallas_call | solution.py:33
  17.9 0.2 collective-permute-done.2.refs_4_.refs_2_
  18.2 0.0 collective-permute-done.refs_5_.refs_1_.refs_3_
  18.2 0.0 collective-permute-done.1.refs_6_.refs_2_.refs_4_
  18.2 1.9 %shard_map.77.refs_3_ = f32[768,128]{1,0:T(8,128)} custom-call(f32[96,896]{1,0:T(8,128)S(1)} %shard_map.76.refs_0_, f32[96,128]{1,0:T(8,128)S(1)} %get-tuple-element.16.refs_1_.refs_0_, f32[2,96,128]{2,1,0:T(8,128)S(1)} %get-tuple-element.17.refs_2_, f32[2,96,128]{2,1,0:T(8,128)S(1)} %get-tuple-element.18.refs_3_, ...), custom_call_target="tpu_custom_call" | custom-call | flops 254803968 | bytes 786432 | tf_op jit(solution)/shard_map/pallas_call | solution.py:33
  20.1 13.5 %all-to-all-start = ((f32[64,1,1536]{2,1,0:T(1,128)}), f32[64,1,1536]{2,1,0:T(1,128)S(1)}, u32[]{:S(2)}, u32[]{:S(2)}) async-start(f32[64,1,1536]{2,1,0:T(1,128)} %bitcast.3), calls=%async_computation | async-start | bytes 786432 | tf_op jit(solution)/shard_map/all_to_all | solution.py:489
  33.6 0.0 copy-start.1
  33.6 0.1 shard_map.78.refs_1_
  33.8 0.0 copy-start
  33.8 3.7 %collective-permute-start.3 = (f32[96,128]{1,0:T(8,128)S(1)}, f32[96,128]{1,0:T(8,128)S(1)}, u32[]{:S(2)}, u32[]{:S(2)}) collective-permute-start(f32[96,128]{1,0:T(8,128)S(1)} %shard_map.78.refs_1_), channel_id=1, source_target_pairs={{0,1},{1,2},{2,3},{3,4},{4,5},{5,6},{6,7},{7,8},{8,9},{9,10},{10,1... | collective-permute-start | bytes 147464 | tf_op jit(solution)/shard_map/ppermute | solution.py:453
  37.5 0.0 copy-done.1
  37.5 0.1 copy.16.refs_6_
  37.6 7.1 %all-to-all-done.refs_7_ = f32[64,1,1536]{2,1,0:T(1,128)S(1)} async-done(((f32[64,1,1536]{2,1,0:T(1,128)}), f32[64,1,1536]{2,1,0:T(1,128)S(1)}, u32[]{:S(2)}, u32[]{:S(2)}) %all-to-all-start) | async-done | bytes 393248 | tf_op jit(solution)/shard_map/all_to_all | solution.py:489
  44.7 0.7 shard_map.80
  45.4 6.4 %all-to-all-start.1 = ((f32[8,1,1408]{2,1,0:T(1,128)}), f32[8,1,1408]{2,1,0:T(1,128)S(1)}, u32[]{:S(2)}, u32[]{:S(2)}) async-start(f32[8,1,1408]{2,1,0:T(1,128)} %bitcast.9), calls=%async_computation.1 | async-start | bytes 90112 | tf_op jit(solution)/shard_map/all_to_all | solution.py:499
  51.8 0.0 collective-permute-done.3.refs_1_
  51.8 0.0 copy-done
  51.8 3.1 %shard_map.79 = (f32[1536,128]{1,0:T(8,128)}, f32[8,128]{1,0:T(8,128)S(1)}) custom-call(f32[1536,128]{1,0:T(8,128)S(1)} %get-tuple-element.15.refs_0_, f32[96,128]{1,0:T(8,128)S(1)} %collective-permute-done.3.refs_1_, f32[96,128]{1,0:T(8,128)S(1)} %collective-permute-done.2.refs_4_.refs_2_, f32[2,96,128]{2,1,0:T(8,128)S(1)} %collective-permute-done.refs_5_.refs_1_.refs_3_, ...), custom_call_target="tpu_custom_call" | custom-call | flops 4076863488 | bytes 2359296 | tf_op jit(solution)/shard_map/pallas_call | solution.py:33
  54.8 8.7 %all-to-all-done.1 = f32[8,1,1408]{2,1,0:T(1,128)S(1)} async-done(((f32[8,1,1408]{2,1,0:T(1,128)}), f32[8,1,1408]{2,1,0:T(1,128)S(1)}, u32[]{:S(2)}, u32[]{:S(2)}) %all-to-all-start.1) | async-done | bytes 45088 | tf_op jit(solution)/shard_map/all_to_all | solution.py:499
  63.6 0.8 shard_map.81.refs_8_
  64.3 6.1 %all-to-all-start.2 = ((f32[64,1,1408]{2,1,0:T(1,128)}), f32[64,1,1408]{2,1,0:T(1,128)S(1)}, u32[]{:S(2)}, u32[]{:S(2)}) async-start(f32[64,1,1408]{2,1,0:T(1,128)} %bitcast.12), calls=%async_computation.2 | async-start | bytes 720896 | tf_op jit(solution)/shard_map/all_to_all | solution.py:511
  70.5 0.2 copy.17
  70.7 0.2 copy.18
  70.9 0.2 copy.20.refs_5_
  71.1 3.4 %shard_map.82 = (f32[1536,128]{1,0:T(8,128)}, f32[8,128]{1,0:T(8,128)}) custom-call(f32[1536,128]{1,0:T(8,128)S(1)} %get-tuple-element.19.refs_1_.refs_0_, f32[96,128]{1,0:T(8,128)S(1)} %collective-permute-done.3.refs_1_, f32[96,128]{1,0:T(8,128)S(1)} %collective-permute-done.2.refs_4_.refs_2_, ...), custom_call_target="tpu_custom_call" | custom-call | flops 4076863488 | bytes 2359296 | tf_op jit(solution)/shard_map/pallas_call | solution.py:33
  74.5 6.7 %all-to-all-done.2 = f32[64,1,1408]{2,1,0:T(1,128)S(1)} async-done(((f32[64,1,1408]{2,1,0:T(1,128)}), f32[64,1,1408]{2,1,0:T(1,128)S(1)}, u32[]{:S(2)}, u32[]{:S(2)}) %all-to-all-start.2) | async-done | bytes 360480 | tf_op jit(solution)/shard_map/all_to_all | solution.py:511
  81.2 0.8 %shard_map.83 = (f32[96,864]{1,0:T(8,128)}, f32[1,96]{1,0:T(1,128)}) custom-call(f32[704,128]{1,0:T(8,128)S(1)} %bitcast.17), custom_call_target="tpu_custom_call" | custom-call | bytes 786432 | tf_op jit(solution)/shard_map/pallas_call | solution.py:33
  (1 shorter events, 0.0 us)
Async XLA Ops:
  2.7 15.4 %collective-permute-start = (f32[2,96,128]{2,1,0:T(8,128)S(1)}, f32[2,96,128]{2,1,0:T(8,128)S(1)}, u32[]{:S(2)}, u32[]{:S(2)}) collective-permute-start(f32[2,96,128]{2,1,0:T(8,128)S(1)} %get-tuple-element.17.refs_2_), channel_id=1, source_target_pairs={{0,64},{1,65},{2,66},{3,67},{4,68},{5,69},{6,70},{7,71},{8,72},{9,... | collective-permute-start | bytes 294920 | tf_op jit(solution)/shard_map/ppermute | solution.py:453
  6.8 11.4 %collective-permute-start.1 = (f32[2,96,128]{2,1,0:T(8,128)S(1)}, f32[2,96,128]{2,1,0:T(8,128)S(1)}, u32[]{:S(2)}, u32[]{:S(2)}) collective-permute-start(f32[2,96,128]{2,1,0:T(8,128)S(1)} %get-tuple-element.18.refs_3_), channel_id=1, source_target_pairs={{0,32},{1,33},{2,34},{3,35},{4,36},{5,37},{6,38},{7,39},{8,40},{9,... | collective-permute-start | bytes 294920 | tf_op jit(solution)/shard_map/ppermute | solution.py:453
  11.4 6.7 %collective-permute-start.2 = (f32[96,128]{1,0:T(8,128)S(1)}, f32[96,128]{1,0:T(8,128)S(1)}, u32[]{:S(2)}, u32[]{:S(2)}) collective-permute-start(f32[96,128]{1,0:T(8,128)S(1)} %get-tuple-element.20), channel_id=1, source_target_pairs={{0,63},{1,0},{2,1},{3,2},{4,3},{5,4},{6,5},{7,6},{8,7},{9,8},{10,9... | collective-permute-start | bytes 147464 | tf_op jit(solution)/shard_map/ppermute | solution.py:453
  20.1 24.6 %all-to-all-start = ((f32[64,1,1536]{2,1,0:T(1,128)}), f32[64,1,1536]{2,1,0:T(1,128)S(1)}, u32[]{:S(2)}, u32[]{:S(2)}) async-start(f32[64,1,1536]{2,1,0:T(1,128)} %bitcast.3), calls=%async_computation | async-start | bytes 786432 | tf_op jit(solution)/shard_map/all_to_all | solution.py:489
  33.6 3.8 %copy-start.1 = (f32[96]{0:T(128)S(1)}, f32[96]{0:T(128)}, u32[]{:S(2)}) copy-start(f32[96]{0:T(128)} %param.6) | copy-start | bytes 1156
  33.8 18.0 %copy-start = (f32[96,864]{1,0:T(8,128)S(1)}, f32[96,864]{1,0:T(8,128)}, u32[]{:S(2)}) copy-start(f32[96,864]{1,0:T(8,128)} %refs_5_.1) | copy-start | bytes 995332
  33.8 18.0 %collective-permute-start.3 = (f32[96,128]{1,0:T(8,128)S(1)}, f32[96,128]{1,0:T(8,128)S(1)}, u32[]{:S(2)}, u32[]{:S(2)}) collective-permute-start(f32[96,128]{1,0:T(8,128)S(1)} %shard_map.78.refs_1_), channel_id=1, source_target_pairs={{0,1},{1,2},{2,3},{3,4},{4,5},{5,6},{6,7},{7,8},{8,9},{9,10},{10,1... | collective-permute-start | bytes 147464 | tf_op jit(solution)/shard_map/ppermute | solution.py:453
  45.4 18.2 %all-to-all-start.1 = ((f32[8,1,1408]{2,1,0:T(1,128)}), f32[8,1,1408]{2,1,0:T(1,128)S(1)}, u32[]{:S(2)}, u32[]{:S(2)}) async-start(f32[8,1,1408]{2,1,0:T(1,128)} %bitcast.9), calls=%async_computation.1 | async-start | bytes 90112 | tf_op jit(solution)/shard_map/all_to_all | solution.py:499
  64.3 16.9 %all-to-all-start.2 = ((f32[64,1,1408]{2,1,0:T(1,128)}), f32[64,1,1408]{2,1,0:T(1,128)S(1)}, u32[]{:S(2)}, u32[]{:S(2)}) async-start(f32[64,1,1408]{2,1,0:T(1,128)} %bitcast.12), calls=%async_computation.2 | async-start | bytes 720896 | tf_op jit(solution)/shard_map/all_to_all | solution.py:511

commit v5 on v4

--- a/solution.py
+++ b/solution.py
@@ -117,7 +117,7 @@
             at += now
 
 
-PIECES = 3
+PIECES = 1
 
 
 def front_kernel(x, g, own_1, own_2, west, east, x_here, g_here, sems):
@@ -216,7 +216,7 @@
 
 
 def outer_weight_kernel(
-    chunks, inner, own_east, own_1, own_2, east, row_1, row_2, packed, s_hi, s_lo, c_hi, c_lo
+    chunks, inner, own_east, own_1, own_2, east, row_1, row_2, packed, s_both, c_hi, c_lo
 ):
     lane = lanes()
     zero = jnp.zeros((C, L), F32)
@@ -233,29 +233,34 @@
     def put(k, left, right):
         at = pl.ds(k * L, L)
         for part, value in enumerate(left):
-            c_hi[pl.ds(part * C, C), at], c_lo[pl.ds(part * C, C), at] = split(value)
+            if value is None:
+                c_hi[pl.ds(part * C, C), at] = c_lo[pl.ds(part * C, C), at] = jnp.zeros((C, L), BF16)
+            else:
+                c_hi[pl.ds(part * C, C), at], c_lo[pl.ds(part * C, C), at] = split(value)
         for part, value in enumerate(right):
-            s_hi[pl.ds(part * C, C), at], s_lo[pl.ds(part * C, C), at] = split(value)
-
-    put(0, (north * at_top, zero, north * (1.0 - at_top)), inner_taps(x_top))
-    put(1, (south * (1.0 - at_bottom), zero, south * at_bottom), inner_taps(x_bottom))
+            high = pl.ds(part * C, C)
+            low = pl.ds((3 + part) * C, C)
+            if value is None:
+                s_both[high, at] = s_both[low, at] = jnp.zeros((C, L), BF16)
+            else:
+                s_both[high, at], s_both[low, at] = split(value)
+
+    put(0, (north * at_top, None, north * (1.0 - at_top)), inner_taps(x_top))
+    put(1, (south * (1.0 - at_bottom), None, south * at_bottom), inner_taps(x_bottom))
     g_column = roll(column, -HALF)
     below = roll(g_column, -2)
     above = g_column
     south_end = jnp.where(lane == R - 1, below * at_bottom, 0.0)
     north_end = jnp.where(lane == 0, above * at_top, 0.0)
-    put(
-        2,
-        (below - south_end + north_end, roll(g_column, -1), above - north_end + south_end),
-        (zero, zero, jnp.where(lane < R, beyond, 0.0)),
-    )
-    g_beyond = jnp.where(lane < R, roll(beyond, -HALF), 0.0)
-    put(
-        3,
-        (g_beyond, roll(g_beyond, 1), roll(g_beyond, 2)),
-        (jnp.where(lane < R + 2, column, 0.0), zero, zero),
-    )
-    grad = nt(c_hi, s_hi) + nt(c_hi, s_lo) + nt(c_lo, s_hi)
+    shifted = (below - south_end + north_end, roll(g_column, -1), above - north_end + south_end)
+    left = []
+    for a, value in enumerate(shifted):
+        other = jnp.where(lane < HALF + a + R, roll(beyond, a), 0.0)
+        left.append(jnp.where(lane < HALF, value, jnp.where(lane < HALF + a, 0.0, other)))
+    own = jnp.where(lane < HALF + R + 2, roll(column, HALF), 0.0)
+    put(2, left, (jnp.where(lane < HALF, 0.0, own), None, jnp.where(lane < R, beyond, 0.0)))
+    both = nt(c_hi, s_both)
+    grad = both[:, : 3 * C] + both[:, 3 * C :] + nt(c_lo, s_both.at[pl.ds(0, 3 * C), :])
     wide = inner[...] + wide_form(grad, jnp.zeros((C, 1), F32))
     cells = zero
     for k, at in enumerate((0, HALF, R - 1, HALF + R - 1)):
@@ -482,7 +487,7 @@
         functools.partial(outer_weight_kernel, chunks),
         [out(n_near * chunks.sent, L)],
         (inner, own_east, own_1, own_2, east, row_1, row_2),
-        [pltpu.VMEM((3 * C, 4 * L), BF16)] * 4,
+        [pltpu.VMEM((6 * C, 3 * L), BF16)] + [pltpu.VMEM((3 * C, 3 * L), BF16)] * 2,
         flops=product // 4,
         moved=block,
     )[0]

time: 82.5 us -> 82.4 us (level)
  no operation moved by 1% of the time
where the time goes in v5:
time: 82.4 us; the launch traced here: 81.9 us
  starting transfers between devices  42.4 us (51%)
  waiting for transfers between devices  22.8 us (28%)
  Pallas kernels  15.3 us (19%)
    ppermute x4, starting transfers between devices, send(): return lax.ppermute(value, AXES, pairs)  16.3 us
    pallas_call x9, Pallas kernels, call(): pl.pallas_call(body, out_shape=outs, in_specs=(specs or [VMEM] * len(args...  15.3 us
    all_to_all x1, starting transfers between devices, shards(): lax.all_to_all(packed.reshape(n_near, 1, chunks.sent * L), NEAR, 0, 0)  13.5 us
    all_to_all x1, waiting for transfers between devices, shards(): others = lax.all_to_all(mine.reshape(n_far, 1, chunks.rows * L), FAR, 0, 0)  8.73 us
    all_to_all x1, waiting for transfers between devices, shards(): lax.all_to_all(packed.reshape(n_near, 1, chunks.sent * L), NEAR, 0, 0)  7.11 us
    all_to_all x1, waiting for transfers between devices, shards(): lax.all_to_all(mine.reshape(n_near, 1, chunks.rows * L), NEAR, 0, 0)  6.71 us
    all_to_all x1, starting transfers between devices, shards(): others = lax.all_to_all(mine.reshape(n_far, 1, chunks.rows * L), FAR, 0, 0)  6.38 us
    all_to_all x1, starting transfers between devices, shards(): lax.all_to_all(mine.reshape(n_near, 1, chunks.rows * L), NEAR, 0, 0)  6.14 us
  transfers between devices with their start and end apart: 7, of which 4 were waited for; matrix products, arithmetic and copies ran while one was open for 1% of the time, Pallas kernels for 12%

profile of v5, /device:TPU:1, one launch (start us, length us, event | category | flops | bytes accessed | tf_op | source)
XLA Modules:
  0.0 81.9 jit_solution(7909356997970679078)
XLA Ops:
  0.6 2.0 %shard_map.75 = (f32[2,96,128]{2,1,0:T(8,128)S(1)}, f32[2,96,128]{2,1,0:T(8,128)S(1)}, f32[96,128]{1,0:T(8,128)S(1)}, f32[96,128]{1,0:T(8,128)S(1)}, f32[1536,128]{1,0:T(8,128)S(1)}, /*index=5*/f32[1536,128]{1,0:T(8,128)S(1)}) custom-call(f32[1536,128]{1,0:T(8,128)} %bitcast.21, f32[1536,128]{1,0:T(8,128)} %bitcast.22), custom_call_target="tpu_custom_call" | custom-call | flops 786432 | bytes 1572864 | tf_op jit(solution)/shard_map/pallas_call | solution.py:33
  2.7 4.0 %collective-permute-start = (f32[2,96,128]{2,1,0:T(8,128)S(1)}, f32[2,96,128]{2,1,0:T(8,128)S(1)}, u32[]{:S(2)}, u32[]{:S(2)}) collective-permute-start(f32[2,96,128]{2,1,0:T(8,128)S(1)} %get-tuple-element.17.refs_2_), channel_id=1, source_target_pairs={{0,64},{1,65},{2,66},{3,67},{4,68},{5,69},{6,70},{7,71},{8,72},{9,... | collective-permute-start | bytes 294920 | tf_op jit(solution)/shard_map/ppermute | solution.py:458
  6.7 4.7 %collective-permute-start.1 = (f32[2,96,128]{2,1,0:T(8,128)S(1)}, f32[2,96,128]{2,1,0:T(8,128)S(1)}, u32[]{:S(2)}, u32[]{:S(2)}) collective-permute-start(f32[2,96,128]{2,1,0:T(8,128)S(1)} %get-tuple-element.18.refs_3_), channel_id=1, source_target_pairs={{0,32},{1,33},{2,34},{3,35},{4,36},{5,37},{6,38},{7,39},{8,40},{9,... | collective-permute-start | bytes 294920 | tf_op jit(solution)/shard_map/ppermute | solution.py:458
  11.4 3.9 %collective-permute-start.2 = (f32[96,128]{1,0:T(8,128)S(1)}, f32[96,128]{1,0:T(8,128)S(1)}, u32[]{:S(2)}, u32[]{:S(2)}) collective-permute-start(f32[96,128]{1,0:T(8,128)S(1)} %get-tuple-element.20), channel_id=1, source_target_pairs={{0,63},{1,0},{2,1},{3,2},{4,3},{5,4},{6,5},{7,6},{8,7},{9,8},{10,9... | collective-permute-start | bytes 147464 | tf_op jit(solution)/shard_map/ppermute | solution.py:458
  15.3 2.5 %shard_map.76.refs_0_ = f32[96,896]{1,0:T(8,128)S(1)} custom-call(f32[1536,128]{1,0:T(8,128)S(1)} %get-tuple-element.15.refs_0_, f32[1536,128]{1,0:T(8,128)S(1)} %get-tuple-element.19.refs_1_.refs_0_), custom_call_target="tpu_custom_call" | custom-call | flops 1019215872 | bytes 1572864 | tf_op jit(solution)/shard_map/pallas_call | solution.py:33
  17.9 0.2 collective-permute-done.2.refs_4_.refs_2_
  18.1 0.0 collective-permute-done.refs_5_.refs_1_.refs_3_
  18.1 0.0 collective-permute-done.1.refs_6_.refs_2_.refs_4_
  18.1 1.8 %shard_map.77.refs_3_ = f32[768,128]{1,0:T(8,128)} custom-call(f32[96,896]{1,0:T(8,128)S(1)} %shard_map.76.refs_0_, f32[96,128]{1,0:T(8,128)S(1)} %get-tuple-element.16.refs_1_.refs_0_, f32[2,96,128]{2,1,0:T(8,128)S(1)} %get-tuple-element.17.refs_2_, f32[2,96,128]{2,1,0:T(8,128)S(1)} %get-tuple-element.18.refs_3_, ...), custom_call_target="tpu_custom_call" | custom-call | flops 254803968 | bytes 786432 | tf_op jit(solution)/shard_map/pallas_call | solution.py:33
  19.9 13.5 %all-to-all-start = ((f32[64,1,1536]{2,1,0:T(1,128)}), f32[64,1,1536]{2,1,0:T(1,128)S(1)}, u32[]{:S(2)}, u32[]{:S(2)}) async-start(f32[64,1,1536]{2,1,0:T(1,128)} %bitcast.3), calls=%async_computation | async-start | bytes 786432 | tf_op jit(solution)/shard_map/all_to_all | solution.py:494
  33.4 0.0 copy-start.1
  33.5 0.1 shard_map.78.refs_1_
  33.6 0.0 copy-start
  33.6 3.7 %collective-permute-start.3 = (f32[96,128]{1,0:T(8,128)S(1)}, f32[96,128]{1,0:T(8,128)S(1)}, u32[]{:S(2)}, u32[]{:S(2)}) collective-permute-start(f32[96,128]{1,0:T(8,128)S(1)} %shard_map.78.refs_1_), channel_id=1, source_target_pairs={{0,1},{1,2},{2,3},{3,4},{4,5},{5,6},{6,7},{7,8},{8,9},{9,10},{10,1... | collective-permute-start | bytes 147464 | tf_op jit(solution)/shard_map/ppermute | solution.py:458
  37.3 0.0 copy-done.1
  37.3 0.1 copy.16.refs_6_
  37.4 7.1 %all-to-all-done.refs_7_ = f32[64,1,1536]{2,1,0:T(1,128)S(1)} async-done(((f32[64,1,1536]{2,1,0:T(1,128)}), f32[64,1,1536]{2,1,0:T(1,128)S(1)}, u32[]{:S(2)}, u32[]{:S(2)}) %all-to-all-start) | async-done | bytes 393248 | tf_op jit(solution)/shard_map/all_to_all | solution.py:494
  44.5 0.7 shard_map.80
  45.2 6.4 %all-to-all-start.1 = ((f32[8,1,1408]{2,1,0:T(1,128)}), f32[8,1,1408]{2,1,0:T(1,128)S(1)}, u32[]{:S(2)}, u32[]{:S(2)}) async-start(f32[8,1,1408]{2,1,0:T(1,128)} %bitcast.9), calls=%async_computation.1 | async-start | bytes 90112 | tf_op jit(solution)/shard_map/all_to_all | solution.py:504
  51.6 0.0 collective-permute-done.3.refs_1_
  51.6 0.0 copy-done
  51.6 3.1 %shard_map.79 = (f32[1536,128]{1,0:T(8,128)}, f32[8,128]{1,0:T(8,128)S(1)}) custom-call(f32[1536,128]{1,0:T(8,128)S(1)} %get-tuple-element.15.refs_0_, f32[96,128]{1,0:T(8,128)S(1)} %collective-permute-done.3.refs_1_, f32[96,128]{1,0:T(8,128)S(1)} %collective-permute-done.2.refs_4_.refs_2_, f32[2,96,128]{2,1,0:T(8,128)S(1)} %collective-permute-done.refs_5_.refs_1_.refs_3_, ...), custom_call_target="tpu_custom_call" | custom-call | flops 4076863488 | bytes 2359296 | tf_op jit(solution)/shard_map/pallas_call | solution.py:33
  54.7 8.7 %all-to-all-done.1 = f32[8,1,1408]{2,1,0:T(1,128)S(1)} async-done(((f32[8,1,1408]{2,1,0:T(1,128)}), f32[8,1,1408]{2,1,0:T(1,128)S(1)}, u32[]{:S(2)}, u32[]{:S(2)}) %all-to-all-start.1) | async-done | bytes 45088 | tf_op jit(solution)/shard_map/all_to_all | solution.py:504
  63.4 0.8 shard_map.81.refs_8_
  64.2 6.1 %all-to-all-start.2 = ((f32[64,1,1408]{2,1,0:T(1,128)}), f32[64,1,1408]{2,1,0:T(1,128)S(1)}, u32[]{:S(2)}, u32[]{:S(2)}) async-start(f32[64,1,1408]{2,1,0:T(1,128)} %bitcast.12), calls=%async_computation.2 | async-start | bytes 720896 | tf_op jit(solution)/shard_map/all_to_all | solution.py:516
  70.3 0.2 copy.17
  70.6 0.2 copy.18
  70.7 0.2 copy.20.refs_5_
  70.9 3.4 %shard_map.82 = (f32[1536,128]{1,0:T(8,128)}, f32[8,128]{1,0:T(8,128)}) custom-call(f32[1536,128]{1,0:T(8,128)S(1)} %get-tuple-element.19.refs_1_.refs_0_, f32[96,128]{1,0:T(8,128)S(1)} %collective-permute-done.3.refs_1_, f32[96,128]{1,0:T(8,128)S(1)} %collective-permute-done.2.refs_4_.refs_2_, ...), custom_call_target="tpu_custom_call" | custom-call | flops 4076863488 | bytes 2359296 | tf_op jit(solution)/shard_map/pallas_call | solution.py:33
  74.4 6.7 %all-to-all-done.2 = f32[64,1,1408]{2,1,0:T(1,128)S(1)} async-done(((f32[64,1,1408]{2,1,0:T(1,128)}), f32[64,1,1408]{2,1,0:T(1,128)S(1)}, u32[]{:S(2)}, u32[]{:S(2)}) %all-to-all-start.2) | async-done | bytes 360480 | tf_op jit(solution)/shard_map/all_to_all | solution.py:516
  81.1 0.8 %shard_map.83 = (f32[96,864]{1,0:T(8,128)}, f32[1,96]{1,0:T(1,128)}) custom-call(f32[704,128]{1,0:T(8,128)S(1)} %bitcast.17), custom_call_target="tpu_custom_call" | custom-call | bytes 786432 | tf_op jit(solution)/shard_map/pallas_call | solution.py:33
  (1 shorter events, 0.0 us)
Async XLA Ops:
  2.7 15.4 %collective-permute-start = (f32[2,96,128]{2,1,0:T(8,128)S(1)}, f32[2,96,128]{2,1,0:T(8,128)S(1)}, u32[]{:S(2)}, u32[]{:S(2)}) collective-permute-start(f32[2,96,128]{2,1,0:T(8,128)S(1)} %get-tuple-element.17.refs_2_), channel_id=1, source_target_pairs={{0,64},{1,65},{2,66},{3,67},{4,68},{5,69},{6,70},{7,71},{8,72},{9,... | collective-permute-start | bytes 294920 | tf_op jit(solution)/shard_map/ppermute | solution.py:458
  6.7 11.4 %collective-permute-start.1 = (f32[2,96,128]{2,1,0:T(8,128)S(1)}, f32[2,96,128]{2,1,0:T(8,128)S(1)}, u32[]{:S(2)}, u32[]{:S(2)}) collective-permute-start(f32[2,96,128]{2,1,0:T(8,128)S(1)} %get-tuple-element.18.refs_3_), channel_id=1, source_target_pairs={{0,32},{1,33},{2,34},{3,35},{4,36},{5,37},{6,38},{7,39},{8,40},{9,... | collective-permute-start | bytes 294920 | tf_op jit(solution)/shard_map/ppermute | solution.py:458
  11.4 6.7 %collective-permute-start.2 = (f32[96,128]{1,0:T(8,128)S(1)}, f32[96,128]{1,0:T(8,128)S(1)}, u32[]{:S(2)}, u32[]{:S(2)}) collective-permute-start(f32[96,128]{1,0:T(8,128)S(1)} %get-tuple-element.20), channel_id=1, source_target_pairs={{0,63},{1,0},{2,1},{3,2},{4,3},{5,4},{6,5},{7,6},{8,7},{9,8},{10,9... | collective-permute-start | bytes 147464 | tf_op jit(solution)/shard_map/ppermute | solution.py:458
  19.9 24.6 %all-to-all-start = ((f32[64,1,1536]{2,1,0:T(1,128)}), f32[64,1,1536]{2,1,0:T(1,128)S(1)}, u32[]{:S(2)}, u32[]{:S(2)}) async-start(f32[64,1,1536]{2,1,0:T(1,128)} %bitcast.3), calls=%async_computation | async-start | bytes 786432 | tf_op jit(solution)/shard_map/all_to_all | solution.py:494
  33.4 3.8 %copy-start.1 = (f32[96]{0:T(128)S(1)}, f32[96]{0:T(128)}, u32[]{:S(2)}) copy-start(f32[96]{0:T(128)} %param.6) | copy-start | bytes 1156
  33.6 18.0 %copy-start = (f32[96,864]{1,0:T(8,128)S(1)}, f32[96,864]{1,0:T(8,128)}, u32[]{:S(2)}) copy-start(f32[96,864]{1,0:T(8,128)} %refs_5_.1) | copy-start | bytes 995332
  33.6 18.0 %collective-permute-start.3 = (f32[96,128]{1,0:T(8,128)S(1)}, f32[96,128]{1,0:T(8,128)S(1)}, u32[]{:S(2)}, u32[]{:S(2)}) collective-permute-start(f32[96,128]{1,0:T(8,128)S(1)} %shard_map.78.refs_1_), channel_id=1, source_target_pairs={{0,1},{1,2},{2,3},{3,4},{4,5},{5,6},{6,7},{7,8},{8,9},{9,10},{10,1... | collective-permute-start | bytes 147464 | tf_op jit(solution)/shard_map/ppermute | solution.py:458
  45.2 18.2 %all-to-all-start.1 = ((f32[8,1,1408]{2,1,0:T(1,128)}), f32[8,1,1408]{2,1,0:T(1,128)S(1)}, u32[]{:S(2)}, u32[]{:S(2)}) async-start(f32[8,1,1408]{2,1,0:T(1,128)} %bitcast.9), calls=%async_computation.1 | async-start | bytes 90112 | tf_op jit(solution)/shard_map/all_to_all | solution.py:504
  64.2 16.9 %all-to-all-start.2 = ((f32[64,1,1408]{2,1,0:T(1,128)}), f32[64,1,1408]{2,1,0:T(1,128)S(1)}, u32[]{:S(2)}, u32[]{:S(2)}) async-start(f32[64,1,1408]{2,1,0:T(1,128)} %bitcast.12), calls=%async_computation.2 | async-start | bytes 720896 | tf_op jit(solution)/shard_map/all_to_all | solution.py:516

commit v6 on v5

--- a/solution.py
+++ b/solution.py
@@ -492,28 +492,27 @@
         moved=block,
     )[0]
     parts = lax.all_to_all(packed.reshape(n_near, 1, chunks.sent * L), NEAR, 0, 0)
-    column = call(column_kernel, [kept(C, L)], (own_east, row_1, row_2), after=(packed,))[0]
-    west = send(column, to_east)
     mine = call(
         functools.partial(sum_kernel, chunks.rows, chunks.sent),
         [out(n_far * chunks.rows, L)],
         (parts.reshape(n_near * chunks.sent, L),),
-        after=(column,),
         moved=block // 2,
     )[0]
+    column = call(column_kernel, [kept(C, L)], (own_east, row_1, row_2), after=(mine,))[0]
+    west = send(column, to_east)
     others = lax.all_to_all(mine.reshape(n_far, 1, chunks.rows * L), FAR, 0, 0)
     flipped = weight.reshape(C, 3, 3, C)[:, ::-1, ::-1].transpose(3, 1, 2, 0).reshape(C, 9 * C)
     halo = (west, east, row_1, row_2)
     bias = bias.reshape(C, 1)
-    output, token = conv(False, x, *halo, weight, bias, parts)
     mine = call(
         functools.partial(sum_kernel, chunks.rows, chunks.rows),
         [out(n_near * chunks.rows, L)],
         (others.reshape(n_far * chunks.rows, L),),
-        after=(token,),
+        after=(west, flipped, bias),
         moved=block // 2,
     )[0]
     gathered = lax.all_to_all(mine.reshape(n_near, 1, chunks.rows * L), NEAR, 0, 0)
+    output, _ = conv(False, x, *halo, weight, bias, parts, after=(mine,))
     grad, _ = conv(True, g, *halo, flipped, bias, parts, after=(mine,))
     weight_grad, bias_grad = call(
         functools.partial(unpack_kernel, chunks, factor),

time: 82.4 us -> 81.4 us (0.988)
  blocking collectives: 0 us -> 24.4 us
  starting transfers between devices: 42.4 us -> 27.7 us
  waiting for transfers between devices: 22.8 us -> 10.5 us
  local copies, waits for them, and re-layouts: 0.72 us -> 3.14 us
    all_to_all x0 -> x1, blocking collectives: none -> 24.4 us  [shards(): lax.all_to_all(packed.reshape(n_near, 1, chunks.sent * L), NEAR, 0, 0)]
    all_to_all x1 -> x0, starting transfers between devices: 13.5 us -> none  [shards(): lax.all_to_all(packed.reshape(n_near, 1, chunks.sent * L), NEAR, 0, 0)]
    all_to_all x1 -> x0, waiting for transfers between devices: 7.11 us -> none  [shards(): lax.all_to_all(packed.reshape(n_near, 1, chunks.sent * L), NEAR, 0, 0)]
    all_to_all x1, waiting for transfers between devices: 8.73 us -> 5.89 us  [shards(): others = lax.all_to_all(mine.reshape(n_far, 1, chunks.rows * L), FAR, 0, 0)]
    all_to_all x1, waiting for transfers between devices: 6.71 us -> 4.35 us  [shards(): lax.all_to_all(mine.reshape(n_near, 1, chunks.rows * L), NEAR, 0, 0)]
    transpose x2, local copies, waits for them, and re-layouts: 0.22 us -> 1.99 us  [shards(): weight.reshape(C, 3, 3, C)[:, ::-1, ::-1].transpose(3, 1, 2, 0)]
  transfers between devices with their start and end apart: 7 -> 6, of which waited for: 4 -> 3; matrix products, arithmetic and copies ran while one was open for 1% -> 3% of each run, Pallas kernels for 12% -> 11%
where the time goes in v6:
time: 81.4 us; the launch traced here: 81 us
  starting transfers between devices  27.7 us (34%)
  blocking collectives  24.4 us (30%)
  Pallas kernels  14.6 us (18%)
  waiting for transfers between devices  10.5 us (13%)
  local copies, waits for them, and re-layouts  3.14 us (4%)
    all_to_all x1, blocking collectives, shards(): lax.all_to_all(packed.reshape(n_near, 1, chunks.sent * L), NEAR, 0, 0)  24.4 us
    ppermute x4, starting transfers between devices, send(): return lax.ppermute(value, AXES, pairs)  15.6 us
    pallas_call x9, Pallas kernels, call(): pl.pallas_call(body, out_shape=outs, in_specs=(specs or [VMEM] * len(args...  14.6 us
    all_to_all x1, starting transfers between devices, shards(): others = lax.all_to_all(mine.reshape(n_far, 1, chunks.rows * L), FAR, 0, 0)  6.38 us
    all_to_all x1, waiting for transfers between devices, shards(): others = lax.all_to_all(mine.reshape(n_far, 1, chunks.rows * L), FAR, 0, 0)  5.89 us
    all_to_all x1, starting transfers between devices, shards(): lax.all_to_all(mine.reshape(n_near, 1, chunks.rows * L), NEAR, 0, 0)  5.69 us
    all_to_all x1, waiting for transfers between devices, shards(): lax.all_to_all(mine.reshape(n_near, 1, chunks.rows * L), NEAR, 0, 0)  4.35 us
    transpose x2, local copies, waits for them, and re-layouts, shards(): weight.reshape(C, 3, 3, C)[:, ::-1, ::-1].transpose(3, 1, 2, 0)  1.99 us
  transfers between devices with their start and end apart: 6, of which 3 were waited for; matrix products, arithmetic and copies ran while one was open for 3% of the time, Pallas kernels for 11%

profile of v6, /device:TPU:1, one launch (start us, length us, event | category | flops | bytes accessed | tf_op | source)
XLA Modules:
  0.0 81.0 jit_solution(6310942735695060854)
XLA Ops:
  0.6 2.0 %shard_map.75 = (f32[2,96,128]{2,1,0:T(8,128)S(1)}, f32[2,96,128]{2,1,0:T(8,128)S(1)}, f32[96,128]{1,0:T(8,128)S(1)}, f32[96,128]{1,0:T(8,128)S(1)}, f32[1536,128]{1,0:T(8,128)S(1)}, /*index=5*/f32[1536,128]{1,0:T(8,128)S(1)}) custom-call(f32[1536,128]{1,0:T(8,128)} %bitcast.22, f32[1536,128]{1,0:T(8,128)} %bitcast.23), custom_call_target="tpu_custom_call" | custom-call | flops 786432 | bytes 1572864 | tf_op jit(solution)/shard_map/pallas_call | solution.py:33
  2.7 4.0 %collective-permute-start = (f32[2,96,128]{2,1,0:T(8,128)S(1)}, f32[2,96,128]{2,1,0:T(8,128)S(1)}, u32[]{:S(2)}, u32[]{:S(2)}) collective-permute-start(f32[2,96,128]{2,1,0:T(8,128)S(1)} %get-tuple-element.16.refs_2_), channel_id=1, source_target_pairs={{0,64},{1,65},{2,66},{3,67},{4,68},{5,69},{6,70},{7,71},{8,72},{9,... | collective-permute-start | bytes 294920 | tf_op jit(solution)/shard_map/ppermute | solution.py:458
  6.7 4.7 %collective-permute-start.1 = (f32[2,96,128]{2,1,0:T(8,128)S(1)}, f32[2,96,128]{2,1,0:T(8,128)S(1)}, u32[]{:S(2)}, u32[]{:S(2)}) collective-permute-start(f32[2,96,128]{2,1,0:T(8,128)S(1)} %get-tuple-element.17.refs_3_), channel_id=1, source_target_pairs={{0,32},{1,33},{2,34},{3,35},{4,36},{5,37},{6,38},{7,39},{8,40},{9,... | collective-permute-start | bytes 294920 | tf_op jit(solution)/shard_map/ppermute | solution.py:458
  11.4 3.9 %collective-permute-start.2 = (f32[96,128]{1,0:T(8,128)S(1)}, f32[96,128]{1,0:T(8,128)S(1)}, u32[]{:S(2)}, u32[]{:S(2)}) collective-permute-start(f32[96,128]{1,0:T(8,128)S(1)} %get-tuple-element.19), channel_id=1, source_target_pairs={{0,63},{1,0},{2,1},{3,2},{4,3},{5,4},{6,5},{7,6},{8,7},{9,8},{10,9... | collective-permute-start | bytes 147464 | tf_op jit(solution)/shard_map/ppermute | solution.py:458
  15.3 2.5 %shard_map.76.refs_0_ = f32[96,896]{1,0:T(8,128)S(1)} custom-call(f32[1536,128]{1,0:T(8,128)S(1)} %get-tuple-element.14.refs_0_, f32[1536,128]{1,0:T(8,128)S(1)} %get-tuple-element.18.refs_1_.refs_0_), custom_call_target="tpu_custom_call" | custom-call | flops 1019215872 | bytes 1572864 | tf_op jit(solution)/shard_map/pallas_call | solution.py:33
  17.9 0.2 collective-permute-done.2.refs_4_.refs_2_
  18.1 0.0 collective-permute-done.refs_5_.refs_1_.refs_3_
  18.1 0.0 collective-permute-done.1.refs_6_.refs_2_.refs_4_
  18.1 1.1 %shard_map.77 = f32[768,128]{1,0:T(8,128)S(1)} custom-call(f32[96,896]{1,0:T(8,128)S(1)} %shard_map.76.refs_0_, f32[96,128]{1,0:T(8,128)S(1)} %get-tuple-element.15.refs_1_.refs_0_, f32[2,96,128]{2,1,0:T(8,128)S(1)} %get-tuple-element.16.refs_2_, f32[2,96,128]{2,1,0:T(8,128)S(1)} %get-tuple-element.17.refs_3_, ...), custom_call_target="tpu_custom_call" | custom-call | flops 254803968 | bytes 786432 | tf_op jit(solution)/shard_map/pallas_call | solution.py:33
  19.2 24.4 %all_to_all.15.refs_7_ = f32[64,1,1536]{2,1,0:T(1,128)S(1)} all-to-all(f32[64,1,1536]{2,1,0:T(1,128)S(1)} %bitcast.17), channel_id=1, replica_groups=mesh['lat'=8,'xh'=2,'zr'=8,'zd'=2,'c'=2] {'lat','xh','zd','c'}, dimensions={0} | all-to-all | bytes 786432 | tf_op jit(solution)/shard_map/all_to_all | solution.py:494
  43.6 0.0 copy-start
  43.6 0.7 shard_map.78.refs_3_
  44.3 6.4 %all-to-all-start.1 = ((f32[8,1,1408]{2,1,0:T(1,128)}), f32[8,1,1408]{2,1,0:T(1,128)S(1)}, u32[]{:S(2)}, u32[]{:S(2)}) async-start(f32[8,1,1408]{2,1,0:T(1,128)} %bitcast.5), calls=%async_computation.1 | async-start | bytes 90112 | tf_op jit(solution)/shard_map/all_to_all | solution.py:503
  50.7 0.0 copy-done
  50.7 0.2 copy.20
  50.9 0.1 shard_map.79
  51.0 3.0 %collective-permute-start.3 = (f32[96,128]{1,0:T(8,128)S(1)}, f32[96,128]{1,0:T(8,128)S(1)}, u32[]{:S(2)}, u32[]{:S(2)}) collective-permute-start(f32[96,128]{1,0:T(8,128)S(1)} %shard_map.79), channel_id=1, source_target_pairs={{0,1},{1,2},{2,3},{3,4},{4,5},{5,6},{6,7},{7,8},{8,9},{9,10},{10,1... | collective-permute-start | bytes 147464 | tf_op jit(solution)/shard_map/ppermute | solution.py:458
  54.0 0.8 reverse_bitcast_fusion
  54.7 0.0 copy-start.1
  54.8 0.7 copy-done.1
  55.4 0.1 copy.24.refs_3_.refs_6_
  55.5 1.2 %copy.21 = f32[96,3,3,96]{0,3,2,1:T(8,128)S(1)} copy(f32[96,3,3,96]{3,0,2,1:T(8,128)} %reverse_bitcast_fusion) | data formatting | bytes 663552 | tf_op jit(solution)/shard_map/transpose | solution.py:504
  56.7 0.2 copy.22.refs_2_.refs_5_
  56.9 0.0 collective-permute-done.3.refs_1_
  56.9 5.9 %all-to-all-done.1 = f32[8,1,1408]{2,1,0:T(1,128)S(1)} async-done(((f32[8,1,1408]{2,1,0:T(1,128)}), f32[8,1,1408]{2,1,0:T(1,128)S(1)}, u32[]{:S(2)}, u32[]{:S(2)}) %all-to-all-start.1) | async-done | bytes 45088 | tf_op jit(solution)/shard_map/all_to_all | solution.py:503
  62.8 0.8 shard_map.80.refs_8_
  63.6 5.7 %all-to-all-start.2 = ((f32[64,1,1408]{2,1,0:T(1,128)}), f32[64,1,1408]{2,1,0:T(1,128)S(1)}, u32[]{:S(2)}, u32[]{:S(2)}) async-start(f32[64,1,1408]{2,1,0:T(1,128)} %bitcast.12), calls=%async_computation.2 | async-start | bytes 720896 | tf_op jit(solution)/shard_map/all_to_all | solution.py:514
  69.3 3.4 %shard_map.82 = (f32[1536,128]{1,0:T(8,128)}, f32[8,128]{1,0:T(8,128)}) custom-call(f32[1536,128]{1,0:T(8,128)S(1)} %get-tuple-element.18.refs_1_.refs_0_, f32[96,128]{1,0:T(8,128)S(1)} %collective-permute-done.3.refs_1_, f32[96,128]{1,0:T(8,128)S(1)} %collective-permute-done.2.refs_4_.refs_2_, ...), custom_call_target="tpu_custom_call" | custom-call | flops 4076863488 | bytes 2359296 | tf_op jit(solution)/shard_map/pallas_call | solution.py:33
  72.7 3.1 %shard_map.81 = (f32[1536,128]{1,0:T(8,128)}, f32[8,128]{1,0:T(8,128)}) custom-call(f32[1536,128]{1,0:T(8,128)S(1)} %get-tuple-element.14.refs_0_, f32[96,128]{1,0:T(8,128)S(1)} %collective-permute-done.3.refs_1_, f32[96,128]{1,0:T(8,128)S(1)} %collective-permute-done.2.refs_4_.refs_2_, f32[2,96,128]{2,1,0:T(8,128)S(1)} %collective-permute-done.refs_5_.refs_1_.refs_3_, ...), custom_call_target="tpu_custom_call" | custom-call | flops 4076863488 | bytes 2359296 | tf_op jit(solution)/shard_map/pallas_call | solution.py:33
  75.8 4.3 %all-to-all-done.2 = f32[64,1,1408]{2,1,0:T(1,128)S(1)} async-done(((f32[64,1,1408]{2,1,0:T(1,128)}), f32[64,1,1408]{2,1,0:T(1,128)S(1)}, u32[]{:S(2)}, u32[]{:S(2)}) %all-to-all-start.2) | async-done | bytes 360480 | tf_op jit(solution)/shard_map/all_to_all | solution.py:514
  80.1 0.8 %shard_map.83 = (f32[96,864]{1,0:T(8,128)}, f32[1,96]{1,0:T(1,128)}) custom-call(f32[704,128]{1,0:T(8,128)S(1)} %bitcast.18), custom_call_target="tpu_custom_call" | custom-call | bytes 786432 | tf_op jit(solution)/shard_map/pallas_call | solution.py:33
Async XLA Ops:
  2.7 15.4 %collective-permute-start = (f32[2,96,128]{2,1,0:T(8,128)S(1)}, f32[2,96,128]{2,1,0:T(8,128)S(1)}, u32[]{:S(2)}, u32[]{:S(2)}) collective-permute-start(f32[2,96,128]{2,1,0:T(8,128)S(1)} %get-tuple-element.16.refs_2_), channel_id=1, source_target_pairs={{0,64},{1,65},{2,66},{3,67},{4,68},{5,69},{6,70},{7,71},{8,72},{9,... | collective-permute-start | bytes 294920 | tf_op jit(solution)/shard_map/ppermute | solution.py:458
  6.7 11.4 %collective-permute-start.1 = (f32[2,96,128]{2,1,0:T(8,128)S(1)}, f32[2,96,128]{2,1,0:T(8,128)S(1)}, u32[]{:S(2)}, u32[]{:S(2)}) collective-permute-start(f32[2,96,128]{2,1,0:T(8,128)S(1)} %get-tuple-element.17.refs_3_), channel_id=1, source_target_pairs={{0,32},{1,33},{2,34},{3,35},{4,36},{5,37},{6,38},{7,39},{8,40},{9,... | collective-permute-start | bytes 294920 | tf_op jit(solution)/shard_map/ppermute | solution.py:458
  11.4 6.7 %collective-permute-start.2 = (f32[96,128]{1,0:T(8,128)S(1)}, f32[96,128]{1,0:T(8,128)S(1)}, u32[]{:S(2)}, u32[]{:S(2)}) collective-permute-start(f32[96,128]{1,0:T(8,128)S(1)} %get-tuple-element.19), channel_id=1, source_target_pairs={{0,63},{1,0},{2,1},{3,2},{4,3},{5,4},{6,5},{7,6},{8,7},{9,8},{10,9... | collective-permute-start | bytes 147464 | tf_op jit(solution)/shard_map/ppermute | solution.py:458
  43.6 7.1 %copy-start = (f32[96,864]{1,0:T(8,128)S(1)}, f32[96,864]{1,0:T(8,128)}, u32[]{:S(2)}) copy-start(f32[96,864]{1,0:T(8,128)} %refs_5_.1) | copy-start | bytes 995332
  44.3 18.5 %all-to-all-start.1 = ((f32[8,1,1408]{2,1,0:T(1,128)}), f32[8,1,1408]{2,1,0:T(1,128)S(1)}, u32[]{:S(2)}, u32[]{:S(2)}) async-start(f32[8,1,1408]{2,1,0:T(1,128)} %bitcast.5), calls=%async_computation.1 | async-start | bytes 90112 | tf_op jit(solution)/shard_map/all_to_all | solution.py:503
  51.0 5.9 %collective-permute-start.3 = (f32[96,128]{1,0:T(8,128)S(1)}, f32[96,128]{1,0:T(8,128)S(1)}, u32[]{:S(2)}, u32[]{:S(2)}) collective-permute-start(f32[96,128]{1,0:T(8,128)S(1)} %shard_map.79), channel_id=1, source_target_pairs={{0,1},{1,2},{2,3},{3,4},{4,5},{5,6},{6,7},{7,8},{8,9},{9,10},{10,1... | collective-permute-start | bytes 147464 | tf_op jit(solution)/shard_map/ppermute | solution.py:458
  54.7 0.7 copy-start.1
  63.6 16.6 %all-to-all-start.2 = ((f32[64,1,1408]{2,1,0:T(1,128)}), f32[64,1,1408]{2,1,0:T(1,128)S(1)}, u32[]{:S(2)}, u32[]{:S(2)}) async-start(f32[64,1,1408]{2,1,0:T(1,128)} %bitcast.12), calls=%async_computation.2 | async-start | bytes 720896 | tf_op jit(solution)/shard_map/all_to_all | solution.py:514

commit v7 on v6

--- a/solution.py
+++ b/solution.py
@@ -418,6 +418,15 @@
     token[...] = jnp.zeros((8, L), F32)
 
 
+def flip_kernel(weight, flipped):
+    blocks = []
+    for tap in reversed(range(9)):
+        block = jnp.concatenate([weight[:, tap * C : (tap + 1) * C], jnp.zeros((C, L - C), F32)], axis=1)
+        block = jnp.concatenate([block, jnp.zeros((L - C, L), F32)], axis=0)
+        blocks.append(block.T[:C, :C])
+    flipped[...] = jnp.concatenate(blocks, axis=1)
+
+
 def conv(is_grad, *args, after=()):
     blocks = 3 + R // 2 + 3 if is_grad else R // 2 + 2
     scratch = pltpu.VMEM((blocks * 3 * C, 2 * L), BF16)
@@ -501,7 +510,7 @@
     column = call(column_kernel, [kept(C, L)], (own_east, row_1, row_2), after=(mine,))[0]
     west = send(column, to_east)
     others = lax.all_to_all(mine.reshape(n_far, 1, chunks.rows * L), FAR, 0, 0)
-    flipped = weight.reshape(C, 3, 3, C)[:, ::-1, ::-1].transpose(3, 1, 2, 0).reshape(C, 9 * C)
+    flipped = call(flip_kernel, [kept(C, 9 * C)], (weight,), after=(column,))[0]
     halo = (west, east, row_1, row_2)
     bias = bias.reshape(C, 1)
     mine = call(

time: 81.4 us -> 81.5 us (level)
  local copies, waits for them, and re-layouts: 3.14 us -> 0.11 us
  waiting for transfers between devices: 10.5 us -> 13.1 us
    all_to_all x1, waiting for transfers between devices: 5.89 us -> 7.92 us  [shards(): others = lax.all_to_all(mine.reshape(n_far, 1, chunks.rows * L), FAR, 0, 0)]
    transpose x2 -> x0, local copies, waits for them, and re-layouts: 1.99 us -> none  [shards(): weight.reshape(C, 3, 3, C)[:, ::-1, ::-1].transpose(3, 1, 2, 0)]
    unnamed x5 -> x4, local copies, waits for them, and re-layouts: 0.85 us -> 0.01 us
    pallas_call x9 -> x10, Pallas kernels: 14.6 us -> 15 us  [call(): pl.pallas_call(body, out_shape=outs, in_specs=(specs or [VMEM] * len(args...]
  transfers between devices with their start and end apart: 6 -> 6, of which waited for: 3 -> 4; matrix products, arithmetic and copies ran while one was open for 3% -> 0% of each run, Pallas kernels for 11% -> 12%
where the time goes in v7:
time: 81.5 us; the launch traced here: 81.1 us
  starting transfers between devices  27.8 us (34%)
  blocking collectives  24.4 us (30%)
  Pallas kernels  15 us (18%)
  waiting for transfers between devices  13.1 us (16%)
    all_to_all x1, blocking collectives, shards(): lax.all_to_all(packed.reshape(n_near, 1, chunks.sent * L), NEAR, 0, 0)  24.4 us
    ppermute x4, starting transfers between devices, send(): return lax.ppermute(value, AXES, pairs)  15.6 us
    pallas_call x10, Pallas kernels, call(): pl.pallas_call(body, out_shape=outs, in_specs=(specs or [VMEM] * len(args...  15 us
    all_to_all x1, waiting for transfers between devices, shards(): others = lax.all_to_all(mine.reshape(n_far, 1, chunks.rows * L), FAR, 0, 0)  7.92 us
    all_to_all x1, starting transfers between devices, shards(): others = lax.all_to_all(mine.reshape(n_far, 1, chunks.rows * L), FAR, 0, 0)  6.52 us
    all_to_all x1, starting transfers between devices, shards(): lax.all_to_all(mine.reshape(n_near, 1, chunks.rows * L), NEAR, 0, 0)  5.66 us
    all_to_all x1, waiting for transfers between devices, shards(): lax.all_to_all(mine.reshape(n_near, 1, chunks.rows * L), NEAR, 0, 0)  4.34 us
  transfers between devices with their start and end apart: 6, of which 4 were waited for; matrix products, arithmetic and copies ran while one was open for 0% of the time, Pallas kernels for 12%

profile of v7, /device:TPU:1, one launch (start us, length us, event | category | flops | bytes accessed | tf_op | source)
XLA Modules:
  0.0 81.1 jit_solution(14013743742027560686)
XLA Ops:
  0.6 2.0 %shard_map.75 = (f32[2,96,128]{2,1,0:T(8,128)S(1)}, f32[2,96,128]{2,1,0:T(8,128)S(1)}, f32[96,128]{1,0:T(8,128)S(1)}, f32[96,128]{1,0:T(8,128)S(1)}, f32[1536,128]{1,0:T(8,128)S(1)}, /*index=5*/f32[1536,128]{1,0:T(8,128)S(1)}) custom-call(f32[1536,128]{1,0:T(8,128)} %bitcast.16, f32[1536,128]{1,0:T(8,128)} %bitcast.17), custom_call_target="tpu_custom_call" | custom-call | flops 786432 | bytes 1572864 | tf_op jit(solution)/shard_map/pallas_call | solution.py:33
  2.7 4.0 %collective-permute-start = (f32[2,96,128]{2,1,0:T(8,128)S(1)}, f32[2,96,128]{2,1,0:T(8,128)S(1)}, u32[]{:S(2)}, u32[]{:S(2)}) collective-permute-start(f32[2,96,128]{2,1,0:T(8,128)S(1)} %get-tuple-element.16.refs_2_), channel_id=1, source_target_pairs={{0,64},{1,65},{2,66},{3,67},{4,68},{5,69},{6,70},{7,71},{8,72},{9,... | collective-permute-start | bytes 294920 | tf_op jit(solution)/shard_map/ppermute | solution.py:467
  6.7 4.7 %collective-permute-start.1 = (f32[2,96,128]{2,1,0:T(8,128)S(1)}, f32[2,96,128]{2,1,0:T(8,128)S(1)}, u32[]{:S(2)}, u32[]{:S(2)}) collective-permute-start(f32[2,96,128]{2,1,0:T(8,128)S(1)} %get-tuple-element.17.refs_3_), channel_id=1, source_target_pairs={{0,32},{1,33},{2,34},{3,35},{4,36},{5,37},{6,38},{7,39},{8,40},{9,... | collective-permute-start | bytes 294920 | tf_op jit(solution)/shard_map/ppermute | solution.py:467
  11.4 3.9 %collective-permute-start.2 = (f32[96,128]{1,0:T(8,128)S(1)}, f32[96,128]{1,0:T(8,128)S(1)}, u32[]{:S(2)}, u32[]{:S(2)}) collective-permute-start(f32[96,128]{1,0:T(8,128)S(1)} %get-tuple-element.19), channel_id=1, source_target_pairs={{0,63},{1,0},{2,1},{3,2},{4,3},{5,4},{6,5},{7,6},{8,7},{9,8},{10,9... | collective-permute-start | bytes 147464 | tf_op jit(solution)/shard_map/ppermute | solution.py:467
  15.3 2.5 %shard_map.76.refs_0_ = f32[96,896]{1,0:T(8,128)S(1)} custom-call(f32[1536,128]{1,0:T(8,128)S(1)} %get-tuple-element.14.refs_0_, f32[1536,128]{1,0:T(8,128)S(1)} %get-tuple-element.18.refs_1_.refs_0_), custom_call_target="tpu_custom_call" | custom-call | flops 1019215872 | bytes 1572864 | tf_op jit(solution)/shard_map/pallas_call | solution.py:33
  17.9 0.2 collective-permute-done.2.refs_4_.refs_2_
  18.1 0.0 collective-permute-done.refs_5_.refs_1_.refs_3_
  18.1 0.0 collective-permute-done.1.refs_6_.refs_2_.refs_4_
  18.1 1.1 %shard_map.77 = f32[768,128]{1,0:T(8,128)S(1)} custom-call(f32[96,896]{1,0:T(8,128)S(1)} %shard_map.76.refs_0_, f32[96,128]{1,0:T(8,128)S(1)} %get-tuple-element.15.refs_1_.refs_0_, f32[2,96,128]{2,1,0:T(8,128)S(1)} %get-tuple-element.16.refs_2_, f32[2,96,128]{2,1,0:T(8,128)S(1)} %get-tuple-element.17.refs_3_, ...), custom_call_target="tpu_custom_call" | custom-call | flops 254803968 | bytes 786432 | tf_op jit(solution)/shard_map/pallas_call | solution.py:33
  19.2 24.4 %all_to_all.15.refs_7_ = f32[64,1,1536]{2,1,0:T(1,128)S(1)} all-to-all(f32[64,1,1536]{2,1,0:T(1,128)S(1)} %bitcast.13), channel_id=1, replica_groups=mesh['lat'=8,'xh'=2,'zr'=8,'zd'=2,'c'=2] {'lat','xh','zd','c'}, dimensions={0} | all-to-all | bytes 786432 | tf_op jit(solution)/shard_map/all_to_all | solution.py:503
  43.6 0.7 shard_map.78.refs_3_
  44.3 0.0 copy-start
  44.3 6.5 %all-to-all-start.1 = ((f32[8,1,1408]{2,1,0:T(1,128)}), f32[8,1,1408]{2,1,0:T(1,128)S(1)}, u32[]{:S(2)}, u32[]{:S(2)}) async-start(f32[8,1,1408]{2,1,0:T(1,128)} %bitcast.5), calls=%async_computation.1 | async-start | bytes 90112 | tf_op jit(solution)/shard_map/all_to_all | solution.py:512
  50.8 0.1 shard_map.79.refs_1_
  50.9 0.0 copy-start.1
  50.9 3.0 %collective-permute-start.3 = (f32[96,128]{1,0:T(8,128)S(1)}, f32[96,128]{1,0:T(8,128)S(1)}, u32[]{:S(2)}, u32[]{:S(2)}) collective-permute-start(f32[96,128]{1,0:T(8,128)S(1)} %shard_map.79.refs_1_), channel_id=1, source_target_pairs={{0,1},{1,2},{2,3},{3,4},{4,5},{5,6},{6,7},{7,8},{8,9},{9,10},{10,1... | collective-permute-start | bytes 147464 | tf_op jit(solution)/shard_map/ppermute | solution.py:467
  53.9 0.0 copy-done.1
  53.9 0.1 copy.13.refs_3_.refs_6_
  54.0 0.0 copy-done
  54.0 0.4 shard_map.80.refs_2_.refs_5_
  54.5 0.6 collective-permute-done.3.refs_1_
  55.0 7.9 %all-to-all-done.1 = f32[8,1,1408]{2,1,0:T(1,128)S(1)} async-done(((f32[8,1,1408]{2,1,0:T(1,128)}), f32[8,1,1408]{2,1,0:T(1,128)S(1)}, u32[]{:S(2)}, u32[]{:S(2)}) %all-to-all-start.1) | async-done | bytes 45088 | tf_op jit(solution)/shard_map/all_to_all | solution.py:512
  63.0 0.8 shard_map.81.refs_8_
  63.7 5.7 %all-to-all-start.2 = ((f32[64,1,1408]{2,1,0:T(1,128)}), f32[64,1,1408]{2,1,0:T(1,128)S(1)}, u32[]{:S(2)}, u32[]{:S(2)}) async-start(f32[64,1,1408]{2,1,0:T(1,128)} %bitcast.9), calls=%async_computation.2 | async-start | bytes 720896 | tf_op jit(solution)/shard_map/all_to_all | solution.py:523
  69.4 3.4 %shard_map.83 = (f32[1536,128]{1,0:T(8,128)}, f32[8,128]{1,0:T(8,128)}) custom-call(f32[1536,128]{1,0:T(8,128)S(1)} %get-tuple-element.18.refs_1_.refs_0_, f32[96,128]{1,0:T(8,128)S(1)} %collective-permute-done.3.refs_1_, f32[96,128]{1,0:T(8,128)S(1)} %collective-permute-done.2.refs_4_.refs_2_, ...), custom_call_target="tpu_custom_call" | custom-call | flops 4076863488 | bytes 2359296 | tf_op jit(solution)/shard_map/pallas_call | solution.py:33
  72.8 3.1 %shard_map.82 = (f32[1536,128]{1,0:T(8,128)}, f32[8,128]{1,0:T(8,128)}) custom-call(f32[1536,128]{1,0:T(8,128)S(1)} %get-tuple-element.14.refs_0_, f32[96,128]{1,0:T(8,128)S(1)} %collective-permute-done.3.refs_1_, f32[96,128]{1,0:T(8,128)S(1)} %collective-permute-done.2.refs_4_.refs_2_, f32[2,96,128]{2,1,0:T(8,128)S(1)} %collective-permute-done.refs_5_.refs_1_.refs_3_, ...), custom_call_target="tpu_custom_call" | custom-call | flops 4076863488 | bytes 2359296 | tf_op jit(solution)/shard_map/pallas_call | solution.py:33
  75.9 4.3 %all-to-all-done.2 = f32[64,1,1408]{2,1,0:T(1,128)S(1)} async-done(((f32[64,1,1408]{2,1,0:T(1,128)}), f32[64,1,1408]{2,1,0:T(1,128)S(1)}, u32[]{:S(2)}, u32[]{:S(2)}) %all-to-all-start.2) | async-done | bytes 360480 | tf_op jit(solution)/shard_map/all_to_all | solution.py:523
  80.3 0.8 %shard_map.84 = (f32[96,864]{1,0:T(8,128)}, f32[1,96]{1,0:T(1,128)}) custom-call(f32[704,128]{1,0:T(8,128)S(1)} %bitcast.14), custom_call_target="tpu_custom_call" | custom-call | bytes 786432 | tf_op jit(solution)/shard_map/pallas_call | solution.py:33
Async XLA Ops:
  2.7 15.4 %collective-permute-start = (f32[2,96,128]{2,1,0:T(8,128)S(1)}, f32[2,96,128]{2,1,0:T(8,128)S(1)}, u32[]{:S(2)}, u32[]{:S(2)}) collective-permute-start(f32[2,96,128]{2,1,0:T(8,128)S(1)} %get-tuple-element.16.refs_2_), channel_id=1, source_target_pairs={{0,64},{1,65},{2,66},{3,67},{4,68},{5,69},{6,70},{7,71},{8,72},{9,... | collective-permute-start | bytes 294920 | tf_op jit(solution)/shard_map/ppermute | solution.py:467
  6.7 11.4 %collective-permute-start.1 = (f32[2,96,128]{2,1,0:T(8,128)S(1)}, f32[2,96,128]{2,1,0:T(8,128)S(1)}, u32[]{:S(2)}, u32[]{:S(2)}) collective-permute-start(f32[2,96,128]{2,1,0:T(8,128)S(1)} %get-tuple-element.17.refs_3_), channel_id=1, source_target_pairs={{0,32},{1,33},{2,34},{3,35},{4,36},{5,37},{6,38},{7,39},{8,40},{9,... | collective-permute-start | bytes 294920 | tf_op jit(solution)/shard_map/ppermute | solution.py:467
  11.4 6.7 %collective-permute-start.2 = (f32[96,128]{1,0:T(8,128)S(1)}, f32[96,128]{1,0:T(8,128)S(1)}, u32[]{:S(2)}, u32[]{:S(2)}) collective-permute-start(f32[96,128]{1,0:T(8,128)S(1)} %get-tuple-element.19), channel_id=1, source_target_pairs={{0,63},{1,0},{2,1},{3,2},{4,3},{5,4},{6,5},{7,6},{8,7},{9,8},{10,9... | collective-permute-start | bytes 147464 | tf_op jit(solution)/shard_map/ppermute | solution.py:467
  44.3 9.7 %copy-start = (f32[96,864]{1,0:T(8,128)S(1)}, f32[96,864]{1,0:T(8,128)}, u32[]{:S(2)}) copy-start(f32[96,864]{1,0:T(8,128)} %refs_5_.1) | copy-start | bytes 995332
  44.3 18.7 %all-to-all-start.1 = ((f32[8,1,1408]{2,1,0:T(1,128)}), f32[8,1,1408]{2,1,0:T(1,128)S(1)}, u32[]{:S(2)}, u32[]{:S(2)}) async-start(f32[8,1,1408]{2,1,0:T(1,128)} %bitcast.5), calls=%async_computation.1 | async-start | bytes 90112 | tf_op jit(solution)/shard_map/all_to_all | solution.py:512
  50.9 3.0 %copy-start.1 = (f32[96]{0:T(128)S(1)}, f32[96]{0:T(128)}, u32[]{:S(2)}) copy-start(f32[96]{0:T(128)} %param.6) | copy-start | bytes 1156
  50.9 4.1 %collective-permute-start.3 = (f32[96,128]{1,0:T(8,128)S(1)}, f32[96,128]{1,0:T(8,128)S(1)}, u32[]{:S(2)}, u32[]{:S(2)}) collective-permute-start(f32[96,128]{1,0:T(8,128)S(1)} %shard_map.79.refs_1_), channel_id=1, source_target_pairs={{0,1},{1,2},{2,3},{3,4},{4,5},{5,6},{6,7},{7,8},{8,9},{9,10},{10,1... | collective-permute-start | bytes 147464 | tf_op jit(solution)/shard_map/ppermute | solution.py:467
  63.7 16.5 %all-to-all-start.2 = ((f32[64,1,1408]{2,1,0:T(1,128)}), f32[64,1,1408]{2,1,0:T(1,128)S(1)}, u32[]{:S(2)}, u32[]{:S(2)}) async-start(f32[64,1,1408]{2,1,0:T(1,128)} %bitcast.9), calls=%async_computation.2 | async-start | bytes 720896 | tf_op jit(solution)/shard_map/all_to_all | solution.py:523
